TPU v7x, 32 devices: a whole 2x2x4 slice. The times are simulated.
32 devices in a mesh: pipe: 4 (over y, core), head: 8 (over z, x).
Axes of the slice: x: 2, y: 2, z: 4, core: 2. Of those that a mesh axis runs over, the one named last changes fastest.
Arguments:
- patch_in: bfloat16 [4, 8, 2048], P(None, 'head'), may hold values from -200 to 200
- patch_start: int32 [4], replicated, may hold values from 0 to 2040, as said below
- mod_scale: float32 [4, 2048], P('pipe'), may hold values from -2.5 to 2.5
- mod_shift: float32 [4, 2048], P('pipe'), may hold values from -2.5 to 2.5
- res_gate: float32 [4, 2048], P('pipe'), may hold values from -4 to 4
- query_weight: bfloat16 [4, 16, 2048, 128], P('pipe', 'head'), may hold values from -0.3125 to 0.3125
- kv_weight: bfloat16 [4, 16, 2048, 256], P('pipe', 'head'), may hold values from -0.125 to 0.125
- stale_keys: bfloat16 [4, 16, 2048, 128], P('pipe', 'head'), may hold values from -3000 to 3000
- stale_values: bfloat16 [4, 16, 2048, 128], P('pipe', 'head'), may hold values from -6 to 6
Outputs:
- hidden_out: bfloat16 [4, 4, 8, 2048], P('pipe', None, 'head')
Inputs may be any that keep to these rules, and one draw needn't show every extreme that they name: `patch_start`: distinct multiples of 8; the first and the last possible start are always among them.
All inputs are finite; a program needn't handle non-finite values.
Results may differ from a plain program's by a relative error of at most 0.035.
Values may be sent and summed in bfloat16 or wider, within the bound.
No kernel may reach another device: no remote copies, remote signals or barrier semaphores. Data moves between devices by JAX's collectives and lax.ppermute only.
A program may use at most 64 MiB of HBM per device.

v0:
```python
import math

import jax
import jax.numpy as jnp
from jax import lax
from jax.sharding import PartitionSpec as P

HEADS = 16


def shifted(value, axis, steps):
    count = lax.axis_size(axis)
    leading, last = (max(0, -steps), min(count, count - steps))
    return lax.ppermute(value, axis, [(source, source + steps) for source in range(leading, last)])


def modulate(rows, scale_row, shift_row):
    values = rows.astype(jnp.float32)
    meansq = jnp.mean(values * values, axis=-1, keepdims=True)
    normed = values * lax.rsqrt(meansq + 1e-06)
    return (normed * (1.0 + scale_row) + shift_row).astype(jnp.bfloat16)


def feature_layout(modded, groups, splits):
    rows_dev, feat = modded.shape
    width = feat // splits
    pieces = jnp.transpose(modded.reshape(rows_dev, splits, width), (1, 0, 2))
    copies = jnp.broadcast_to(pieces[None], (groups, splits, rows_dev, width))
    return copies.reshape(groups * splits, rows_dev, width)


def project_partial(received, w_both):
    n_src, rows_dev, width = received.shape
    inputs = received.reshape(n_src * rows_dev, width)
    partial_sum = jnp.einsum("pf,hfe->phe", inputs, w_both, preferred_element_type=jnp.float32)
    return partial_sum.reshape(n_src, rows_dev, -1)


def sum_partials(returned, groups, splits, heads_dev):
    n_src, rows_dev, width = returned.shape
    triple = width // heads_dev
    summed = jnp.sum(returned.reshape(groups, splits, rows_dev, heads_dev, triple), axis=1)
    ordered = jnp.transpose(summed, (1, 0, 2, 3))
    return ordered.reshape(rows_dev, groups * heads_dev, triple).astype(jnp.bfloat16)


def head_layout(qkv_own, groups, splits):
    rows_dev, heads_all, triple = qkv_own.shape
    width = heads_all // groups * triple
    grouped = jnp.transpose(qkv_own.reshape(rows_dev, groups, width), (1, 0, 2))
    copies = jnp.broadcast_to(grouped[:, None], (groups, splits, rows_dev, width))
    return copies.reshape(groups * splits, rows_dev, width)


def attend_block(query_blk, keys_buf, vals_buf):
    score_scale = 1.0 / math.sqrt(query_blk.shape[-1])
    logit_scores = (
        jnp.einsum("qhd,hkd->hqk", query_blk, keys_buf, preferred_element_type=jnp.float32)
        * score_scale
    )
    top = jnp.max(logit_scores, axis=-1)
    expo = jnp.exp(logit_scores - top[..., None])
    total = jnp.sum(expo, axis=-1)
    softmax_weight = expo.astype(jnp.bfloat16)
    blended_values = jnp.einsum(
        "hqk,hkd->qhd", softmax_weight, vals_buf, preferred_element_type=jnp.float32
    )
    partial_out = blended_values / jnp.transpose(total)[..., None]
    return (partial_out, jnp.transpose(top), jnp.transpose(total))


def segment_attend(received, offset, keys_buf, vals_buf, key_base):
    heads_dev, shard_keys, head_dim = keys_buf.shape
    patch = received.shape[0] * received.shape[1]
    triples = received.reshape(patch, heads_dev, 3 * head_dim)
    query = triples[..., :head_dim]
    fresh = triples[..., head_dim:]
    position = key_base + jnp.arange(shard_keys, dtype=jnp.int32)
    relative = position - offset
    inside = ((relative >= 0) & (relative < patch))[None, :, None]
    picked = jnp.clip(relative, 0, patch - 1)
    taken = jnp.transpose(jnp.take(fresh, picked, axis=0), (1, 0, 2))
    new_keys = jnp.where(inside, taken[..., :head_dim], keys_buf)
    new_vals = jnp.where(inside, taken[..., head_dim:], vals_buf)
    block = min(512, patch)
    blocks = query.reshape(patch // block, block, heads_dev, head_dim)
    outs, tops, totals = lax.map(lambda blk: attend_block(blk, new_keys, new_vals), blocks)
    return (
        new_keys,
        new_vals,
        outs.reshape(patch, heads_dev, head_dim),
        tops.reshape(patch, heads_dev),
        totals.reshape(patch, heads_dev),
    )


def merge_parts(outs, tops, totals, groups, splits):
    n_dev, rows_dev, width = outs.shape
    heads_dev = tops.shape[-1]
    head_dim = width // heads_dev
    outs = outs.reshape(groups, splits, rows_dev, heads_dev, head_dim)
    tops = tops.reshape(groups, splits, rows_dev, heads_dev)
    totals = totals.reshape(groups, splits, rows_dev, heads_dev)
    peak = jnp.max(tops, axis=1, keepdims=True)
    weight = jnp.exp(tops - peak) * totals
    summed = jnp.sum(weight[..., None] * outs, axis=1) / jnp.sum(weight, axis=1)[..., None]
    return jnp.transpose(summed, (1, 0, 2, 3)).reshape(rows_dev, groups * width)


def per_device(
    patch_in,
    patch_start,
    mod_scale,
    mod_shift,
    res_gate,
    query_weight,
    kv_weight,
    stale_keys,
    stale_values,
):
    n_head = lax.axis_size("head")
    n_pipe = lax.axis_size("pipe")
    micro, rows_dev, feat = patch_in.shape
    heads_dev = stale_keys.shape[1]
    shard_keys = stale_keys.shape[2]
    head_dim = stale_keys.shape[3]
    splits = max(n_head // HEADS, 1)
    groups = n_head // splits
    patch = rows_dev * n_head
    head_index = lax.axis_index("head")
    segment = lax.axis_index("pipe")
    key_base = head_index % splits * shard_keys
    w_both = jnp.concatenate([query_weight[0], kv_weight[0]], axis=-1)
    scale_row = mod_scale[0]
    shift_row = mod_shift[0]
    gate_row = res_gate[0]

    def run_attention(valid, received, offset, keys_buf, vals_buf):

        def active(operands):
            return segment_attend(operands[0], operands[1], operands[2], operands[3], key_base)

        def resting(operands):
            return (
                operands[2],
                operands[3],
                jnp.zeros((patch, heads_dev, head_dim), jnp.float32),
                jnp.zeros((patch, heads_dev), jnp.float32),
                jnp.ones((patch, heads_dev), jnp.float32),
            )

        return lax.cond(valid, active, resting, (received, offset, keys_buf, vals_buf))

    def write_out(outputs, valid, index, updated):
        old = lax.dynamic_index_in_dim(outputs, index, 0, keepdims=False)
        return lax.dynamic_update_index_in_dim(outputs, jnp.where(valid, updated, old), index, 0)

    def entering(index, incoming):
        first = lax.dynamic_index_in_dim(patch_in, index, 0, keepdims=False)
        return jnp.where(segment == 0, first, incoming)

    outputs = jnp.zeros((micro, rows_dev, feat), jnp.bfloat16)
    incoming = jnp.zeros((rows_dev, feat), jnp.bfloat16)
    keys_buf = stale_keys[0]
    vals_buf = stale_values[0]

    def apart_step(step, carry):
        keys_buf, vals_buf, incoming, outputs = carry
        index = step - segment
        valid = (index >= 0) & (index < micro)
        safe = jnp.clip(index, 0, micro - 1)
        current = entering(safe, incoming)
        modded = modulate(current, scale_row, shift_row)
        recv_feat = lax.all_to_all(
            feature_layout(modded, groups, splits), "head", split_axis=0, concat_axis=0, tiled=True
        )
        partial_sum = project_partial(recv_feat, w_both)
        returned = lax.all_to_all(partial_sum, "head", split_axis=0, concat_axis=0, tiled=True)
        qkv_own = sum_partials(returned, groups, splits, heads_dev)
        recv_qkv = lax.all_to_all(
            head_layout(qkv_own, groups, splits), "head", split_axis=0, concat_axis=0, tiled=True
        )
        keys_buf, vals_buf, part_out, tops, totals = run_attention(
            valid, recv_qkv, patch_start[safe], keys_buf, vals_buf
        )
        outs_back, tops_back, totals_back = (
            lax.all_to_all(
                part_out.reshape(n_head, rows_dev, heads_dev * head_dim),
                "head",
                split_axis=0,
                concat_axis=0,
                tiled=True,
            ),
            lax.all_to_all(
                tops.reshape(n_head, rows_dev, heads_dev),
                "head",
                split_axis=0,
                concat_axis=0,
                tiled=True,
            ),
            lax.all_to_all(
                totals.reshape(n_head, rows_dev, heads_dev),
                "head",
                split_axis=0,
                concat_axis=0,
                tiled=True,
            ),
        )
        blended_values = merge_parts(outs_back, tops_back, totals_back, groups, splits)
        updated = (current.astype(jnp.float32) + gate_row * blended_values).astype(jnp.bfloat16)
        outputs = write_out(outputs, valid, safe, updated)
        incoming = shifted(updated, "pipe", 1)
        return (keys_buf, vals_buf, incoming, outputs)

    final = lax.fori_loop(
        0, micro + n_pipe - 1, apart_step, (keys_buf, vals_buf, incoming, outputs)
    )
    outputs = final[3]
    return outputs[None]


def solution(mesh):
    placed = (
        P(None, "head", None),
        P(),
        P("pipe", None),
        P("pipe", None),
        P("pipe", None),
        P("pipe", "head", None, None),
        P("pipe", "head", None, None),
        P("pipe", "head", None, None),
        P("pipe", "head", None, None),
    )
    return jax.shard_map(
        per_device,
        mesh=mesh,
        in_specs=placed,
        out_specs=P("pipe", None, "head", None),
        check_vma=False,
    )
```

profile of v0, /device:TPU:5, one launch (start us, length us, event | category | flops | bytes accessed | tf_op | source)
XLA Modules:
  0.0 741.9 jit_solution(10199970590400082071)
XLA Ops:
  6.7 12.1 %copy_bitcast_fusion = (bf16[2,2048,128]{2,0,1:T(2,128)(2,1)S(1)}, bf16[2,2048,128]{2,0,1:T(2,128)(2,1)}) fusion(bf16[1,2,2048,128]{3,2,1,0:T(8,128)(2,1)S(1)} %copy-done.1, bf16[1,2,2048,128]{3,2,1,0:T(8,128)(2,1)S(1)} %copy-done.2), kind=kLoop, calls=%fused_computation.41 | loop fusion | bytes 4194304 | tf_op jit(solution)/shard_map/squeeze | solution.py:165
  18.9 722.4 %while.19 = (s32[]{:T(128)}, bf16[2,2048,128]{2,0,1:T(2,128)(2,1)}, bf16[2,2048,128]{2,0,1:T(2,128)(2,1)S(1)}, bf16[1,2048]{1,0:T(2,128)(2,1)S(1)}, bf16[4,1,204...) while((s32[]{:T(128)}, bf16[2,2048,128]{2,0,1:T(2,128)(2,1)}, ...), condition=%wide.region_6.7_spmd, body=%wide.region_0.6_spmd.sunk | while | flops 44304392 | bytes 21247964 | solution.py:215
  21.7 10.9 %all_to_all.78 = bf16[8,2,1024]{2,1,0:T(2,128)(2,1)S(1)} all-to-all(bf16[8,2,1024]{2,1,0:T(2,128)(2,1)S(1)} %reshape.339), channel_id=1, replica_groups=mesh['pipe'=4,'head'=8] {'head'}, dimensions={0} | all-to-all | bytes 65536 | tf_op jit(solution)/shard_map/while/body/eval_jaxpr/all_to_all | solution.py:174
  84.6 9.0 %collective-permute-done = bf16[1,2048]{1,0:T(2,128)(2,1)S(1)} collective-permute-done((bf16[1,2048]{1,0:T(2,128)(2,1)S(1)}, bf16[1,2048]{1,0:T(2,128)(2,1)S(1)}, u32[]{:S(2)}, u32[]{:S(2)}) %collective-permute-start) | collective-permute-done | bytes 4128 | tf_op jit(solution)/shard_map/while/body/eval_jaxpr/ppermute | solution.py:14
  96.4 7.9 %all_to_all.78 = bf16[8,2,1024]{2,1,0:T(2,128)(2,1)S(1)} all-to-all(bf16[8,2,1024]{2,1,0:T(2,128)(2,1)S(1)} %reshape.339), channel_id=1, replica_groups=mesh['pipe'=4,'head'=8] {'head'}, dimensions={0} | all-to-all | bytes 65536 | tf_op jit(solution)/shard_map/while/body/eval_jaxpr/all_to_all | solution.py:174
  156.3 10.5 %collective-permute-done = bf16[1,2048]{1,0:T(2,128)(2,1)S(1)} collective-permute-done((bf16[1,2048]{1,0:T(2,128)(2,1)S(1)}, bf16[1,2048]{1,0:T(2,128)(2,1)S(1)}, u32[]{:S(2)}, u32[]{:S(2)}) %collective-permute-start) | collective-permute-done | bytes 4128 | tf_op jit(solution)/shard_map/while/body/eval_jaxpr/ppermute | solution.py:14
  229.4 97.4 %collective-permute-done = bf16[1,2048]{1,0:T(2,128)(2,1)S(1)} collective-permute-done((bf16[1,2048]{1,0:T(2,128)(2,1)S(1)}, bf16[1,2048]{1,0:T(2,128)(2,1)S(1)}, u32[]{:S(2)}, u32[]{:S(2)}) %collective-permute-start) | collective-permute-done | bytes 4128 | tf_op jit(solution)/shard_map/while/body/eval_jaxpr/ppermute | solution.py:14
  329.6 7.9 %all_to_all.78 = bf16[8,2,1024]{2,1,0:T(2,128)(2,1)S(1)} all-to-all(bf16[8,2,1024]{2,1,0:T(2,128)(2,1)S(1)} %reshape.339), channel_id=1, replica_groups=mesh['pipe'=4,'head'=8] {'head'}, dimensions={0} | all-to-all | bytes 65536 | tf_op jit(solution)/shard_map/while/body/eval_jaxpr/all_to_all | solution.py:174
  359.9 33.8 %conditional.2 = (bf16[2,2048,128]{2,0,1:T(2,128)(2,1)}, bf16[2,2048,128]{2,0,1:T(2,128)(2,1)S(1)}, f32[8,2,128]{2,0,1:T(8,128)S(1)}, f32[8,2]{0,1:T(2,128)}, f32[8,2]{0,1:T(2,128)}) conditional(s32[]{:T(128)} %convert_element_type.68, (bf16[2,2048,128]{2,0,1:T(2,128)(2,1)}, bf16[2,2048,128]{2,0,1:T(2,128)(2,1)S(1)}) %tuple.61, (s32[4]{0:T(128)S(1)}, ...), branch_computations={%region_2.2_spmd, %region_3.5_spmd} | conditional | flops 19107808 | bytes 17351090 | solution.py:152
  377.5 11.6 %broadcast_select_fusion.1 = (bf16[2,2048,128]{2,0,1:T(2,128)(2,1)S(1)}, bf16[2,2048,128]{2,0,1:T(2,128)(2,1)}) fusion(bf16[2,2048,128]{2,0,1:T(2,128)(2,1)S(1)} %get-tuple-element.353, pred[2048]{0:T(1024)(128)(4,1)S(1)} %get-tuple-element.425, bf16[2,2048,256]{2,0,1:T(2,128)(2,1)S(1)} %fusion.1, bf16[2,2048,128]{2,0,1:T(2,128)(2,1)} %get-tuple-element.352), kind=kLoop, calls=%fused_computation.5 | loop fusion | flops 1048576 | bytes 6293504 | tf_op jit(solution)/shard_map/while/body/eval_jaxpr/cond/branch_1_fun/jit(_where)/select_n | solution.py:84
  422.2 10.5 %collective-permute-done = bf16[1,2048]{1,0:T(2,128)(2,1)S(1)} collective-permute-done((bf16[1,2048]{1,0:T(2,128)(2,1)S(1)}, bf16[1,2048]{1,0:T(2,128)(2,1)S(1)}, u32[]{:S(2)}, u32[]{:S(2)}) %collective-permute-start) | collective-permute-done | bytes 4128 | tf_op jit(solution)/shard_map/while/body/eval_jaxpr/ppermute | solution.py:14
  435.4 7.9 %all_to_all.78 = bf16[8,2,1024]{2,1,0:T(2,128)(2,1)S(1)} all-to-all(bf16[8,2,1024]{2,1,0:T(2,128)(2,1)S(1)} %reshape.339), channel_id=1, replica_groups=mesh['pipe'=4,'head'=8] {'head'}, dimensions={0} | all-to-all | bytes 65536 | tf_op jit(solution)/shard_map/while/body/eval_jaxpr/all_to_all | solution.py:174
  465.7 33.8 %conditional.2 = (bf16[2,2048,128]{2,0,1:T(2,128)(2,1)}, bf16[2,2048,128]{2,0,1:T(2,128)(2,1)S(1)}, f32[8,2,128]{2,0,1:T(8,128)S(1)}, f32[8,2]{0,1:T(2,128)}, f32[8,2]{0,1:T(2,128)}) conditional(s32[]{:T(128)} %convert_element_type.68, (bf16[2,2048,128]{2,0,1:T(2,128)(2,1)}, bf16[2,2048,128]{2,0,1:T(2,128)(2,1)S(1)}) %tuple.61, (s32[4]{0:T(128)S(1)}, ...), branch_computations={%region_2.2_spmd, %region_3.5_spmd} | conditional | flops 19107808 | bytes 17351090 | solution.py:152
  467.8 7.9 %gather_fusion = bf16[2048,2,256]{2,1,0:T(2,128)(2,1)S(1)} fusion(bf16[8,2,256]{2,1,0:T(2,128)(2,1)S(1)} %slice.14, s32[2048]{0:T(1024)S(1)} %broadcast_clamp_fusion), kind=kCustom, calls=%fused_computation | custom fusion | bytes 4202496 | tf_op jit(solution)/shard_map/while/body/eval_jaxpr/cond/branch_1_fun/jit(_take)/gather | solution.py:82
  483.3 11.6 %broadcast_select_fusion.1 = (bf16[2,2048,128]{2,0,1:T(2,128)(2,1)S(1)}, bf16[2,2048,128]{2,0,1:T(2,128)(2,1)}) fusion(bf16[2,2048,128]{2,0,1:T(2,128)(2,1)S(1)} %get-tuple-element.353, pred[2048]{0:T(1024)(128)(4,1)S(1)} %get-tuple-element.425, bf16[2,2048,256]{2,0,1:T(2,128)(2,1)S(1)} %fusion.1, bf16[2,2048,128]{2,0,1:T(2,128)(2,1)} %get-tuple-element.352), kind=kLoop, calls=%fused_computation.5 | loop fusion | flops 1048576 | bytes 6293504 | tf_op jit(solution)/shard_map/while/body/eval_jaxpr/cond/branch_1_fun/jit(_where)/select_n | solution.py:84
  528.0 10.4 %collective-permute-done = bf16[1,2048]{1,0:T(2,128)(2,1)S(1)} collective-permute-done((bf16[1,2048]{1,0:T(2,128)(2,1)S(1)}, bf16[1,2048]{1,0:T(2,128)(2,1)S(1)}, u32[]{:S(2)}, u32[]{:S(2)}) %collective-permute-start) | collective-permute-done | bytes 4128 | tf_op jit(solution)/shard_map/while/body/eval_jaxpr/ppermute | solution.py:14
  541.2 7.9 %all_to_all.78 = bf16[8,2,1024]{2,1,0:T(2,128)(2,1)S(1)} all-to-all(bf16[8,2,1024]{2,1,0:T(2,128)(2,1)S(1)} %reshape.339), channel_id=1, replica_groups=mesh['pipe'=4,'head'=8] {'head'}, dimensions={0} | all-to-all | bytes 65536 | tf_op jit(solution)/shard_map/while/body/eval_jaxpr/all_to_all | solution.py:174
  571.5 33.8 %conditional.2 = (bf16[2,2048,128]{2,0,1:T(2,128)(2,1)}, bf16[2,2048,128]{2,0,1:T(2,128)(2,1)S(1)}, f32[8,2,128]{2,0,1:T(8,128)S(1)}, f32[8,2]{0,1:T(2,128)}, f32[8,2]{0,1:T(2,128)}) conditional(s32[]{:T(128)} %convert_element_type.68, (bf16[2,2048,128]{2,0,1:T(2,128)(2,1)}, bf16[2,2048,128]{2,0,1:T(2,128)(2,1)S(1)}) %tuple.61, (s32[4]{0:T(128)S(1)}, ...), branch_computations={%region_2.2_spmd, %region_3.5_spmd} | conditional | flops 19107808 | bytes 17351090 | solution.py:152
  589.1 11.6 %broadcast_select_fusion.1 = (bf16[2,2048,128]{2,0,1:T(2,128)(2,1)S(1)}, bf16[2,2048,128]{2,0,1:T(2,128)(2,1)}) fusion(bf16[2,2048,128]{2,0,1:T(2,128)(2,1)S(1)} %get-tuple-element.353, pred[2048]{0:T(1024)(128)(4,1)S(1)} %get-tuple-element.425, bf16[2,2048,256]{2,0,1:T(2,128)(2,1)S(1)} %fusion.1, bf16[2,2048,128]{2,0,1:T(2,128)(2,1)} %get-tuple-element.352), kind=kLoop, calls=%fused_computation.5 | loop fusion | flops 1048576 | bytes 6293504 | tf_op jit(solution)/shard_map/while/body/eval_jaxpr/cond/branch_1_fun/jit(_where)/select_n | solution.py:84
  633.8 10.5 %collective-permute-done = bf16[1,2048]{1,0:T(2,128)(2,1)S(1)} collective-permute-done((bf16[1,2048]{1,0:T(2,128)(2,1)S(1)}, bf16[1,2048]{1,0:T(2,128)(2,1)S(1)}, u32[]{:S(2)}, u32[]{:S(2)}) %collective-permute-start) | collective-permute-done | bytes 4128 | tf_op jit(solution)/shard_map/while/body/eval_jaxpr/ppermute | solution.py:14
  647.0 7.9 %all_to_all.78 = bf16[8,2,1024]{2,1,0:T(2,128)(2,1)S(1)} all-to-all(bf16[8,2,1024]{2,1,0:T(2,128)(2,1)S(1)} %reshape.339), channel_id=1, replica_groups=mesh['pipe'=4,'head'=8] {'head'}, dimensions={0} | all-to-all | bytes 65536 | tf_op jit(solution)/shard_map/while/body/eval_jaxpr/all_to_all | solution.py:174
  677.3 33.8 %conditional.2 = (bf16[2,2048,128]{2,0,1:T(2,128)(2,1)}, bf16[2,2048,128]{2,0,1:T(2,128)(2,1)S(1)}, f32[8,2,128]{2,0,1:T(8,128)S(1)}, f32[8,2]{0,1:T(2,128)}, f32[8,2]{0,1:T(2,128)}) conditional(s32[]{:T(128)} %convert_element_type.68, (bf16[2,2048,128]{2,0,1:T(2,128)(2,1)}, bf16[2,2048,128]{2,0,1:T(2,128)(2,1)S(1)}) %tuple.61, (s32[4]{0:T(128)S(1)}, ...), branch_computations={%region_2.2_spmd, %region_3.5_spmd} | conditional | flops 19107808 | bytes 17351090 | solution.py:152
  679.4 7.9 %gather_fusion = bf16[2048,2,256]{2,1,0:T(2,128)(2,1)S(1)} fusion(bf16[8,2,256]{2,1,0:T(2,128)(2,1)S(1)} %slice.14, s32[2048]{0:T(1024)S(1)} %broadcast_clamp_fusion), kind=kCustom, calls=%fused_computation | custom fusion | bytes 4202496 | tf_op jit(solution)/shard_map/while/body/eval_jaxpr/cond/branch_1_fun/jit(_take)/gather | solution.py:82
  695.0 11.6 %broadcast_select_fusion.1 = (bf16[2,2048,128]{2,0,1:T(2,128)(2,1)S(1)}, bf16[2,2048,128]{2,0,1:T(2,128)(2,1)}) fusion(bf16[2,2048,128]{2,0,1:T(2,128)(2,1)S(1)} %get-tuple-element.353, pred[2048]{0:T(1024)(128)(4,1)S(1)} %get-tuple-element.425, bf16[2,2048,256]{2,0,1:T(2,128)(2,1)S(1)} %fusion.1, bf16[2,2048,128]{2,0,1:T(2,128)(2,1)} %get-tuple-element.352), kind=kLoop, calls=%fused_computation.5 | loop fusion | flops 1048576 | bytes 6293504 | tf_op jit(solution)/shard_map/while/body/eval_jaxpr/cond/branch_1_fun/jit(_where)/select_n | solution.py:84
  (356 shorter events, 466.0 us)
Async XLA Ops:
  46.3 8.7 %all-to-all-start.2 = ((bf16[8,2,384]{2,1,0:T(2,128)(2,1)}), bf16[8,2,384]{2,1,0:T(2,128)(2,1)S(1)}, u32[]{:S(2)}, u32[]{:S(2)}) async-start(bf16[8,2,384]{2,1,0:T(2,128)(2,1)} %reshape.343), calls=%async_computation.2 | async-start | bytes 24576 | tf_op jit(solution)/shard_map/while/body/eval_jaxpr/all_to_all | solution.py:180
  65.9 8.5 %all-to-all-start.3 = ((f32[8,1,2]{2,1,0:T(1,128)}), f32[8,1,2]{2,1,0:T(1,128)S(1)}, u32[]{:S(2)}, u32[]{:S(2)}) async-start(f32[8,1,2]{2,1,0:T(1,128)} %copy.84), calls=%async_computation.3 | async-start | bytes 8192 | tf_op jit(solution)/shard_map/while/body/eval_jaxpr/all_to_all | solution.py:201
  74.4 8.6 %all-to-all-start.5 = ((f32[8,1,256]{2,1,0:T(1,128)}), f32[8,1,256]{2,1,0:T(1,128)S(1)}, u32[]{:S(2)}, u32[]{:S(2)}) async-start(f32[8,1,256]{2,1,0:T(1,128)} %bitcast.73), calls=%async_computation.5 | async-start | bytes 16384 | tf_op jit(solution)/shard_map/while/body/eval_jaxpr/all_to_all | solution.py:187
  83.2 10.4 %collective-permute-start = (bf16[1,2048]{1,0:T(2,128)(2,1)S(1)}, bf16[1,2048]{1,0:T(2,128)(2,1)S(1)}, u32[]{:S(2)}, u32[]{:S(2)}) collective-permute-start(bf16[1,2048]{1,0:T(2,128)(2,1)S(1)} %get-tuple-element.523), channel_id=1, source_target_pairs={{0,8},{8,16},{16,24},{1,9},{9,17},{17,25},{2,10},{10,18},{18,26},{... | collective-permute-start | bytes 12296 | tf_op jit(solution)/shard_map/while/body/eval_jaxpr/ppermute | solution.py:14
  118.0 8.7 %all-to-all-start.2 = ((bf16[8,2,384]{2,1,0:T(2,128)(2,1)}), bf16[8,2,384]{2,1,0:T(2,128)(2,1)S(1)}, u32[]{:S(2)}, u32[]{:S(2)}) async-start(bf16[8,2,384]{2,1,0:T(2,128)(2,1)} %reshape.343), calls=%async_computation.2 | async-start | bytes 24576 | tf_op jit(solution)/shard_map/while/body/eval_jaxpr/all_to_all | solution.py:180
  137.6 8.5 %all-to-all-start.3 = ((f32[8,1,2]{2,1,0:T(1,128)}), f32[8,1,2]{2,1,0:T(1,128)S(1)}, u32[]{:S(2)}, u32[]{:S(2)}) async-start(f32[8,1,2]{2,1,0:T(1,128)} %copy.84), calls=%async_computation.3 | async-start | bytes 8192 | tf_op jit(solution)/shard_map/while/body/eval_jaxpr/all_to_all | solution.py:201
  146.1 8.6 %all-to-all-start.5 = ((f32[8,1,256]{2,1,0:T(1,128)}), f32[8,1,256]{2,1,0:T(1,128)S(1)}, u32[]{:S(2)}, u32[]{:S(2)}) async-start(f32[8,1,256]{2,1,0:T(1,128)} %bitcast.73), calls=%async_computation.5 | async-start | bytes 16384 | tf_op jit(solution)/shard_map/while/body/eval_jaxpr/all_to_all | solution.py:187
  154.9 11.8 %collective-permute-start = (bf16[1,2048]{1,0:T(2,128)(2,1)S(1)}, bf16[1,2048]{1,0:T(2,128)(2,1)S(1)}, u32[]{:S(2)}, u32[]{:S(2)}) collective-permute-start(bf16[1,2048]{1,0:T(2,128)(2,1)S(1)} %get-tuple-element.523), channel_id=1, source_target_pairs={{0,8},{8,16},{16,24},{1,9},{9,17},{17,25},{2,10},{10,18},{18,26},{... | collective-permute-start | bytes 12296 | tf_op jit(solution)/shard_map/while/body/eval_jaxpr/ppermute | solution.py:14
  191.1 8.7 %all-to-all-start.2 = ((bf16[8,2,384]{2,1,0:T(2,128)(2,1)}), bf16[8,2,384]{2,1,0:T(2,128)(2,1)S(1)}, u32[]{:S(2)}, u32[]{:S(2)}) async-start(bf16[8,2,384]{2,1,0:T(2,128)(2,1)} %reshape.343), calls=%async_computation.2 | async-start | bytes 24576 | tf_op jit(solution)/shard_map/while/body/eval_jaxpr/all_to_all | solution.py:180
  219.2 8.6 %all-to-all-start.5 = ((f32[8,1,256]{2,1,0:T(1,128)}), f32[8,1,256]{2,1,0:T(1,128)S(1)}, u32[]{:S(2)}, u32[]{:S(2)}) async-start(f32[8,1,256]{2,1,0:T(1,128)} %bitcast.73), calls=%async_computation.5 | async-start | bytes 16384 | tf_op jit(solution)/shard_map/while/body/eval_jaxpr/all_to_all | solution.py:187
  228.0 98.8 %collective-permute-start = (bf16[1,2048]{1,0:T(2,128)(2,1)S(1)}, bf16[1,2048]{1,0:T(2,128)(2,1)S(1)}, u32[]{:S(2)}, u32[]{:S(2)}) collective-permute-start(bf16[1,2048]{1,0:T(2,128)(2,1)S(1)} %get-tuple-element.523), channel_id=1, source_target_pairs={{0,8},{8,16},{16,24},{1,9},{9,17},{17,25},{2,10},{10,18},{18,26},{... | collective-permute-start | bytes 12296 | tf_op jit(solution)/shard_map/while/body/eval_jaxpr/ppermute | solution.py:14
  351.2 8.7 %all-to-all-start.2 = ((bf16[8,2,384]{2,1,0:T(2,128)(2,1)}), bf16[8,2,384]{2,1,0:T(2,128)(2,1)S(1)}, u32[]{:S(2)}, u32[]{:S(2)}) async-start(bf16[8,2,384]{2,1,0:T(2,128)(2,1)} %reshape.343), calls=%async_computation.2 | async-start | bytes 24576 | tf_op jit(solution)/shard_map/while/body/eval_jaxpr/all_to_all | solution.py:180
  412.0 8.6 %all-to-all-start.5 = ((f32[8,1,256]{2,1,0:T(1,128)}), f32[8,1,256]{2,1,0:T(1,128)S(1)}, u32[]{:S(2)}, u32[]{:S(2)}) async-start(f32[8,1,256]{2,1,0:T(1,128)} %bitcast.73), calls=%async_computation.5 | async-start | bytes 16384 | tf_op jit(solution)/shard_map/while/body/eval_jaxpr/all_to_all | solution.py:187
  420.8 11.9 %collective-permute-start = (bf16[1,2048]{1,0:T(2,128)(2,1)S(1)}, bf16[1,2048]{1,0:T(2,128)(2,1)S(1)}, u32[]{:S(2)}, u32[]{:S(2)}) collective-permute-start(bf16[1,2048]{1,0:T(2,128)(2,1)S(1)} %get-tuple-element.523), channel_id=1, source_target_pairs={{0,8},{8,16},{16,24},{1,9},{9,17},{17,25},{2,10},{10,18},{18,26},{... | collective-permute-start | bytes 12296 | tf_op jit(solution)/shard_map/while/body/eval_jaxpr/ppermute | solution.py:14
  457.0 8.7 %all-to-all-start.2 = ((bf16[8,2,384]{2,1,0:T(2,128)(2,1)}), bf16[8,2,384]{2,1,0:T(2,128)(2,1)S(1)}, u32[]{:S(2)}, u32[]{:S(2)}) async-start(bf16[8,2,384]{2,1,0:T(2,128)(2,1)} %reshape.343), calls=%async_computation.2 | async-start | bytes 24576 | tf_op jit(solution)/shard_map/while/body/eval_jaxpr/all_to_all | solution.py:180
  509.4 8.5 %all-to-all-start.3 = ((f32[8,1,2]{2,1,0:T(1,128)}), f32[8,1,2]{2,1,0:T(1,128)S(1)}, u32[]{:S(2)}, u32[]{:S(2)}) async-start(f32[8,1,2]{2,1,0:T(1,128)} %copy.84), calls=%async_computation.3 | async-start | bytes 8192 | tf_op jit(solution)/shard_map/while/body/eval_jaxpr/all_to_all | solution.py:201
  517.9 8.6 %all-to-all-start.5 = ((f32[8,1,256]{2,1,0:T(1,128)}), f32[8,1,256]{2,1,0:T(1,128)S(1)}, u32[]{:S(2)}, u32[]{:S(2)}) async-start(f32[8,1,256]{2,1,0:T(1,128)} %bitcast.73), calls=%async_computation.5 | async-start | bytes 16384 | tf_op jit(solution)/shard_map/while/body/eval_jaxpr/all_to_all | solution.py:187
  526.6 11.8 %collective-permute-start = (bf16[1,2048]{1,0:T(2,128)(2,1)S(1)}, bf16[1,2048]{1,0:T(2,128)(2,1)S(1)}, u32[]{:S(2)}, u32[]{:S(2)}) collective-permute-start(bf16[1,2048]{1,0:T(2,128)(2,1)S(1)} %get-tuple-element.523), channel_id=1, source_target_pairs={{0,8},{8,16},{16,24},{1,9},{9,17},{17,25},{2,10},{10,18},{18,26},{... | collective-permute-start | bytes 12296 | tf_op jit(solution)/shard_map/while/body/eval_jaxpr/ppermute | solution.py:14
  562.8 8.7 %all-to-all-start.2 = ((bf16[8,2,384]{2,1,0:T(2,128)(2,1)}), bf16[8,2,384]{2,1,0:T(2,128)(2,1)S(1)}, u32[]{:S(2)}, u32[]{:S(2)}) async-start(bf16[8,2,384]{2,1,0:T(2,128)(2,1)} %reshape.343), calls=%async_computation.2 | async-start | bytes 24576 | tf_op jit(solution)/shard_map/while/body/eval_jaxpr/all_to_all | solution.py:180
  615.1 8.5 %all-to-all-start.3 = ((f32[8,1,2]{2,1,0:T(1,128)}), f32[8,1,2]{2,1,0:T(1,128)S(1)}, u32[]{:S(2)}, u32[]{:S(2)}) async-start(f32[8,1,2]{2,1,0:T(1,128)} %copy.84), calls=%async_computation.3 | async-start | bytes 8192 | tf_op jit(solution)/shard_map/while/body/eval_jaxpr/all_to_all | solution.py:201
  623.6 8.6 %all-to-all-start.5 = ((f32[8,1,256]{2,1,0:T(1,128)}), f32[8,1,256]{2,1,0:T(1,128)S(1)}, u32[]{:S(2)}, u32[]{:S(2)}) async-start(f32[8,1,256]{2,1,0:T(1,128)} %bitcast.73), calls=%async_computation.5 | async-start | bytes 16384 | tf_op jit(solution)/shard_map/while/body/eval_jaxpr/all_to_all | solution.py:187
  632.4 11.9 %collective-permute-start = (bf16[1,2048]{1,0:T(2,128)(2,1)S(1)}, bf16[1,2048]{1,0:T(2,128)(2,1)S(1)}, u32[]{:S(2)}, u32[]{:S(2)}) collective-permute-start(bf16[1,2048]{1,0:T(2,128)(2,1)S(1)} %get-tuple-element.523), channel_id=1, source_target_pairs={{0,8},{8,16},{16,24},{1,9},{9,17},{17,25},{2,10},{10,18},{18,26},{... | collective-permute-start | bytes 12296 | tf_op jit(solution)/shard_map/while/body/eval_jaxpr/ppermute | solution.py:14
  668.6 8.7 %all-to-all-start.2 = ((bf16[8,2,384]{2,1,0:T(2,128)(2,1)}), bf16[8,2,384]{2,1,0:T(2,128)(2,1)S(1)}, u32[]{:S(2)}, u32[]{:S(2)}) async-start(bf16[8,2,384]{2,1,0:T(2,128)(2,1)} %reshape.343), calls=%async_computation.2 | async-start | bytes 24576 | tf_op jit(solution)/shard_map/while/body/eval_jaxpr/all_to_all | solution.py:180
  729.5 8.6 %all-to-all-start.5 = ((f32[8,1,256]{2,1,0:T(1,128)}), f32[8,1,256]{2,1,0:T(1,128)S(1)}, u32[]{:S(2)}, u32[]{:S(2)}) async-start(f32[8,1,256]{2,1,0:T(1,128)} %bitcast.73), calls=%async_computation.5 | async-start | bytes 16384 | tf_op jit(solution)/shard_map/while/body/eval_jaxpr/all_to_all | solution.py:187
  (27 other events, 232.0 us)
where the time goes:
time: 747 us; the launch traced here: 742 us
  waiting for transfers between devices  282 us (38%)
  blocking collectives  113 us (15%)
  other arithmetic  110 us (15%)
  starting transfers between devices  102 us (14%)
  local copies, waits for them, and re-layouts  96.5 us (13%)
  matrix products  32.5 us (4%)
    ppermute x7, waiting for transfers between devices, shifted(): lax.ppermute(value, axis, [(source, source + steps) for source in range(l...  150 us
    all_to_all x7, blocking collectives, apart_step(): lax.all_to_all(feature_layout(modded, groups, splits), 'head', split_axis...  58.4 us
    all_to_all x7, blocking collectives, apart_step(): lax.all_to_all(partial_sum, 'head', split_axis=0, concat_axis=0, tiled=True)  54.4 us
    select_n x4, other arithmetic, segment_attend(): new_vals = jnp.where(inside, taken[..., head_dim:], vals_buf)  46.3 us
    all_to_all x7, waiting for transfers between devices, apart_step(): lax.all_to_all(head_layout(qkv_own, groups, splits), 'head', split_axis=0...  37.3 us
    all_to_all x7, waiting for transfers between devices, apart_step(): lax.all_to_all(part_out.reshape(n_head, rows_dev, heads_dev * head_dim),...  35.9 us
    select_n x8, other arithmetic, segment_attend(): taken = jnp.transpose(jnp.take(fresh, picked, axis=0), (1, 0, 2))  33.1 us
    all_to_all x7, waiting for transfers between devices, apart_step(): lax.all_to_all(totals.reshape(n_head, rows_dev, heads_dev), 'head', split...  32 us
  transfers between devices with their start and end apart: 35, of which 35 were waited for; matrix products, arithmetic and copies ran while one was open for 2% of the time, Pallas kernels for 0%

commit v1 on v0

--- a/solution.py
+++ b/solution.py
@@ -1,11 +1,164 @@
+import functools
 import math
 
 import jax
 import jax.numpy as jnp
 from jax import lax
+from jax.experimental import pallas as pl
+from jax.experimental.pallas import tpu as pltpu
 from jax.sharding import PartitionSpec as P
 
 HEADS = 16
+MASKED = -3.0e38
+
+
+def layer_kernel(step, offsets, micro, patch, *refs):
+    n_groups = len(offsets)
+    start_ref, scale_ref, shift_ref, gate_ref, wq_ref, wkv_ref, key_ref, val_ref, held_ref = refs[:9]
+    group_refs = refs[9 : 9 + n_groups]
+    out_ref = refs[9 + n_groups]
+    stage = lax.axis_index("pipe")
+    head = lax.axis_index("head")
+    heads_dev, feat, head_dim = wq_ref.shape
+    positions = key_ref.shape[1]
+    rows, width = out_ref.shape
+
+    def column(offset):
+        return pl.multiple_of(lax.bitwise_xor(head, offset) * width, width)
+
+    @pl.when(stage != step)
+    def _():
+        out_ref[...] = held_ref[...]
+
+    @pl.when(stage == step)
+    def _():
+        pieces = []
+        for ref, group in zip(group_refs, offsets):
+            for slot, offset in enumerate(group):
+                if ref.shape[1] == feat:
+                    at = column(offset)
+                    pieces.append((at, ref[:, pl.ds(at, width)]))
+                else:
+                    pieces.append((column(offset), ref[slot * rows : (slot + 1) * rows, :]))
+        square = None
+        for _, piece in pieces:
+            value = piece.astype(jnp.float32)
+            square = value * value if square is None else square + value * value
+        meansq = jnp.sum(square, axis=-1, keepdims=True) / feat
+        inverse = lax.rsqrt(meansq + 1e-06)
+        query = [None] * heads_dev
+        fresh = [None] * heads_dev
+        for at, piece in pieces:
+            scale = 1.0 + scale_ref[:, pl.ds(at, width)]
+            shift = shift_ref[:, pl.ds(at, width)]
+            modded = (piece.astype(jnp.float32) * inverse * scale + shift).astype(jnp.bfloat16)
+            for h in range(heads_dev):
+                q = jnp.dot(modded, wq_ref[h, pl.ds(at, width), :], preferred_element_type=jnp.float32)
+                kv = jnp.dot(modded, wkv_ref[h, pl.ds(at, width), :], preferred_element_type=jnp.float32)
+                query[h] = q if query[h] is None else query[h] + q
+                fresh[h] = kv if fresh[h] is None else fresh[h] + kv
+        position = lax.broadcasted_iota(jnp.int32, (8, positions), 1)
+        patch_row = lax.rem(lax.broadcasted_iota(jnp.int32, (8, positions), 0), micro)
+        replaced = None
+        for m in range(micro):
+            relative = position - start_ref[m]
+            inside = (relative >= 0) & (relative < patch) & (patch_row >= m)
+            replaced = inside if replaced is None else replaced | inside
+        asking = lax.rem(lax.broadcasted_iota(jnp.int32, (rows, rows), 0), micro)
+        asked = lax.rem(lax.broadcasted_iota(jnp.int32, (rows, rows), 1), micro)
+        later = asked > asking
+        score_scale = 1.0 / math.sqrt(head_dim)
+        over_last = (((1,), (1,)), ((), ()))
+        attended = []
+        for h in range(heads_dev):
+            q = query[h].astype(jnp.bfloat16)
+            k = fresh[h][:, :head_dim].astype(jnp.bfloat16)
+            v = fresh[h][:, head_dim:].astype(jnp.bfloat16)
+            old = lax.dot_general(q, key_ref[h], over_last, preferred_element_type=jnp.float32)
+            old = old.reshape(rows // 8, 8, positions) * score_scale
+            old = jnp.where(replaced[None], MASKED, old).reshape(rows, positions)
+            new = lax.dot_general(q, k, over_last, preferred_element_type=jnp.float32)
+            new = jnp.where(later, MASKED, new * score_scale)
+            top = jnp.maximum(
+                jnp.max(old, axis=-1, keepdims=True), jnp.max(new, axis=-1, keepdims=True)
+            )
+            old = jnp.exp(old - top)
+            new = jnp.exp(new - top)
+            total = jnp.sum(old, axis=-1, keepdims=True) + jnp.sum(new, axis=-1, keepdims=True)
+            summed = jnp.dot(
+                old.astype(jnp.bfloat16), val_ref[h], preferred_element_type=jnp.float32
+            ) + jnp.dot(new.astype(jnp.bfloat16), v, preferred_element_type=jnp.float32)
+            attended.append(summed / total)
+        own = pl.multiple_of(head * width, width)
+        residual = pieces[0][1].astype(jnp.float32)
+        gate = gate_ref[:, pl.ds(own, width)]
+        out_ref[...] = (residual + gate * jnp.concatenate(attended, axis=1)).astype(out_ref.dtype)
+
+
+def run_layer(step, offsets, micro, patch, constants, held, groups):
+    smem = pl.BlockSpec(memory_space=pltpu.SMEM)
+    vmem = pl.BlockSpec(memory_space=pltpu.VMEM)
+    return pl.pallas_call(
+        functools.partial(layer_kernel, step, offsets, micro, patch),
+        out_shape=jax.ShapeDtypeStruct(held.shape, held.dtype),
+        in_specs=[smem] + [vmem] * (len(constants) + len(groups)),
+        out_specs=vmem,
+        compiler_params=pltpu.CompilerParams(vmem_limit_bytes=16 * 1024 * 1024),
+    )(*constants, held, *groups)
+
+
+def routed(value, route):
+    n_pipe, n_head = lax.axis_size("pipe"), lax.axis_size("head")
+    pairs = []
+    for p in range(n_pipe):
+        for h in range(n_head):
+            to_pipe, to_head = route(p, h)
+            pairs.append((p * n_head + h, to_pipe % n_pipe * n_head + to_head))
+    return lax.ppermute(value, ("pipe", "head"), pairs)
+
+
+def whole_heads(
+    patch_in, patch_start, mod_scale, mod_shift, res_gate, query_weight, kv_weight, stale_keys, stale_values
+):
+    n_head = lax.axis_size("head")
+    n_pipe = lax.axis_size("pipe")
+    micro, rows_dev, feat = patch_in.shape
+    heads_dev, head_dim = stale_keys.shape[1], stale_keys.shape[3]
+    width = heads_dev * head_dim
+    patch = rows_dev * n_head
+    rows = micro * patch
+    constants = (
+        patch_start,
+        mod_scale,
+        mod_shift,
+        res_gate,
+        query_weight[0],
+        kv_weight[0],
+        stale_keys[0],
+        stale_values[0],
+    )
+    mine = jnp.transpose(patch_in, (1, 0, 2)).reshape(rows // n_head, feat)
+    copies = jnp.broadcast_to(mine[None], (n_head,) + mine.shape)
+    gathered = lax.all_to_all(copies, "head", split_axis=0, concat_axis=0, tiled=True)
+    held = jnp.zeros((rows, width), jnp.bfloat16)
+    groups = [gathered.reshape(rows, feat)]
+    offsets = [tuple(range(n_head))]
+    for step in range(n_pipe):
+        held = run_layer(step, offsets, micro, patch, constants, held, groups)
+        if step + 1 < n_pipe:
+            value = jnp.concatenate(
+                [routed(held, lambda p, h: (p + 1, h)), routed(held, lambda p, h: (p + 1, h ^ 1))], 0
+            )
+            bit = 2
+            while bit < n_head:
+                value = jnp.concatenate([value, routed(value, lambda p, h: (p, h ^ bit))], 0)
+                bit *= 2
+            groups = [value]
+    back = lax.all_to_all(
+        held.reshape(n_head, rows // n_head, width), "head", split_axis=0, concat_axis=0, tiled=True
+    )
+    back = jnp.transpose(back.reshape(n_head, rows_dev, micro, width), (2, 1, 0, 3))
+    return back.reshape(1, micro, rows_dev, feat)
 
 
 def shifted(value, axis, steps):
@@ -220,6 +373,8 @@
 
 
 def solution(mesh):
+    n_head = mesh.shape["head"]
+    whole = n_head <= HEADS and n_head & (n_head - 1) == 0
     placed = (
         P(None, "head", None),
         P(),
@@ -232,7 +387,7 @@
         P("pipe", "head", None, None),
     )
     return jax.shard_map(
-        per_device,
+        whole_heads if whole else per_device,
         mesh=mesh,
         in_specs=placed,
         out_specs=P("pipe", None, "head", None),

time: 747 us -> 79.9 us (0.11)
  the two profiles are of different devices: /device:TPU:5 before, /device:TPU:0 now
where the time goes in v1:
time: 79.9 us; the launch traced here: 79.4 us
  waiting for transfers between devices  36.5 us (46%)
  blocking collectives  23.8 us (30%)
  local copies, waits for them, and re-layouts  9.41 us (12%)
  starting transfers between devices  5.57 us (7%)
  Pallas kernels  3.9 us (5%)
    ppermute x12, waiting for transfers between devices, routed(): return lax.ppermute(value, ('pipe', 'head'), pairs)  36.5 us
    all_to_all x1, blocking collectives, whole_heads(): lax.all_to_all(copies, 'head', split_axis=0, concat_axis=0, tiled=True)  14.4 us
    all_to_all x1, blocking collectives, whole_heads(): lax.all_to_all(held.reshape(n_head, rows // n_head, width), 'head', split...  9.38 us
    unnamed x17, local copies, waits for them, and re-layouts  8.61 us
    ppermute x12, starting transfers between devices, routed(): return lax.ppermute(value, ('pipe', 'head'), pairs)  5.57 us
    pallas_call x4, Pallas kernels, run_layer(): pl.pallas_call(functools.partial(layer_kernel, step, offsets, micro, patc...  3.9 us
  transfers between devices with their start and end apart: 12, of which 11 were waited for; matrix products, arithmetic and copies ran while one was open for 0% of the time, Pallas kernels for 0%

profile of v1, /device:TPU:0, one launch (start us, length us, event | category | flops | bytes accessed | tf_op | source)
XLA Modules:
  0.0 79.4 jit_solution(4842805970767547056)
XLA Ops:
  0.0 0.8 broadcast_in_dim.12
  0.8 14.4 %all_to_all.10 = bf16[8,4,2048]{2,1,0:T(4,128)(2,1)S(1)} all-to-all(bf16[8,4,2048]{2,1,0:T(4,128)(2,1)S(1)} %broadcast_in_dim.12), channel_id=1, replica_groups=mesh['pipe'=4,'head'=8] {'head'}, dimensions={0} | all-to-all | bytes 262144 | tf_op jit(solution)/shard_map/all_to_all | solution.py:142
  15.2 1.6 %copy-done = bf16[1,2,2048,256]{3,2,1,0:T(8,128)(2,1)S(1)} copy-done((bf16[1,2,2048,256]{3,2,1,0:T(8,128)(2,1)S(1)}, bf16[1,2,2048,256]{3,2,1,0:T(8,128)(2,1)}, u32[]{:S(2)}) %copy-start) | copy-done | bytes 2097176
  16.8 1.2 %copy-done.1 = bf16[1,2,2048,128]{3,2,1,0:T(8,128)(2,1)S(1)} copy-done((bf16[1,2,2048,128]{3,2,1,0:T(8,128)(2,1)S(1)}, bf16[1,2,2048,128]{3,2,1,0:T(8,128)(2,1)}, u32[]{:S(2)}) %copy-start.1) | copy-done | bytes 1048600
  18.0 1.2 %copy-done.2 = bf16[1,2,2048,128]{3,2,1,0:T(8,128)(2,1)S(1)} copy-done((bf16[1,2,2048,128]{3,2,1,0:T(8,128)(2,1)S(1)}, bf16[1,2,2048,128]{3,2,1,0:T(8,128)(2,1)}, u32[]{:S(2)}) %copy-start.2) | copy-done | bytes 1048600
  19.2 1.2 %copy-done.3 = bf16[1,2,2048,128]{3,2,1,0:T(8,128)(2,1)S(1)} copy-done((bf16[1,2,2048,128]{3,2,1,0:T(8,128)(2,1)S(1)}, bf16[1,2,2048,128]{3,2,1,0:T(8,128)(2,1)}, u32[]{:S(2)}) %copy-start.3) | copy-done | bytes 1048600
  20.5 0.7 copy-done.4
  21.2 0.7 copy-done.5
  21.9 0.7 copy-done.6
  23.2 2.2 %shard_map.91.refs_8_ = bf16[32,256]{1,0:T(8,128)(2,1)S(1)} custom-call(s32[4]{0:T(128)S(1)} %copy-done.7, f32[1,2048]{1,0:T(1,128)S(1)} %copy-done.4, f32[1,2048]{1,0:T(1,128)S(1)} %copy-done.5, f32[1,2048]{1,0:T(1,128)S(1)} %copy-done.6, bf16[2,2048,128]{2,1,0:T(8,128)(2,1)S(1)} %bitcast.14, bf16[2,2048,256]{2,1,0:T(8,128)(2,1)S(1)} %bitcast.10, ...), custom_call_target="tpu_custom_call" | custom-call | tf_op jit(solution)/shard_map/pallas_call | solution.py:101
  25.6 3.1 %collective-permute-done = bf16[32,256]{1,0:T(8,128)(2,1)S(1)} collective-permute-done((bf16[32,256]{1,0:T(8,128)(2,1)S(1)}, bf16[32,256]{1,0:T(8,128)(2,1)S(1)}, u32[]{:S(2)}, u32[]{:S(2)}) %collective-permute-start) | collective-permute-done | bytes 16416 | tf_op jit(solution)/shard_map/ppermute | solution.py:117
  28.7 1.0 %collective-permute-done.1 = bf16[32,256]{1,0:T(8,128)(2,1)S(1)} collective-permute-done((bf16[32,256]{1,0:T(8,128)(2,1)S(1)}, bf16[32,256]{1,0:T(8,128)(2,1)S(1)}, u32[]{:S(2)}, u32[]{:S(2)}) %collective-permute-start.1) | collective-permute-done | bytes 16416 | tf_op jit(solution)/shard_map/ppermute | solution.py:117
  29.6 3.9 %collective-permute-done.2 = bf16[64,256]{1,0:T(8,128)(2,1)S(1)} collective-permute-done((bf16[64,256]{1,0:T(8,128)(2,1)S(1)}, bf16[64,256]{1,0:T(8,128)(2,1)S(1)}, u32[]{:S(2)}, u32[]{:S(2)}) %collective-permute-start.2) | collective-permute-done | bytes 32800 | tf_op jit(solution)/shard_map/ppermute | solution.py:117
  33.9 4.9 %collective-permute-done.3 = bf16[128,256]{1,0:T(8,128)(2,1)S(1)} collective-permute-done((bf16[128,256]{1,0:T(8,128)(2,1)S(1)}, bf16[128,256]{1,0:T(8,128)(2,1)S(1)}, u32[]{:S(2)}, u32[]{:S(2)}) %collective-permute-start.3) | collective-permute-done | bytes 65568 | tf_op jit(solution)/shard_map/ppermute | solution.py:117
  39.5 0.9 %collective-permute-start.5 = (bf16[32,256]{1,0:T(8,128)(2,1)S(1)}, bf16[32,256]{1,0:T(8,128)(2,1)S(1)}, u32[]{:S(2)}, u32[]{:S(2)}) collective-permute-start(bf16[32,256]{1,0:T(8,128)(2,1)S(1)} %shard_map.92.refs_8_), channel_id=1, source_target_pairs={{0,9},{1,8},{2,11},{3,10},{4,13},{5,12},{6,15},{7,14},{8,17},{9,16... | collective-permute-start | bytes 49160 | tf_op jit(solution)/shard_map/ppermute | solution.py:117
  40.4 2.2 %collective-permute-done.4 = bf16[32,256]{1,0:T(8,128)(2,1)S(1)} collective-permute-done((bf16[32,256]{1,0:T(8,128)(2,1)S(1)}, bf16[32,256]{1,0:T(8,128)(2,1)S(1)}, u32[]{:S(2)}, u32[]{:S(2)}) %collective-permute-start.4) | collective-permute-done | bytes 16416 | tf_op jit(solution)/shard_map/ppermute | solution.py:117
  42.7 1.0 %collective-permute-done.5 = bf16[32,256]{1,0:T(8,128)(2,1)S(1)} collective-permute-done((bf16[32,256]{1,0:T(8,128)(2,1)S(1)}, bf16[32,256]{1,0:T(8,128)(2,1)S(1)}, u32[]{:S(2)}, u32[]{:S(2)}) %collective-permute-start.5) | collective-permute-done | bytes 16416 | tf_op jit(solution)/shard_map/ppermute | solution.py:117
  43.6 3.9 %collective-permute-done.6 = bf16[64,256]{1,0:T(8,128)(2,1)S(1)} collective-permute-done((bf16[64,256]{1,0:T(8,128)(2,1)S(1)}, bf16[64,256]{1,0:T(8,128)(2,1)S(1)}, u32[]{:S(2)}, u32[]{:S(2)}) %collective-permute-start.6) | collective-permute-done | bytes 32800 | tf_op jit(solution)/shard_map/ppermute | solution.py:117
  47.8 5.1 %collective-permute-done.7 = bf16[128,256]{1,0:T(8,128)(2,1)S(1)} collective-permute-done((bf16[128,256]{1,0:T(8,128)(2,1)S(1)}, bf16[128,256]{1,0:T(8,128)(2,1)S(1)}, u32[]{:S(2)}, u32[]{:S(2)}) %collective-permute-start.7) | collective-permute-done | bytes 65568 | tf_op jit(solution)/shard_map/ppermute | solution.py:117
  53.5 3.7 %collective-permute-start.9 = (bf16[32,256]{1,0:T(8,128)(2,1)S(1)}, bf16[32,256]{1,0:T(8,128)(2,1)S(1)}, u32[]{:S(2)}, u32[]{:S(2)}) collective-permute-start(bf16[32,256]{1,0:T(8,128)(2,1)S(1)} %shard_map.93.refs_8_), channel_id=1, source_target_pairs={{0,9},{1,8},{2,11},{3,10},{4,13},{5,12},{6,15},{7,14},{8,17},{9,16... | collective-permute-start | bytes 49160 | tf_op jit(solution)/shard_map/ppermute | solution.py:117
  57.3 1.4 %collective-permute-done.9 = bf16[32,256]{1,0:T(8,128)(2,1)S(1)} collective-permute-done((bf16[32,256]{1,0:T(8,128)(2,1)S(1)}, bf16[32,256]{1,0:T(8,128)(2,1)S(1)}, u32[]{:S(2)}, u32[]{:S(2)}) %collective-permute-start.9) | collective-permute-done | bytes 16416 | tf_op jit(solution)/shard_map/ppermute | solution.py:117
  58.7 4.0 %collective-permute-done.10 = bf16[64,256]{1,0:T(8,128)(2,1)S(1)} collective-permute-done((bf16[64,256]{1,0:T(8,128)(2,1)S(1)}, bf16[64,256]{1,0:T(8,128)(2,1)S(1)}, u32[]{:S(2)}, u32[]{:S(2)}) %collective-permute-start.10) | collective-permute-done | bytes 32800 | tf_op jit(solution)/shard_map/ppermute | solution.py:117
  62.7 6.0 %collective-permute-done.11 = bf16[128,256]{1,0:T(8,128)(2,1)S(1)} collective-permute-done((bf16[128,256]{1,0:T(8,128)(2,1)S(1)}, bf16[128,256]{1,0:T(8,128)(2,1)S(1)}, u32[]{:S(2)}, u32[]{:S(2)}) %collective-permute-start.11) | collective-permute-done | bytes 65568 | tf_op jit(solution)/shard_map/ppermute | solution.py:117
  69.4 9.4 %all_to_all.11 = bf16[8,4,256]{2,1,0:T(4,128)(2,1)S(1)} all-to-all(bf16[8,4,256]{2,1,0:T(4,128)(2,1)S(1)} %reshape.14), channel_id=1, replica_groups=mesh['pipe'=4,'head'=8] {'head'}, dimensions={0} | all-to-all | bytes 32768 | tf_op jit(solution)/shard_map/all_to_all | solution.py:157
  (36 shorter events, 3.9 us)
Async XLA Ops:
  15.2 1.6 %copy-start = (bf16[1,2,2048,256]{3,2,1,0:T(8,128)(2,1)S(1)}, bf16[1,2,2048,256]{3,2,1,0:T(8,128)(2,1)}, u32[]{:S(2)}) copy-start(bf16[1,2,2048,256]{3,2,1,0:T(8,128)(2,1)} %param.15) | copy-start | bytes 6291460
  16.8 1.2 %copy-start.1 = (bf16[1,2,2048,128]{3,2,1,0:T(8,128)(2,1)S(1)}, bf16[1,2,2048,128]{3,2,1,0:T(8,128)(2,1)}, u32[]{:S(2)}) copy-start(bf16[1,2,2048,128]{3,2,1,0:T(8,128)(2,1)} %param.14) | copy-start | bytes 3145732
  18.0 1.2 %copy-start.2 = (bf16[1,2,2048,128]{3,2,1,0:T(8,128)(2,1)S(1)}, bf16[1,2,2048,128]{3,2,1,0:T(8,128)(2,1)}, u32[]{:S(2)}) copy-start(bf16[1,2,2048,128]{3,2,1,0:T(8,128)(2,1)} %param.16) | copy-start | bytes 3145732
  19.2 1.2 %copy-start.3 = (bf16[1,2,2048,128]{3,2,1,0:T(8,128)(2,1)S(1)}, bf16[1,2,2048,128]{3,2,1,0:T(8,128)(2,1)}, u32[]{:S(2)}) copy-start(bf16[1,2,2048,128]{3,2,1,0:T(8,128)(2,1)} %param.17) | copy-start | bytes 3145732
  20.5 0.7 copy-start.4
  21.2 0.7 copy-start.5
  21.9 0.7 copy-start.6
  22.6 0.7 copy-start.7
  25.4 3.2 %collective-permute-start = (bf16[32,256]{1,0:T(8,128)(2,1)S(1)}, bf16[32,256]{1,0:T(8,128)(2,1)S(1)}, u32[]{:S(2)}, u32[]{:S(2)}) collective-permute-start(bf16[32,256]{1,0:T(8,128)(2,1)S(1)} %shard_map.91.refs_8_), channel_id=1, source_target_pairs={{0,8},{1,9},{2,10},{3,11},{4,12},{5,13},{6,14},{7,15},{8,16},{9,17... | collective-permute-start | bytes 49160 | tf_op jit(solution)/shard_map/ppermute | solution.py:117
  25.5 4.1 %collective-permute-start.1 = (bf16[32,256]{1,0:T(8,128)(2,1)S(1)}, bf16[32,256]{1,0:T(8,128)(2,1)S(1)}, u32[]{:S(2)}, u32[]{:S(2)}) collective-permute-start(bf16[32,256]{1,0:T(8,128)(2,1)S(1)} %shard_map.91.refs_8_), channel_id=1, source_target_pairs={{0,9},{1,8},{2,11},{3,10},{4,13},{5,12},{6,15},{7,14},{8,17},{9,16... | collective-permute-start | bytes 49160 | tf_op jit(solution)/shard_map/ppermute | solution.py:117
  29.6 3.9 %collective-permute-start.2 = (bf16[64,256]{1,0:T(8,128)(2,1)S(1)}, bf16[64,256]{1,0:T(8,128)(2,1)S(1)}, u32[]{:S(2)}, u32[]{:S(2)}) collective-permute-start(bf16[64,256]{1,0:T(8,128)(2,1)S(1)} %pad_maximum_fusion.6), channel_id=1, source_target_pairs={{0,2},{1,3},{2,0},{3,1},{4,6},{5,7},{6,4},{7,5},{8,10},{9,11},{10,... | collective-permute-start | bytes 98312 | tf_op jit(solution)/shard_map/ppermute | solution.py:117
  33.5 5.3 %collective-permute-start.3 = (bf16[128,256]{1,0:T(8,128)(2,1)S(1)}, bf16[128,256]{1,0:T(8,128)(2,1)S(1)}, u32[]{:S(2)}, u32[]{:S(2)}) collective-permute-start(bf16[128,256]{1,0:T(8,128)(2,1)S(1)} %pad_maximum_fusion.3), channel_id=1, source_target_pairs={{0,4},{1,5},{2,6},{3,7},{4,0},{5,1},{6,2},{7,3},{8,12},{9,13},{10,... | collective-permute-start | bytes 196616 | tf_op jit(solution)/shard_map/ppermute | solution.py:117
  39.4 3.2 %collective-permute-start.4 = (bf16[32,256]{1,0:T(8,128)(2,1)S(1)}, bf16[32,256]{1,0:T(8,128)(2,1)S(1)}, u32[]{:S(2)}, u32[]{:S(2)}) collective-permute-start(bf16[32,256]{1,0:T(8,128)(2,1)S(1)} %shard_map.92.refs_8_), channel_id=1, source_target_pairs={{0,8},{1,9},{2,10},{3,11},{4,12},{5,13},{6,14},{7,15},{8,16},{9,17... | collective-permute-start | bytes 49160 | tf_op jit(solution)/shard_map/ppermute | solution.py:117
  39.5 4.1 %collective-permute-start.5 = (bf16[32,256]{1,0:T(8,128)(2,1)S(1)}, bf16[32,256]{1,0:T(8,128)(2,1)S(1)}, u32[]{:S(2)}, u32[]{:S(2)}) collective-permute-start(bf16[32,256]{1,0:T(8,128)(2,1)S(1)} %shard_map.92.refs_8_), channel_id=1, source_target_pairs={{0,9},{1,8},{2,11},{3,10},{4,13},{5,12},{6,15},{7,14},{8,17},{9,16... | collective-permute-start | bytes 49160 | tf_op jit(solution)/shard_map/ppermute | solution.py:117
  43.6 3.9 %collective-permute-start.6 = (bf16[64,256]{1,0:T(8,128)(2,1)S(1)}, bf16[64,256]{1,0:T(8,128)(2,1)S(1)}, u32[]{:S(2)}, u32[]{:S(2)}) collective-permute-start(bf16[64,256]{1,0:T(8,128)(2,1)S(1)} %pad_maximum_fusion.7), channel_id=1, source_target_pairs={{0,2},{1,3},{2,0},{3,1},{4,6},{5,7},{6,4},{7,5},{8,10},{9,11},{10,... | collective-permute-start | bytes 98312 | tf_op jit(solution)/shard_map/ppermute | solution.py:117
  47.5 5.3 %collective-permute-start.7 = (bf16[128,256]{1,0:T(8,128)(2,1)S(1)}, bf16[128,256]{1,0:T(8,128)(2,1)S(1)}, u32[]{:S(2)}, u32[]{:S(2)}) collective-permute-start(bf16[128,256]{1,0:T(8,128)(2,1)S(1)} %pad_maximum_fusion.4), channel_id=1, source_target_pairs={{0,4},{1,5},{2,6},{3,7},{4,0},{5,1},{6,2},{7,3},{8,12},{9,13},{10,... | collective-permute-start | bytes 196616 | tf_op jit(solution)/shard_map/ppermute | solution.py:117
  53.4 3.8 %collective-permute-start.8 = (bf16[32,256]{1,0:T(8,128)(2,1)S(1)}, bf16[32,256]{1,0:T(8,128)(2,1)S(1)}, u32[]{:S(2)}, u32[]{:S(2)}) collective-permute-start(bf16[32,256]{1,0:T(8,128)(2,1)S(1)} %shard_map.93.refs_8_), channel_id=1, source_target_pairs={{0,8},{1,9},{2,10},{3,11},{4,12},{5,13},{6,14},{7,15},{8,16},{9,17... | collective-permute-start | bytes 49160 | tf_op jit(solution)/shard_map/ppermute | solution.py:117
  53.5 5.2 %collective-permute-start.9 = (bf16[32,256]{1,0:T(8,128)(2,1)S(1)}, bf16[32,256]{1,0:T(8,128)(2,1)S(1)}, u32[]{:S(2)}, u32[]{:S(2)}) collective-permute-start(bf16[32,256]{1,0:T(8,128)(2,1)S(1)} %shard_map.93.refs_8_), channel_id=1, source_target_pairs={{0,9},{1,8},{2,11},{3,10},{4,13},{5,12},{6,15},{7,14},{8,17},{9,16... | collective-permute-start | bytes 49160 | tf_op jit(solution)/shard_map/ppermute | solution.py:117
  58.7 4.0 %collective-permute-start.10 = (bf16[64,256]{1,0:T(8,128)(2,1)S(1)}, bf16[64,256]{1,0:T(8,128)(2,1)S(1)}, u32[]{:S(2)}, u32[]{:S(2)}) collective-permute-start(bf16[64,256]{1,0:T(8,128)(2,1)S(1)} %pad_maximum_fusion.8), channel_id=1, source_target_pairs={{0,2},{1,3},{2,0},{3,1},{4,6},{5,7},{6,4},{7,5},{8,10},{9,11},{10,... | collective-permute-start | bytes 98312 | tf_op jit(solution)/shard_map/ppermute | solution.py:117
  62.7 6.0 %collective-permute-start.11 = (bf16[128,256]{1,0:T(8,128)(2,1)S(1)}, bf16[128,256]{1,0:T(8,128)(2,1)S(1)}, u32[]{:S(2)}, u32[]{:S(2)}) collective-permute-start(bf16[128,256]{1,0:T(8,128)(2,1)S(1)} %pad_maximum_fusion.5), channel_id=1, source_target_pairs={{0,4},{1,5},{2,6},{3,7},{4,0},{5,1},{6,2},{7,3},{8,12},{9,13},{10,... | collective-permute-start | bytes 196616 | tf_op jit(solution)/shard_map/ppermute | solution.py:117

commit v2 on v1

--- a/solution.py
+++ b/solution.py
@@ -10,36 +10,122 @@
 
 HEADS = 16
 MASKED = -3.0e38
-
-
-def layer_kernel(step, offsets, micro, patch, *refs):
-    n_groups = len(offsets)
-    start_ref, scale_ref, shift_ref, gate_ref, wq_ref, wkv_ref, key_ref, val_ref, held_ref = refs[:9]
-    group_refs = refs[9 : 9 + n_groups]
-    out_ref = refs[9 + n_groups]
+LIMIT = 4 * 1024 * 1024
+SMEM = pl.BlockSpec(memory_space=pltpu.SMEM)
+VMEM = pl.BlockSpec(memory_space=pltpu.VMEM)
+ANY = pl.BlockSpec(memory_space=pl.ANY)
+
+
+def origin(head, kind, amount, count):
+    if kind == "turn":
+        return (head - amount + count) % count
+    return head ^ amount
+
+
+def traced(maps, head, count):
+    for kind, amount in maps:
+        head = origin(head, kind, amount, count)
+    return head
+
+
+def distinct(offsets, count):
+    slots = {}
+    for slot, maps in enumerate(offsets):
+        slots.setdefault(tuple(traced(maps, head, count) for head in range(count)), (slot, maps))
+    own = tuple(range(count))
+    return [slots[own]] + [slots[key] for key in slots if key != own]
+
+
+def routed(value, kind, amount, shift):
+    n_pipe, n_head = lax.axis_size("pipe"), lax.axis_size("head")
+    pairs = []
+    for p in range(n_pipe):
+        for h in range(n_head):
+            source = p * n_head + origin(h, kind, amount, n_head)
+            pairs.append((source, (p + shift) % n_pipe * n_head + h))
+    return lax.ppermute(value, ("pipe", "head"), pairs)
+
+
+def exchange(block, plan):
+    value, offsets = block, [()]
+    for shift, moves in plan:
+        parts, known = [], []
+        for kind, amount in moves:
+            if shift == 0 and amount == 0:
+                parts.append(value)
+                known += offsets
+            else:
+                parts.append(routed(value, kind, amount, shift))
+                known += [((kind, amount),) + maps for maps in offsets]
+        value, offsets = jnp.concatenate(parts, 0), known
+    return value, offsets
+
+
+def load_kernel(micro, patch, start_ref, *refs):
+    count = (len(refs) - 2) // 2
+    sources, results = refs[:count], refs[count : 2 * count]
+    hidden_ref, sems = refs[2 * count], refs[2 * count + 1]
+    copies = [
+        pltpu.make_async_copy(source, result, sems.at[index])
+        for index, (source, result) in enumerate(zip(sources, results))
+    ]
+    for copy in copies:
+        copy.start()
+    position = lax.broadcasted_iota(jnp.int32, hidden_ref.shape, 1)
+    patch_row = lax.rem(lax.broadcasted_iota(jnp.int32, hidden_ref.shape, 0), micro)
+    hidden = jnp.zeros(hidden_ref.shape, jnp.int32)
+    for m in range(micro):
+        relative = position - start_ref[m]
+        inside = (relative >= 0) & (relative < patch) & (patch_row >= m)
+        hidden = jnp.where(inside, 1, hidden)
+    hidden_ref[...] = hidden
+    for copy in copies:
+        copy.wait()
+
+
+def load(patch_start, arrays, micro, patch, positions):
+    shapes = [pltpu.VMEM(array.shape, array.dtype) for array in arrays]
+    shapes.append(pltpu.VMEM((8, positions), jnp.int32))
+    return pl.pallas_call(
+        functools.partial(load_kernel, micro, patch),
+        out_shape=shapes,
+        in_specs=[SMEM] + [ANY] * len(arrays),
+        out_specs=[VMEM] * len(shapes),
+        scratch_shapes=[pltpu.SemaphoreType.DMA((len(arrays),))],
+        compiler_params=pltpu.CompilerParams(vmem_limit_bytes=LIMIT),
+        cost_estimate=pl.CostEstimate(flops=0, bytes_accessed=10 * 1024 * 1024, transcendentals=0),
+    )(patch_start, *(pltpu.with_memory_space_constraint(array, pltpu.HBM) for array in arrays))
+
+
+def layer_kernel(step, slots, micro, *refs):
+    scale_ref, shift_ref, gate_ref, wq_ref, wkv_ref, key_ref, val_ref, hidden_ref, held_ref, in_ref = refs[:10]
+    out_ref = refs[10]
     stage = lax.axis_index("pipe")
     head = lax.axis_index("head")
+    n_head = lax.axis_size("head")
     heads_dev, feat, head_dim = wq_ref.shape
     positions = key_ref.shape[1]
-    rows, width = out_ref.shape
-
-    def column(offset):
-        return pl.multiple_of(lax.bitwise_xor(head, offset) * width, width)
+    rows, width = held_ref.shape
+    by_token = len(in_ref.shape) == 3
+    own = pl.multiple_of(head * width, width)
 
     @pl.when(stage != step)
     def _():
-        out_ref[...] = held_ref[...]
+        out_ref[...] = held_ref[...].reshape(out_ref.shape)
 
     @pl.when(stage == step)
     def _():
         pieces = []
-        for ref, group in zip(group_refs, offsets):
-            for slot, offset in enumerate(group):
-                if ref.shape[1] == feat:
-                    at = column(offset)
-                    pieces.append((at, ref[:, pl.ds(at, width)]))
-                else:
-                    pieces.append((column(offset), ref[slot * rows : (slot + 1) * rows, :]))
+        if by_token:
+            for index in range(n_head):
+                at = index * width
+                pieces.append((at, in_ref[:, :, at : at + width].astype(jnp.float32).reshape(rows, width)))
+            residual = in_ref[:, :, pl.ds(own, width)].astype(jnp.float32).reshape(rows, width)
+        else:
+            for slot, maps in slots:
+                at = pl.multiple_of(traced(maps, head, n_head) * width, width)
+                pieces.append((at, in_ref[slot * rows : (slot + 1) * rows, :]))
+            residual = pieces[0][1]
         square = None
         for _, piece in pieces:
             value = piece.astype(jnp.float32)
@@ -57,13 +143,7 @@
                 kv = jnp.dot(modded, wkv_ref[h, pl.ds(at, width), :], preferred_element_type=jnp.float32)
                 query[h] = q if query[h] is None else query[h] + q
                 fresh[h] = kv if fresh[h] is None else fresh[h] + kv
-        position = lax.broadcasted_iota(jnp.int32, (8, positions), 1)
-        patch_row = lax.rem(lax.broadcasted_iota(jnp.int32, (8, positions), 0), micro)
-        replaced = None
-        for m in range(micro):
-            relative = position - start_ref[m]
-            inside = (relative >= 0) & (relative < patch) & (patch_row >= m)
-            replaced = inside if replaced is None else replaced | inside
+        hidden = hidden_ref[...] != 0
         asking = lax.rem(lax.broadcasted_iota(jnp.int32, (rows, rows), 0), micro)
         asked = lax.rem(lax.broadcasted_iota(jnp.int32, (rows, rows), 1), micro)
         later = asked > asking
@@ -76,7 +156,7 @@
             v = fresh[h][:, head_dim:].astype(jnp.bfloat16)
             old = lax.dot_general(q, key_ref[h], over_last, preferred_element_type=jnp.float32)
             old = old.reshape(rows // 8, 8, positions) * score_scale
-            old = jnp.where(replaced[None], MASKED, old).reshape(rows, positions)
+            old = jnp.where(hidden[None], MASKED, old).reshape(rows, positions)
             new = lax.dot_general(q, k, over_last, preferred_element_type=jnp.float32)
             new = jnp.where(later, MASKED, new * score_scale)
             top = jnp.maximum(
@@ -89,32 +169,34 @@
                 old.astype(jnp.bfloat16), val_ref[h], preferred_element_type=jnp.float32
             ) + jnp.dot(new.astype(jnp.bfloat16), v, preferred_element_type=jnp.float32)
             attended.append(summed / total)
-        own = pl.multiple_of(head * width, width)
-        residual = pieces[0][1].astype(jnp.float32)
         gate = gate_ref[:, pl.ds(own, width)]
-        out_ref[...] = (residual + gate * jnp.concatenate(attended, axis=1)).astype(out_ref.dtype)
-
-
-def run_layer(step, offsets, micro, patch, constants, held, groups):
-    smem = pl.BlockSpec(memory_space=pltpu.SMEM)
-    vmem = pl.BlockSpec(memory_space=pltpu.VMEM)
+        result = residual.astype(jnp.float32) + gate * jnp.concatenate(attended, axis=1)
+        if by_token:
+            order_ref = refs[11]
+            part = rows // n_head
+            for slot, maps in slots:
+                order_ref[traced(maps, head, n_head)] = result[slot * part : (slot + 1) * part, :]
+            result = order_ref[...].reshape(rows, width)
+        out_ref[...] = result.reshape(out_ref.shape).astype(out_ref.dtype)
+
+
+def run_layer(step, slots, micro, constants, held, blocks, out_shape):
+    rows, width = held.shape
+    n_head = lax.axis_size("head")
     return pl.pallas_call(
-        functools.partial(layer_kernel, step, offsets, micro, patch),
-        out_shape=jax.ShapeDtypeStruct(held.shape, held.dtype),
-        in_specs=[smem] + [vmem] * (len(constants) + len(groups)),
-        out_specs=vmem,
-        compiler_params=pltpu.CompilerParams(vmem_limit_bytes=16 * 1024 * 1024),
-    )(*constants, held, *groups)
-
-
-def routed(value, route):
-    n_pipe, n_head = lax.axis_size("pipe"), lax.axis_size("head")
-    pairs = []
-    for p in range(n_pipe):
-        for h in range(n_head):
-            to_pipe, to_head = route(p, h)
-            pairs.append((p * n_head + h, to_pipe % n_pipe * n_head + to_head))
-    return lax.ppermute(value, ("pipe", "head"), pairs)
+        functools.partial(layer_kernel, step, slots, micro),
+        out_shape=jax.ShapeDtypeStruct(out_shape, held.dtype),
+        in_specs=[VMEM] * (len(constants) + 2),
+        out_specs=VMEM,
+        scratch_shapes=[pltpu.VMEM((n_head, rows // n_head, width), jnp.float32)],
+        compiler_params=pltpu.CompilerParams(vmem_limit_bytes=LIMIT),
+    )(*(pltpu.with_memory_space_constraint(array, pltpu.VMEM) for array in constants), held, blocks)
+
+
+def plans(n_head):
+    pair = (("swap", 0), ("swap", n_head // 2))
+    rest = tuple(("swap", k) for k in [0] + list(range(n_head // 2 - 1, 0, -1)))
+    return ((0, pair), (0, rest)), ((1, pair), (0, rest))
 
 
 def whole_heads(
@@ -123,40 +205,22 @@
     n_head = lax.axis_size("head")
     n_pipe = lax.axis_size("pipe")
     micro, rows_dev, feat = patch_in.shape
-    heads_dev, head_dim = stale_keys.shape[1], stale_keys.shape[3]
+    heads_dev, positions, head_dim = stale_keys.shape[1:]
     width = heads_dev * head_dim
     patch = rows_dev * n_head
     rows = micro * patch
-    constants = (
-        patch_start,
-        mod_scale,
-        mod_shift,
-        res_gate,
-        query_weight[0],
-        kv_weight[0],
-        stale_keys[0],
-        stale_values[0],
-    )
-    mine = jnp.transpose(patch_in, (1, 0, 2)).reshape(rows // n_head, feat)
-    copies = jnp.broadcast_to(mine[None], (n_head,) + mine.shape)
-    gathered = lax.all_to_all(copies, "head", split_axis=0, concat_axis=0, tiled=True)
+    entry_plan, step_plan = plans(n_head)
+    mine = jnp.transpose(patch_in, (1, 0, 2)).reshape(1, rows // n_head, feat)
+    arrays = (mod_scale, mod_shift, res_gate, query_weight[0], kv_weight[0], stale_keys[0], stale_values[0])
+    constants = load(patch_start, arrays, micro, patch, positions)
+    value, offsets = exchange(mine, entry_plan)
     held = jnp.zeros((rows, width), jnp.bfloat16)
-    groups = [gathered.reshape(rows, feat)]
-    offsets = [tuple(range(n_head))]
     for step in range(n_pipe):
-        held = run_layer(step, offsets, micro, patch, constants, held, groups)
+        out_shape = held.shape if step + 1 < n_pipe else (n_head, rows // n_head, width)
+        held = run_layer(step, distinct(offsets, n_head), micro, constants, held, value, out_shape)
         if step + 1 < n_pipe:
-            value = jnp.concatenate(
-                [routed(held, lambda p, h: (p + 1, h)), routed(held, lambda p, h: (p + 1, h ^ 1))], 0
-            )
-            bit = 2
-            while bit < n_head:
-                value = jnp.concatenate([value, routed(value, lambda p, h: (p, h ^ bit))], 0)
-                bit *= 2
-            groups = [value]
-    back = lax.all_to_all(
-        held.reshape(n_head, rows // n_head, width), "head", split_axis=0, concat_axis=0, tiled=True
-    )
+            value, offsets = exchange(held, step_plan)
+    back = lax.all_to_all(held, "head", split_axis=0, concat_axis=0, tiled=True)
     back = jnp.transpose(back.reshape(n_head, rows_dev, micro, width), (2, 1, 0, 3))
     return back.reshape(1, micro, rows_dev, feat)
 

time: 79.9 us -> 62.4 us (0.78)
  starting transfers between devices: 5.57 us -> 21.5 us
  blocking collectives: 23.8 us -> 10.4 us
  waiting for transfers between devices: 36.5 us -> 23.2 us
  local copies, waits for them, and re-layouts: 9.41 us -> 2.15 us
  Pallas kernels: 3.9 us -> 4.8 us
    ppermute x12 -> x19, starting transfers between devices: 5.57 us -> 21.5 us  [routed(): return lax.ppermute(value, ('pipe', 'head'), pairs)]
    all_to_all x2 -> x1, blocking collectives: 23.8 us -> 10.4 us  [whole_heads(): back = lax.all_to_all(held, 'head', split_axis=0, concat_axis=0, tiled=True)]
    ppermute x12 -> x19, waiting for transfers between devices: 36.5 us -> 23.2 us  [routed(): return lax.ppermute(value, ('pipe', 'head'), pairs)]
    unnamed x17 -> x18, local copies, waits for them, and re-layouts: 8.61 us -> 2.1 us
    pallas_call x4 -> x5, Pallas kernels: 3.9 us -> 4.8 us  [the longest x1 3.14 us: load(): pl.pallas_call(functools.partial(load_kernel, micro, patch), out_shape=sh...]
  transfers between devices with their start and end apart: 12 -> 19, of which waited for: 11 -> 18; matrix products, arithmetic and copies ran while one was open for 0% -> 1% of each run, Pallas kernels for 0% -> 5%
where the time goes in v2:
time: 62.4 us; the launch traced here: 62.1 us
  waiting for transfers between devices  23.2 us (37%)
  starting transfers between devices  21.5 us (34%)
  blocking collectives  10.4 us (17%)
  Pallas kernels  4.8 us (8%)
  local copies, waits for them, and re-layouts  2.15 us (3%)
    ppermute x19, waiting for transfers between devices, routed(): return lax.ppermute(value, ('pipe', 'head'), pairs)  23.2 us
    ppermute x19, starting transfers between devices, routed(): return lax.ppermute(value, ('pipe', 'head'), pairs)  21.5 us
    all_to_all x1, blocking collectives, whole_heads(): back = lax.all_to_all(held, 'head', split_axis=0, concat_axis=0, tiled=True)  10.4 us
    pallas_call x1, Pallas kernels, load(): pl.pallas_call(functools.partial(load_kernel, micro, patch), out_shape=sh...  3.14 us
    unnamed x18, local copies, waits for them, and re-layouts  2.1 us
    pallas_call x4, Pallas kernels, run_layer(): pl.pallas_call(functools.partial(layer_kernel, step, slots, micro), out_s...  1.66 us
  transfers between devices with their start and end apart: 19, of which 18 were waited for; matrix products, arithmetic and copies ran while one was open for 1% of the time, Pallas kernels for 5%

profile of v2, /device:TPU:0, one launch (start us, length us, event | category | flops | bytes accessed | tf_op | source)
XLA Modules:
  0.0 62.1 jit_solution(15649478555943962537)
XLA Ops:
  0.0 4.0 %collective-permute-start = (bf16[1,4,2048]{2,1,0:T(4,128)(2,1)}, bf16[1,4,2048]{2,1,0:T(4,128)(2,1)S(1)}, u32[]{:S(2)}, u32[]{:S(2)}) collective-permute-start(bf16[1,4,2048]{2,1,0:T(4,128)(2,1)} %bitcast.16), channel_id=1, source_target_pairs={{4,0},{5,1},{6,2},{7,3},{0,4},{1,5},{2,6},{3,7},{12,8},{13,9},{14,... | collective-permute-start | bytes 49160 | tf_op jit(solution)/shard_map/ppermute | solution.py:46
  4.0 0.8 %constant_dynamic-update-slice_fusion.4 = bf16[8,4,2048]{2,1,0:T(4,128)(2,1)S(1)} fusion(bf16[4,1,2048]{2,0,1:T(4,128)(2,1)} %param.9), kind=kLoop, calls=%fused_computation.4 | loop fusion | bytes 32768
  5.5 3.1 %shard_map.91 = (f32[1,2048]{1,0:T(1,128)S(1)}, f32[1,2048]{1,0:T(1,128)S(1)}, f32[1,2048]{1,0:T(1,128)S(1)}, bf16[2,2048,128]{2,1,0:T(8,128)(2,1)S(1)}, bf16[2,...) custom-call(s32[4]{0:T(128)S(1)} %copy-done, ...), custom_call_target="tpu_custom_call" | custom-call | bytes 10485760 | tf_op jit(solution)/shard_map/pallas_call | solution.py:89
  8.7 2.6 %collective-permute-start.1 = (bf16[2,4,2048]{2,1,0:T(4,128)(2,1)S(1)}, bf16[2,4,2048]{2,1,0:T(4,128)(2,1)S(1)}, u32[]{:S(2)}, u32[]{:S(2)}) collective-permute-start(bf16[2,4,2048]{2,1,0:T(4,128)(2,1)S(1)} %pad_maximum_fusion), channel_id=1, source_target_pairs={{3,0},{2,1},{1,2},{0,3},{7,4},{6,5},{5,6},{4,7},{11,8},{10,9},{9,1... | collective-permute-start | bytes 98312 | tf_op jit(solution)/shard_map/ppermute | solution.py:46
  12.2 1.6 %collective-permute-done.1 = bf16[2,4,2048]{2,1,0:T(4,128)(2,1)S(1)} collective-permute-done((bf16[2,4,2048]{2,1,0:T(4,128)(2,1)S(1)}, bf16[2,4,2048]{2,1,0:T(4,128)(2,1)S(1)}, u32[]{:S(2)}, u32[]{:S(2)}) %collective-permute-start.1) | collective-permute-done | bytes 32800 | tf_op jit(solution)/shard_map/ppermute | solution.py:46
  13.9 1.2 %collective-permute-done.2 = bf16[2,4,2048]{2,1,0:T(4,128)(2,1)S(1)} collective-permute-done((bf16[2,4,2048]{2,1,0:T(4,128)(2,1)S(1)}, bf16[2,4,2048]{2,1,0:T(4,128)(2,1)S(1)}, u32[]{:S(2)}, u32[]{:S(2)}) %collective-permute-start.2) | collective-permute-done | bytes 32800 | tf_op jit(solution)/shard_map/ppermute | solution.py:46
  15.6 1.7 %shard_map.92.refs_8_ = bf16[32,256]{1,0:T(8,128)(2,1)S(1)} custom-call(f32[1,2048]{1,0:T(1,128)S(1)} %get-tuple-element.13.refs_0_, f32[1,2048]{1,0:T(1,128)S(1)} %get-tuple-element.14.refs_1_, f32[1,2048]{1,0:T(1,128)S(1)} %get-tuple-element.15.refs_2_, bf16[2,2048,128]{2,1,0:T(8,128)(2,1)S(1)} %get-tuple-element.16.refs_3_, ...), custom_call_target="tpu_custom_call" | custom-call | tf_op jit(solution)/shard_map/pallas_call | solution.py:186
  17.4 3.1 %collective-permute-done.4 = bf16[32,256]{1,0:T(8,128)(2,1)S(1)} collective-permute-done((bf16[32,256]{1,0:T(8,128)(2,1)S(1)}, bf16[32,256]{1,0:T(8,128)(2,1)S(1)}, u32[]{:S(2)}, u32[]{:S(2)}) %collective-permute-start.4) | collective-permute-done | bytes 16416 | tf_op jit(solution)/shard_map/ppermute | solution.py:46
  20.5 1.9 %collective-permute-done.5 = bf16[32,256]{1,0:T(8,128)(2,1)S(1)} collective-permute-done((bf16[32,256]{1,0:T(8,128)(2,1)S(1)}, bf16[32,256]{1,0:T(8,128)(2,1)S(1)}, u32[]{:S(2)}, u32[]{:S(2)}) %collective-permute-start.5) | collective-permute-done | bytes 16416 | tf_op jit(solution)/shard_map/ppermute | solution.py:46
  22.4 1.5 %collective-permute-start.6 = (bf16[64,256]{1,0:T(8,128)(2,1)S(1)}, bf16[64,256]{1,0:T(8,128)(2,1)S(1)}, u32[]{:S(2)}, u32[]{:S(2)}) collective-permute-start(bf16[64,256]{1,0:T(8,128)(2,1)S(1)} %get-tuple-element.29), channel_id=1, source_target_pairs={{3,0},{2,1},{1,2},{0,3},{7,4},{6,5},{5,6},{4,7},{11,8},{10,9},{9,1... | collective-permute-start | bytes 98312 | tf_op jit(solution)/shard_map/ppermute | solution.py:46
  24.4 1.5 %collective-permute-start.8 = (bf16[64,256]{1,0:T(8,128)(2,1)S(1)}, bf16[64,256]{1,0:T(8,128)(2,1)S(1)}, u32[]{:S(2)}, u32[]{:S(2)}) collective-permute-start(bf16[64,256]{1,0:T(8,128)(2,1)S(1)} %get-tuple-element.29), channel_id=1, source_target_pairs={{1,0},{0,1},{3,2},{2,3},{5,4},{4,5},{7,6},{6,7},{9,8},{8,9},{11,10... | collective-permute-start | bytes 98312 | tf_op jit(solution)/shard_map/ppermute | solution.py:46
  25.9 1.3 %collective-permute-done.6 = bf16[64,256]{1,0:T(8,128)(2,1)S(1)} collective-permute-done((bf16[64,256]{1,0:T(8,128)(2,1)S(1)}, bf16[64,256]{1,0:T(8,128)(2,1)S(1)}, u32[]{:S(2)}, u32[]{:S(2)}) %collective-permute-start.6) | collective-permute-done | bytes 32800 | tf_op jit(solution)/shard_map/ppermute | solution.py:46
  28.3 0.8 %collective-permute-start.10 = (bf16[32,256]{1,0:T(8,128)(2,1)S(1)}, bf16[32,256]{1,0:T(8,128)(2,1)S(1)}, u32[]{:S(2)}, u32[]{:S(2)}) collective-permute-start(bf16[32,256]{1,0:T(8,128)(2,1)S(1)} %shard_map.93.refs_8_), channel_id=1, source_target_pairs={{4,8},{5,9},{6,10},{7,11},{0,12},{1,13},{2,14},{3,15},{12,16},{13,... | collective-permute-start | bytes 49160 | tf_op jit(solution)/shard_map/ppermute | solution.py:46
  29.1 2.3 %collective-permute-done.9 = bf16[32,256]{1,0:T(8,128)(2,1)S(1)} collective-permute-done((bf16[32,256]{1,0:T(8,128)(2,1)S(1)}, bf16[32,256]{1,0:T(8,128)(2,1)S(1)}, u32[]{:S(2)}, u32[]{:S(2)}) %collective-permute-start.9) | collective-permute-done | bytes 16416 | tf_op jit(solution)/shard_map/ppermute | solution.py:46
  31.4 1.9 %collective-permute-done.10 = bf16[32,256]{1,0:T(8,128)(2,1)S(1)} collective-permute-done((bf16[32,256]{1,0:T(8,128)(2,1)S(1)}, bf16[32,256]{1,0:T(8,128)(2,1)S(1)}, u32[]{:S(2)}, u32[]{:S(2)}) %collective-permute-start.10) | collective-permute-done | bytes 16416 | tf_op jit(solution)/shard_map/ppermute | solution.py:46
  33.3 2.5 %collective-permute-start.11 = (bf16[64,256]{1,0:T(8,128)(2,1)S(1)}, bf16[64,256]{1,0:T(8,128)(2,1)S(1)}, u32[]{:S(2)}, u32[]{:S(2)}) collective-permute-start(bf16[64,256]{1,0:T(8,128)(2,1)S(1)} %get-tuple-element.25), channel_id=1, source_target_pairs={{3,0},{2,1},{1,2},{0,3},{7,4},{6,5},{5,6},{4,7},{11,8},{10,9},{9,1... | collective-permute-start | bytes 98312 | tf_op jit(solution)/shard_map/ppermute | solution.py:46
  36.8 1.4 %collective-permute-done.11 = bf16[64,256]{1,0:T(8,128)(2,1)S(1)} collective-permute-done((bf16[64,256]{1,0:T(8,128)(2,1)S(1)}, bf16[64,256]{1,0:T(8,128)(2,1)S(1)}, u32[]{:S(2)}, u32[]{:S(2)}) %collective-permute-start.11) | collective-permute-done | bytes 32800 | tf_op jit(solution)/shard_map/ppermute | solution.py:46
  38.2 1.6 %collective-permute-done.12 = bf16[64,256]{1,0:T(8,128)(2,1)S(1)} collective-permute-done((bf16[64,256]{1,0:T(8,128)(2,1)S(1)}, bf16[64,256]{1,0:T(8,128)(2,1)S(1)}, u32[]{:S(2)}, u32[]{:S(2)}) %collective-permute-start.12) | collective-permute-done | bytes 32800 | tf_op jit(solution)/shard_map/ppermute | solution.py:46
  40.2 2.5 %collective-permute-start.15 = (bf16[32,256]{1,0:T(8,128)(2,1)S(1)}, bf16[32,256]{1,0:T(8,128)(2,1)S(1)}, u32[]{:S(2)}, u32[]{:S(2)}) collective-permute-start(bf16[32,256]{1,0:T(8,128)(2,1)S(1)} %shard_map.94.refs_8_), channel_id=1, source_target_pairs={{4,8},{5,9},{6,10},{7,11},{0,12},{1,13},{2,14},{3,15},{12,16},{13,... | collective-permute-start | bytes 49160 | tf_op jit(solution)/shard_map/ppermute | solution.py:46
  43.4 1.9 %collective-permute-done.15 = bf16[32,256]{1,0:T(8,128)(2,1)S(1)} collective-permute-done((bf16[32,256]{1,0:T(8,128)(2,1)S(1)}, bf16[32,256]{1,0:T(8,128)(2,1)S(1)}, u32[]{:S(2)}, u32[]{:S(2)}) %collective-permute-start.15) | collective-permute-done | bytes 16416 | tf_op jit(solution)/shard_map/ppermute | solution.py:46
  45.2 1.5 %collective-permute-start.16 = (bf16[64,256]{1,0:T(8,128)(2,1)S(1)}, bf16[64,256]{1,0:T(8,128)(2,1)S(1)}, u32[]{:S(2)}, u32[]{:S(2)}) collective-permute-start(bf16[64,256]{1,0:T(8,128)(2,1)S(1)} %get-tuple-element.21), channel_id=1, source_target_pairs={{3,0},{2,1},{1,2},{0,3},{7,4},{6,5},{5,6},{4,7},{11,8},{10,9},{9,1... | collective-permute-start | bytes 98312 | tf_op jit(solution)/shard_map/ppermute | solution.py:46
  47.2 1.5 %collective-permute-start.18 = (bf16[64,256]{1,0:T(8,128)(2,1)S(1)}, bf16[64,256]{1,0:T(8,128)(2,1)S(1)}, u32[]{:S(2)}, u32[]{:S(2)}) collective-permute-start(bf16[64,256]{1,0:T(8,128)(2,1)S(1)} %get-tuple-element.21), channel_id=1, source_target_pairs={{1,0},{0,1},{3,2},{2,3},{5,4},{4,5},{7,6},{6,7},{9,8},{8,9},{11,10... | collective-permute-start | bytes 98312 | tf_op jit(solution)/shard_map/ppermute | solution.py:46
  48.7 1.6 %collective-permute-done.16 = bf16[64,256]{1,0:T(8,128)(2,1)S(1)} collective-permute-done((bf16[64,256]{1,0:T(8,128)(2,1)S(1)}, bf16[64,256]{1,0:T(8,128)(2,1)S(1)}, u32[]{:S(2)}, u32[]{:S(2)}) %collective-permute-start.16) | collective-permute-done | bytes 32800 | tf_op jit(solution)/shard_map/ppermute | solution.py:46
  51.1 10.4 %all_to_all.5 = bf16[8,4,256]{2,1,0:T(4,128)(2,1)S(1)} all-to-all(bf16[8,4,256]{2,1,0:T(4,128)(2,1)S(1)} %shard_map.95), channel_id=1, replica_groups=mesh['pipe'=4,'head'=8] {'head'}, dimensions={0} | all-to-all | bytes 32768 | tf_op jit(solution)/shard_map/all_to_all | solution.py:223
  (47 shorter events, 7.9 us)
Async XLA Ops:
  0.0 8.6 %collective-permute-start = (bf16[1,4,2048]{2,1,0:T(4,128)(2,1)}, bf16[1,4,2048]{2,1,0:T(4,128)(2,1)S(1)}, u32[]{:S(2)}, u32[]{:S(2)}) collective-permute-start(bf16[1,4,2048]{2,1,0:T(4,128)(2,1)} %bitcast.16), channel_id=1, source_target_pairs={{4,0},{5,1},{6,2},{7,3},{0,4},{1,5},{2,6},{3,7},{12,8},{13,9},{14,... | collective-permute-start | bytes 49160 | tf_op jit(solution)/shard_map/ppermute | solution.py:46
  4.8 0.7 %copy-start = (s32[4]{0:T(128)S(1)}, s32[4]{0:T(128)}, u32[]{:S(2)}) copy-start(s32[4]{0:T(128)} %start_ref.1) | copy-start | bytes 52
  5.5 3.2 %copy-start.1 = (bf16[4,1,2048]{2,0,1:T(4,128)(2,1)S(1)}, bf16[4,1,2048]{2,0,1:T(4,128)(2,1)}, u32[]{:S(2)}) copy-start(bf16[4,1,2048]{2,0,1:T(4,128)(2,1)} %param.9) | copy-start | bytes 49156
  8.7 5.2 %collective-permute-start.1 = (bf16[2,4,2048]{2,1,0:T(4,128)(2,1)S(1)}, bf16[2,4,2048]{2,1,0:T(4,128)(2,1)S(1)}, u32[]{:S(2)}, u32[]{:S(2)}) collective-permute-start(bf16[2,4,2048]{2,1,0:T(4,128)(2,1)S(1)} %pad_maximum_fusion), channel_id=1, source_target_pairs={{3,0},{2,1},{1,2},{0,3},{7,4},{6,5},{5,6},{4,7},{11,8},{10,9},{9,1... | collective-permute-start | bytes 98312 | tf_op jit(solution)/shard_map/ppermute | solution.py:46
  11.2 3.9 %collective-permute-start.2 = (bf16[2,4,2048]{2,1,0:T(4,128)(2,1)S(1)}, bf16[2,4,2048]{2,1,0:T(4,128)(2,1)S(1)}, u32[]{:S(2)}, u32[]{:S(2)}) collective-permute-start(bf16[2,4,2048]{2,1,0:T(4,128)(2,1)S(1)} %pad_maximum_fusion), channel_id=1, source_target_pairs={{2,0},{3,1},{0,2},{1,3},{6,4},{7,5},{4,6},{5,7},{10,8},{11,9},{8,1... | collective-permute-start | bytes 98312 | tf_op jit(solution)/shard_map/ppermute | solution.py:46
  11.7 3.9 %collective-permute-start.3 = (bf16[2,4,2048]{2,1,0:T(4,128)(2,1)S(1)}, bf16[2,4,2048]{2,1,0:T(4,128)(2,1)S(1)}, u32[]{:S(2)}, u32[]{:S(2)}) collective-permute-start(bf16[2,4,2048]{2,1,0:T(4,128)(2,1)S(1)} %pad_maximum_fusion), channel_id=1, source_target_pairs={{1,0},{0,1},{3,2},{2,3},{5,4},{4,5},{7,6},{6,7},{9,8},{8,9},{11,10... | collective-permute-start | bytes 98312 | tf_op jit(solution)/shard_map/ppermute | solution.py:46
  17.3 3.2 %collective-permute-start.4 = (bf16[32,256]{1,0:T(8,128)(2,1)S(1)}, bf16[32,256]{1,0:T(8,128)(2,1)S(1)}, u32[]{:S(2)}, u32[]{:S(2)}) collective-permute-start(bf16[32,256]{1,0:T(8,128)(2,1)S(1)} %shard_map.92.refs_8_), channel_id=1, source_target_pairs={{0,8},{1,9},{2,10},{3,11},{4,12},{5,13},{6,14},{7,15},{8,16},{9,17... | collective-permute-start | bytes 49160 | tf_op jit(solution)/shard_map/ppermute | solution.py:46
  17.3 5.0 %collective-permute-start.5 = (bf16[32,256]{1,0:T(8,128)(2,1)S(1)}, bf16[32,256]{1,0:T(8,128)(2,1)S(1)}, u32[]{:S(2)}, u32[]{:S(2)}) collective-permute-start(bf16[32,256]{1,0:T(8,128)(2,1)S(1)} %shard_map.92.refs_8_), channel_id=1, source_target_pairs={{4,8},{5,9},{6,10},{7,11},{0,12},{1,13},{2,14},{3,15},{12,16},{13,... | collective-permute-start | bytes 49160 | tf_op jit(solution)/shard_map/ppermute | solution.py:46
  22.4 4.8 %collective-permute-start.6 = (bf16[64,256]{1,0:T(8,128)(2,1)S(1)}, bf16[64,256]{1,0:T(8,128)(2,1)S(1)}, u32[]{:S(2)}, u32[]{:S(2)}) collective-permute-start(bf16[64,256]{1,0:T(8,128)(2,1)S(1)} %get-tuple-element.29), channel_id=1, source_target_pairs={{3,0},{2,1},{1,2},{0,3},{7,4},{6,5},{5,6},{4,7},{11,8},{10,9},{9,1... | collective-permute-start | bytes 98312 | tf_op jit(solution)/shard_map/ppermute | solution.py:46
  23.9 3.9 %collective-permute-start.7 = (bf16[64,256]{1,0:T(8,128)(2,1)S(1)}, bf16[64,256]{1,0:T(8,128)(2,1)S(1)}, u32[]{:S(2)}, u32[]{:S(2)}) collective-permute-start(bf16[64,256]{1,0:T(8,128)(2,1)S(1)} %get-tuple-element.29), channel_id=1, source_target_pairs={{2,0},{3,1},{0,2},{1,3},{6,4},{7,5},{4,6},{5,7},{10,8},{11,9},{8,1... | collective-permute-start | bytes 98312 | tf_op jit(solution)/shard_map/ppermute | solution.py:46
  24.4 3.9 %collective-permute-start.8 = (bf16[64,256]{1,0:T(8,128)(2,1)S(1)}, bf16[64,256]{1,0:T(8,128)(2,1)S(1)}, u32[]{:S(2)}, u32[]{:S(2)}) collective-permute-start(bf16[64,256]{1,0:T(8,128)(2,1)S(1)} %get-tuple-element.29), channel_id=1, source_target_pairs={{1,0},{0,1},{3,2},{2,3},{5,4},{4,5},{7,6},{6,7},{9,8},{8,9},{11,10... | collective-permute-start | bytes 98312 | tf_op jit(solution)/shard_map/ppermute | solution.py:46
  28.3 3.2 %collective-permute-start.9 = (bf16[32,256]{1,0:T(8,128)(2,1)S(1)}, bf16[32,256]{1,0:T(8,128)(2,1)S(1)}, u32[]{:S(2)}, u32[]{:S(2)}) collective-permute-start(bf16[32,256]{1,0:T(8,128)(2,1)S(1)} %shard_map.93.refs_8_), channel_id=1, source_target_pairs={{0,8},{1,9},{2,10},{3,11},{4,12},{5,13},{6,14},{7,15},{8,16},{9,17... | collective-permute-start | bytes 49160 | tf_op jit(solution)/shard_map/ppermute | solution.py:46
  28.3 5.0 %collective-permute-start.10 = (bf16[32,256]{1,0:T(8,128)(2,1)S(1)}, bf16[32,256]{1,0:T(8,128)(2,1)S(1)}, u32[]{:S(2)}, u32[]{:S(2)}) collective-permute-start(bf16[32,256]{1,0:T(8,128)(2,1)S(1)} %shard_map.93.refs_8_), channel_id=1, source_target_pairs={{4,8},{5,9},{6,10},{7,11},{0,12},{1,13},{2,14},{3,15},{12,16},{13,... | collective-permute-start | bytes 49160 | tf_op jit(solution)/shard_map/ppermute | solution.py:46
  33.3 4.8 %collective-permute-start.11 = (bf16[64,256]{1,0:T(8,128)(2,1)S(1)}, bf16[64,256]{1,0:T(8,128)(2,1)S(1)}, u32[]{:S(2)}, u32[]{:S(2)}) collective-permute-start(bf16[64,256]{1,0:T(8,128)(2,1)S(1)} %get-tuple-element.25), channel_id=1, source_target_pairs={{3,0},{2,1},{1,2},{0,3},{7,4},{6,5},{5,6},{4,7},{11,8},{10,9},{9,1... | collective-permute-start | bytes 98312 | tf_op jit(solution)/shard_map/ppermute | solution.py:46
  35.8 3.9 %collective-permute-start.12 = (bf16[64,256]{1,0:T(8,128)(2,1)S(1)}, bf16[64,256]{1,0:T(8,128)(2,1)S(1)}, u32[]{:S(2)}, u32[]{:S(2)}) collective-permute-start(bf16[64,256]{1,0:T(8,128)(2,1)S(1)} %get-tuple-element.25), channel_id=1, source_target_pairs={{2,0},{3,1},{0,2},{1,3},{6,4},{7,5},{4,6},{5,7},{10,8},{11,9},{8,1... | collective-permute-start | bytes 98312 | tf_op jit(solution)/shard_map/ppermute | solution.py:46
  36.3 3.9 %collective-permute-start.13 = (bf16[64,256]{1,0:T(8,128)(2,1)S(1)}, bf16[64,256]{1,0:T(8,128)(2,1)S(1)}, u32[]{:S(2)}, u32[]{:S(2)}) collective-permute-start(bf16[64,256]{1,0:T(8,128)(2,1)S(1)} %get-tuple-element.25), channel_id=1, source_target_pairs={{1,0},{0,1},{3,2},{2,3},{5,4},{4,5},{7,6},{6,7},{9,8},{8,9},{11,10... | collective-permute-start | bytes 98312 | tf_op jit(solution)/shard_map/ppermute | solution.py:46
  40.2 3.2 %collective-permute-start.14 = (bf16[32,256]{1,0:T(8,128)(2,1)S(1)}, bf16[32,256]{1,0:T(8,128)(2,1)S(1)}, u32[]{:S(2)}, u32[]{:S(2)}) collective-permute-start(bf16[32,256]{1,0:T(8,128)(2,1)S(1)} %shard_map.94.refs_8_), channel_id=1, source_target_pairs={{0,8},{1,9},{2,10},{3,11},{4,12},{5,13},{6,14},{7,15},{8,16},{9,17... | collective-permute-start | bytes 49160 | tf_op jit(solution)/shard_map/ppermute | solution.py:46
  40.2 5.0 %collective-permute-start.15 = (bf16[32,256]{1,0:T(8,128)(2,1)S(1)}, bf16[32,256]{1,0:T(8,128)(2,1)S(1)}, u32[]{:S(2)}, u32[]{:S(2)}) collective-permute-start(bf16[32,256]{1,0:T(8,128)(2,1)S(1)} %shard_map.94.refs_8_), channel_id=1, source_target_pairs={{4,8},{5,9},{6,10},{7,11},{0,12},{1,13},{2,14},{3,15},{12,16},{13,... | collective-permute-start | bytes 49160 | tf_op jit(solution)/shard_map/ppermute | solution.py:46
  45.2 5.0 %collective-permute-start.16 = (bf16[64,256]{1,0:T(8,128)(2,1)S(1)}, bf16[64,256]{1,0:T(8,128)(2,1)S(1)}, u32[]{:S(2)}, u32[]{:S(2)}) collective-permute-start(bf16[64,256]{1,0:T(8,128)(2,1)S(1)} %get-tuple-element.21), channel_id=1, source_target_pairs={{3,0},{2,1},{1,2},{0,3},{7,4},{6,5},{5,6},{4,7},{11,8},{10,9},{9,1... | collective-permute-start | bytes 98312 | tf_op jit(solution)/shard_map/ppermute | solution.py:46
  46.8 3.9 %collective-permute-start.17 = (bf16[64,256]{1,0:T(8,128)(2,1)S(1)}, bf16[64,256]{1,0:T(8,128)(2,1)S(1)}, u32[]{:S(2)}, u32[]{:S(2)}) collective-permute-start(bf16[64,256]{1,0:T(8,128)(2,1)S(1)} %get-tuple-element.21), channel_id=1, source_target_pairs={{2,0},{3,1},{0,2},{1,3},{6,4},{7,5},{4,6},{5,7},{10,8},{11,9},{8,1... | collective-permute-start | bytes 98312 | tf_op jit(solution)/shard_map/ppermute | solution.py:46
  47.2 3.9 %collective-permute-start.18 = (bf16[64,256]{1,0:T(8,128)(2,1)S(1)}, bf16[64,256]{1,0:T(8,128)(2,1)S(1)}, u32[]{:S(2)}, u32[]{:S(2)}) collective-permute-start(bf16[64,256]{1,0:T(8,128)(2,1)S(1)} %get-tuple-element.21), channel_id=1, source_target_pairs={{1,0},{0,1},{3,2},{2,3},{5,4},{4,5},{7,6},{6,7},{9,8},{8,9},{11,10... | collective-permute-start | bytes 98312 | tf_op jit(solution)/shard_map/ppermute | solution.py:46

commit v3 on v2

--- a/solution.py
+++ b/solution.py
@@ -19,6 +19,12 @@
 def origin(head, kind, amount, count):
     if kind == "turn":
         return (head - amount + count) % count
+    if kind == "ring":
+        half = count // 2
+        place = head // 2 + (head % 2) * (count - 1 - 2 * (head // 2))
+        place = (place - amount + count) % count
+        outer = place // half
+        return 2 * (place + outer * (count - 1 - 2 * place)) + outer
     return head ^ amount
 
 
@@ -36,41 +42,81 @@
     return [slots[own]] + [slots[key] for key in slots if key != own]
 
 
-def routed(value, kind, amount, shift):
+def routed(value, kind, amount, shift, stage, turn):
     n_pipe, n_head = lax.axis_size("pipe"), lax.axis_size("head")
+    target = (stage + shift) % n_pipe
+    onto = {p: (p + shift) % n_pipe for p in range(n_pipe)}
+    if shift and turn > 1 and n_pipe % 2 == 0:
+        rest = [p for p in range(n_pipe) if p not in (stage, target)]
+        onto = {stage: target, target: stage}
+        for first, second in zip(rest[::2], rest[1::2]):
+            onto[first], onto[second] = second, first
     pairs = []
     for p in range(n_pipe):
         for h in range(n_head):
-            source = p * n_head + origin(h, kind, amount, n_head)
-            pairs.append((source, (p + shift) % n_pipe * n_head + h))
+            if p == stage:
+                source = origin(h, kind, amount, n_head)
+            else:
+                source = h if shift else origin(h, "swap", 1, n_head)
+            pairs.append((p * n_head + source, onto[p] * n_head + h))
     return lax.ppermute(value, ("pipe", "head"), pairs)
 
 
-def exchange(block, plan):
-    value, offsets = block, [()]
+def exchange(value, plan, stage, own=None, offsets=((),)):
+    own = value if own is None else own
     for shift, moves in plan:
-        parts, known = [], []
+        parts, known, turn = [], [], 0
         for kind, amount in moves:
-            if shift == 0 and amount == 0:
-                parts.append(value)
+            if kind == "keep":
+                parts.append(own)
                 known += offsets
             else:
-                parts.append(routed(value, kind, amount, shift))
+                parts.append(routed(value, kind, amount, shift, stage, turn))
                 known += [((kind, amount),) + maps for maps in offsets]
+                turn += 1
         value, offsets = jnp.concatenate(parts, 0), known
+        own = value
+        stage = (stage + shift) % lax.axis_size("pipe")
     return value, offsets
 
 
-def load_kernel(micro, patch, start_ref, *refs):
-    count = (len(refs) - 2) // 2
-    sources, results = refs[:count], refs[count : 2 * count]
-    hidden_ref, sems = refs[2 * count], refs[2 * count + 1]
+def copied(pairs, sems):
     copies = [
         pltpu.make_async_copy(source, result, sems.at[index])
-        for index, (source, result) in enumerate(zip(sources, results))
+        for index, (source, result) in enumerate(pairs)
     ]
     for copy in copies:
         copy.start()
+    return copies
+
+
+def weight_kernel(scale_in, shift_in, gate_in, wq_in, wkv_in, own_in, *refs):
+    scale_ref, shift_ref, gate_ref, weight_ref, own_ref, sems = refs
+    heads_dev, _, head_dim = wq_in.shape
+    width = heads_dev * head_dim
+    pairs = [(own_in, own_ref)]
+    for h in range(heads_dev):
+        begin = h * head_dim
+        pairs.append((wq_in.at[h], weight_ref.at[:, begin : begin + head_dim]))
+        for part in range(2):
+            begin += width
+            source = wkv_in.at[h, :, part * head_dim : (part + 1) * head_dim]
+            pairs.append((source, weight_ref.at[:, begin : begin + head_dim]))
+    pairs += [(scale_in, scale_ref), (shift_in, shift_ref), (gate_in, gate_ref)]
+    for copy in copied(pairs, sems):
+        copy.wait()
+
+
+def cache_kernel(micro, patch, start_in, key_in, val_in, after_ref, *refs):
+    key_ref, val_ref, hidden_ref, start_ref, sems = refs
+    heads_dev, _, head_dim = key_in.shape
+    pairs = [(start_in, start_ref)]
+    for h in range(heads_dev):
+        lanes = slice(h * head_dim, (h + 1) * head_dim)
+        pairs.append((key_in.at[h], key_ref.at[:, lanes]))
+        pairs.append((val_in.at[h], val_ref.at[:, lanes]))
+    copies = copied(pairs, sems)
+    copies[0].wait()
     position = lax.broadcasted_iota(jnp.int32, hidden_ref.shape, 1)
     patch_row = lax.rem(lax.broadcasted_iota(jnp.int32, hidden_ref.shape, 0), micro)
     hidden = jnp.zeros(hidden_ref.shape, jnp.int32)
@@ -79,33 +125,30 @@
         inside = (relative >= 0) & (relative < patch) & (patch_row >= m)
         hidden = jnp.where(inside, 1, hidden)
     hidden_ref[...] = hidden
-    for copy in copies:
+    for copy in copies[1:]:
         copy.wait()
 
 
-def load(patch_start, arrays, micro, patch, positions):
-    shapes = [pltpu.VMEM(array.shape, array.dtype) for array in arrays]
-    shapes.append(pltpu.VMEM((8, positions), jnp.int32))
+def loaded(kernel, arrays, shapes, scratch, copies, cost, after=()):
     return pl.pallas_call(
-        functools.partial(load_kernel, micro, patch),
-        out_shape=shapes,
-        in_specs=[SMEM] + [ANY] * len(arrays),
+        kernel,
+        out_shape=[pltpu.VMEM(shape, dtype) for shape, dtype in shapes],
+        in_specs=[ANY] * (len(arrays) + len(after)),
         out_specs=[VMEM] * len(shapes),
-        scratch_shapes=[pltpu.SemaphoreType.DMA((len(arrays),))],
+        scratch_shapes=scratch + [pltpu.SemaphoreType.DMA((copies,))],
         compiler_params=pltpu.CompilerParams(vmem_limit_bytes=LIMIT),
-        cost_estimate=pl.CostEstimate(flops=0, bytes_accessed=10 * 1024 * 1024, transcendentals=0),
-    )(patch_start, *(pltpu.with_memory_space_constraint(array, pltpu.HBM) for array in arrays))
-
-
-def layer_kernel(step, slots, micro, *refs):
-    scale_ref, shift_ref, gate_ref, wq_ref, wkv_ref, key_ref, val_ref, hidden_ref, held_ref, in_ref = refs[:10]
-    out_ref = refs[10]
+        cost_estimate=pl.CostEstimate(flops=0, bytes_accessed=cost, transcendentals=0),
+    )(*(pltpu.with_memory_space_constraint(array, pltpu.HBM) for array in arrays), *after)
+
+
+def layer_kernel(step, slots, micro, head_dim, *refs):
+    scale_ref, shift_ref, gate_ref, weight_ref, key_ref, val_ref, hidden_ref, held_ref, in_ref, out_ref = refs[:10]
     stage = lax.axis_index("pipe")
     head = lax.axis_index("head")
     n_head = lax.axis_size("head")
-    heads_dev, feat, head_dim = wq_ref.shape
-    positions = key_ref.shape[1]
+    feat, positions = weight_ref.shape[0], key_ref.shape[0]
     rows, width = held_ref.shape
+    heads_dev = width // head_dim
     by_token = len(in_ref.shape) == 3
     own = pl.multiple_of(head * width, width)
 
@@ -132,47 +175,46 @@
             square = value * value if square is None else square + value * value
         meansq = jnp.sum(square, axis=-1, keepdims=True) / feat
         inverse = lax.rsqrt(meansq + 1e-06)
-        query = [None] * heads_dev
-        fresh = [None] * heads_dev
+        projected = None
         for at, piece in pieces:
             scale = 1.0 + scale_ref[:, pl.ds(at, width)]
             shift = shift_ref[:, pl.ds(at, width)]
             modded = (piece.astype(jnp.float32) * inverse * scale + shift).astype(jnp.bfloat16)
-            for h in range(heads_dev):
-                q = jnp.dot(modded, wq_ref[h, pl.ds(at, width), :], preferred_element_type=jnp.float32)
-                kv = jnp.dot(modded, wkv_ref[h, pl.ds(at, width), :], preferred_element_type=jnp.float32)
-                query[h] = q if query[h] is None else query[h] + q
-                fresh[h] = kv if fresh[h] is None else fresh[h] + kv
+            term = jnp.dot(modded, weight_ref[pl.ds(at, width), :], preferred_element_type=jnp.float32)
+            projected = term if projected is None else projected + term
+        projected = projected.astype(jnp.bfloat16)
+        query, fresh_keys, fresh_vals = (projected[:, part * width : (part + 1) * width] for part in range(3))
+        lane_head = lax.broadcasted_iota(jnp.int32, (rows, width), 1) // head_dim
+        queries = jnp.concatenate(
+            [jnp.where(lane_head == h, query, jnp.zeros_like(query)) for h in range(heads_dev)], axis=0
+        )
+        asked_rows = heads_dev * rows
         hidden = hidden_ref[...] != 0
-        asking = lax.rem(lax.broadcasted_iota(jnp.int32, (rows, rows), 0), micro)
-        asked = lax.rem(lax.broadcasted_iota(jnp.int32, (rows, rows), 1), micro)
+        asking = lax.rem(lax.broadcasted_iota(jnp.int32, (asked_rows, rows), 0), micro)
+        asked = lax.rem(lax.broadcasted_iota(jnp.int32, (asked_rows, rows), 1), micro)
         later = asked > asking
         score_scale = 1.0 / math.sqrt(head_dim)
         over_last = (((1,), (1,)), ((), ()))
-        attended = []
-        for h in range(heads_dev):
-            q = query[h].astype(jnp.bfloat16)
-            k = fresh[h][:, :head_dim].astype(jnp.bfloat16)
-            v = fresh[h][:, head_dim:].astype(jnp.bfloat16)
-            old = lax.dot_general(q, key_ref[h], over_last, preferred_element_type=jnp.float32)
-            old = old.reshape(rows // 8, 8, positions) * score_scale
-            old = jnp.where(hidden[None], MASKED, old).reshape(rows, positions)
-            new = lax.dot_general(q, k, over_last, preferred_element_type=jnp.float32)
-            new = jnp.where(later, MASKED, new * score_scale)
-            top = jnp.maximum(
-                jnp.max(old, axis=-1, keepdims=True), jnp.max(new, axis=-1, keepdims=True)
-            )
-            old = jnp.exp(old - top)
-            new = jnp.exp(new - top)
-            total = jnp.sum(old, axis=-1, keepdims=True) + jnp.sum(new, axis=-1, keepdims=True)
-            summed = jnp.dot(
-                old.astype(jnp.bfloat16), val_ref[h], preferred_element_type=jnp.float32
-            ) + jnp.dot(new.astype(jnp.bfloat16), v, preferred_element_type=jnp.float32)
-            attended.append(summed / total)
+        old = lax.dot_general(queries, key_ref[...], over_last, preferred_element_type=jnp.float32)
+        old = old.reshape(asked_rows // 8, 8, positions) * score_scale
+        old = jnp.where(hidden[None], MASKED, old).reshape(asked_rows, positions)
+        new = lax.dot_general(queries, fresh_keys, over_last, preferred_element_type=jnp.float32)
+        new = jnp.where(later, MASKED, new * score_scale)
+        top = jnp.maximum(jnp.max(old, axis=-1, keepdims=True), jnp.max(new, axis=-1, keepdims=True))
+        old = jnp.exp(old - top)
+        new = jnp.exp(new - top)
+        total = jnp.sum(old, axis=-1, keepdims=True) + jnp.sum(new, axis=-1, keepdims=True)
+        summed = jnp.dot(
+            old.astype(jnp.bfloat16), val_ref[...], preferred_element_type=jnp.float32
+        ) + jnp.dot(new.astype(jnp.bfloat16), fresh_vals, preferred_element_type=jnp.float32)
+        averaged = summed / total
+        attended = [
+            averaged[h * rows : (h + 1) * rows, h * head_dim : (h + 1) * head_dim] for h in range(heads_dev)
+        ]
         gate = gate_ref[:, pl.ds(own, width)]
         result = residual.astype(jnp.float32) + gate * jnp.concatenate(attended, axis=1)
         if by_token:
-            order_ref = refs[11]
+            order_ref = refs[10]
             part = rows // n_head
             for slot, maps in slots:
                 order_ref[traced(maps, head, n_head)] = result[slot * part : (slot + 1) * part, :]
@@ -180,11 +222,11 @@
         out_ref[...] = result.reshape(out_ref.shape).astype(out_ref.dtype)
 
 
-def run_layer(step, slots, micro, constants, held, blocks, out_shape):
+def run_layer(step, slots, micro, head_dim, constants, held, blocks, out_shape):
     rows, width = held.shape
     n_head = lax.axis_size("head")
     return pl.pallas_call(
-        functools.partial(layer_kernel, step, slots, micro),
+        functools.partial(layer_kernel, step, slots, micro, head_dim),
         out_shape=jax.ShapeDtypeStruct(out_shape, held.dtype),
         in_specs=[VMEM] * (len(constants) + 2),
         out_specs=VMEM,
@@ -194,9 +236,10 @@
 
 
 def plans(n_head):
-    pair = (("swap", 0), ("swap", n_head // 2))
-    rest = tuple(("swap", k) for k in [0] + list(range(n_head // 2 - 1, 0, -1)))
-    return ((0, pair), (0, rest)), ((1, pair), (0, rest))
+    keep = ("keep", 0)
+    far = tuple(("swap", k) for k in range(n_head - 2, 0, -2))
+    entry = ((1, (keep,) + far), (0, (keep, ("swap", 1))))
+    return entry, ((1, tuple(("swap", k) for k in range(n_head - 1, -1, -1))),)
 
 
 def whole_heads(
@@ -205,21 +248,40 @@
     n_head = lax.axis_size("head")
     n_pipe = lax.axis_size("pipe")
     micro, rows_dev, feat = patch_in.shape
-    heads_dev, positions, head_dim = stale_keys.shape[1:]
+    heads_dev, head_dim = stale_keys.shape[1], stale_keys.shape[3]
     width = heads_dev * head_dim
     patch = rows_dev * n_head
     rows = micro * patch
     entry_plan, step_plan = plans(n_head)
     mine = jnp.transpose(patch_in, (1, 0, 2)).reshape(1, rows // n_head, feat)
-    arrays = (mod_scale, mod_shift, res_gate, query_weight[0], kv_weight[0], stale_keys[0], stale_values[0])
-    constants = load(patch_start, arrays, micro, patch, positions)
-    value, offsets = exchange(mine, entry_plan)
+    positions = stale_keys.shape[2]
+    row, half = (mod_scale.shape, mod_scale.dtype), jnp.bfloat16
+    *params, own = loaded(
+        weight_kernel,
+        (mod_scale, mod_shift, res_gate, query_weight[0], kv_weight[0], mine),
+        [row] * 3 + [((feat, 3 * width), half), (mine.shape, half)],
+        [],
+        4 + 3 * heads_dev,
+        6 * feat * 3 * width,
+    )
+    value, offsets = exchange(mine, entry_plan[:1], n_pipe - 1, own)
+    caches = loaded(
+        functools.partial(cache_kernel, micro, patch),
+        (patch_start, stale_keys[0], stale_values[0]),
+        [((positions, width), half)] * 2 + [((8, positions), jnp.int32)],
+        [pltpu.SMEM(patch_start.shape, patch_start.dtype)],
+        1 + 2 * heads_dev,
+        6 * positions * 2 * width,
+        (value,),
+    )
+    value, offsets = exchange(value, entry_plan[1:], 0, offsets=offsets)
+    constants = (*params, *caches)
     held = jnp.zeros((rows, width), jnp.bfloat16)
     for step in range(n_pipe):
         out_shape = held.shape if step + 1 < n_pipe else (n_head, rows // n_head, width)
-        held = run_layer(step, distinct(offsets, n_head), micro, constants, held, value, out_shape)
+        held = run_layer(step, distinct(offsets, n_head), micro, head_dim, constants, held, value, out_shape)
         if step + 1 < n_pipe:
-            value, offsets = exchange(held, step_plan)
+            value, offsets = exchange(held, step_plan, step)
     back = lax.all_to_all(held, "head", split_axis=0, concat_axis=0, tiled=True)
     back = jnp.transpose(back.reshape(n_head, rows_dev, micro, width), (2, 1, 0, 3))
     return back.reshape(1, micro, rows_dev, feat)

time: 62.4 us -> 51.8 us (0.83)
  the two profiles are of different devices: /device:TPU:0 before, /device:TPU:5 now
where the time goes in v3:
time: 51.8 us; the launch traced here: 51.6 us
  starting transfers between devices  29.3 us (57%)
  blocking collectives  8.2 us (16%)
  waiting for transfers between devices  7.88 us (15%)
  Pallas kernels  5.25 us (10%)
  local copies, waits for them, and re-layouts  0.78 us (2%)
    ppermute x28, starting transfers between devices, routed(): return lax.ppermute(value, ('pipe', 'head'), pairs)  29.3 us
    all_to_all x1, blocking collectives, whole_heads(): back = lax.all_to_all(held, 'head', split_axis=0, concat_axis=0, tiled=True)  8.2 us
    ppermute x28, waiting for transfers between devices, routed(): return lax.ppermute(value, ('pipe', 'head'), pairs)  7.88 us
    pallas_call x2, Pallas kernels, loaded(): pl.pallas_call(kernel, out_shape=[pltpu.VMEM(shape, dtype) for shape, dty...  3.5 us
    pallas_call x4, Pallas kernels, run_layer(): pl.pallas_call(functools.partial(layer_kernel, step, slots, micro, head_d...  1.75 us
  transfers between devices with their start and end apart: 28, of which 11 were waited for; matrix products, arithmetic and copies ran while one was open for 0% of the time, Pallas kernels for 7%

profile of v3, /device:TPU:5, one launch (start us, length us, event | category | flops | bytes accessed | tf_op | source)
XLA Modules:
  0.0 51.6 jit_solution(12477156931987237926)
XLA Ops:
  0.0 3.8 %collective-permute-start = (bf16[1,4,2048]{2,1,0:T(4,128)(2,1)}, bf16[1,4,2048]{2,1,0:T(4,128)(2,1)S(1)}, u32[]{:S(2)}, u32[]{:S(2)}) collective-permute-start(bf16[1,4,2048]{2,1,0:T(4,128)(2,1)} %bitcast.15), channel_id=1, source_target_pairs={{0,8},{1,9},{2,10},{3,11},{4,12},{5,13},{6,14},{7,15},{8,16},{9,17... | collective-permute-start | bytes 49160 | tf_op jit(solution)/shard_map/ppermute | solution.py:62
  3.8 1.9 %shard_map.91 = (f32[1,2048]{1,0:T(1,128)S(1)}, f32[1,2048]{1,0:T(1,128)S(1)}, f32[1,2048]{1,0:T(1,128)S(1)}, bf16[2048,768]{1,0:T(8,128)(2,1)S(1)}, bf16[1,4,2048]{2,1,0:T(4,128)(2,1)S(1)}) custom-call(f32[1,2048]{1,0:T(1,128)} %scale_in.1, f32[1,2048]{1,0:T(1,128)} %shift_in.1, f32[1,2048]{1,0:T(1,128)} %gate_in.1, bf16[2,2048,128]{2,1,0:T(8,128)(2,1)} %bitcast.11, ...), custom_call_target="tpu_custom_call" | custom-call | bytes 9437184 | tf_op jit(solution)/shard_map/pallas_call | solution.py:133
  5.9 1.4 %collective-permute-done.2 = bf16[1,4,2048]{2,1,0:T(4,128)(2,1)S(1)} collective-permute-done((bf16[1,4,2048]{2,1,0:T(4,128)(2,1)}, bf16[1,4,2048]{2,1,0:T(4,128)(2,1)S(1)}, u32[]{:S(2)}, u32[]{:S(2)}) %collective-permute-start.2) | collective-permute-done | bytes 16416 | tf_op jit(solution)/shard_map/ppermute | solution.py:62
  7.3 1.3 %collective-permute-start.3 = (bf16[4,4,2048]{2,1,0:T(4,128)(2,1)S(1)}, bf16[4,4,2048]{2,1,0:T(4,128)(2,1)S(1)}, u32[]{:S(2)}, u32[]{:S(2)}) collective-permute-start(bf16[4,4,2048]{2,1,0:T(4,128)(2,1)S(1)} %get-tuple-element.22.after_ref), channel_id=1, source_target_pairs={{1,0},{0,1},{3,2},{2,3},{5,4},{4,5},{7,6},{6,7},{9,8},{8,9},{11,10... | collective-permute-start | bytes 196616 | tf_op jit(solution)/shard_map/ppermute | solution.py:62
  8.6 1.6 %shard_map.92 = (bf16[2048,256]{1,0:T(8,128)(2,1)S(1)}, bf16[2048,256]{1,0:T(8,128)(2,1)S(1)}, s32[8,2048]{1,0:T(8,128)S(1)}) custom-call(s32[4]{0:T(128)} %start_in.1, bf16[2,2048,128]{2,1,0:T(8,128)(2,1)} %bitcast.12, bf16[2,2048,128]{2,1,0:T(8,128)(2,1)} %bitcast.13, bf16[4,4,2048]{2,1,0:T(4,128)(2,1)S(1)} %get-tuple-element.22.after_ref), custom_call_target="tpu_custom_call" | custom-call | bytes 6291456 | tf_op jit(solution)/shard_map/pallas_call | solution.py:133
  10.6 3.5 %collective-permute-start.4 = (bf16[32,256]{1,0:T(8,128)(2,1)S(1)}, bf16[32,256]{1,0:T(8,128)(2,1)S(1)}, u32[]{:S(2)}, u32[]{:S(2)}) collective-permute-start(bf16[32,256]{1,0:T(8,128)(2,1)S(1)} %shard_map.93.refs_7_), channel_id=1, source_target_pairs={{7,8},{6,9},{5,10},{4,11},{3,12},{2,13},{1,14},{0,15},{8,16},{9,17... | collective-permute-start | bytes 49160 | tf_op jit(solution)/shard_map/ppermute | solution.py:62
  14.1 0.4 collective-permute-start.6
  14.6 0.4 collective-permute-start.8
  16.8 4.8 %collective-permute-start.12 = (bf16[32,256]{1,0:T(8,128)(2,1)S(1)}, bf16[32,256]{1,0:T(8,128)(2,1)S(1)}, u32[]{:S(2)}, u32[]{:S(2)}) collective-permute-start(bf16[32,256]{1,0:T(8,128)(2,1)S(1)} %shard_map.94.refs_7_), channel_id=1, source_target_pairs={{0,8},{1,9},{2,10},{3,11},{4,12},{5,13},{6,14},{7,15},{15,16},{14,... | collective-permute-start | bytes 49160 | tf_op jit(solution)/shard_map/ppermute | solution.py:62
  21.6 2.7 %collective-permute-start.13 = (bf16[32,256]{1,0:T(8,128)(2,1)S(1)}, bf16[32,256]{1,0:T(8,128)(2,1)S(1)}, u32[]{:S(2)}, u32[]{:S(2)}) collective-permute-start(bf16[32,256]{1,0:T(8,128)(2,1)S(1)} %shard_map.94.refs_7_), channel_id=1, source_target_pairs={{0,8},{1,9},{2,10},{3,11},{4,12},{5,13},{6,14},{7,15},{14,16},{15,... | collective-permute-start | bytes 49160 | tf_op jit(solution)/shard_map/ppermute | solution.py:62
  24.3 1.7 %collective-permute-start.15 = (bf16[32,256]{1,0:T(8,128)(2,1)S(1)}, bf16[32,256]{1,0:T(8,128)(2,1)S(1)}, u32[]{:S(2)}, u32[]{:S(2)}) collective-permute-start(bf16[32,256]{1,0:T(8,128)(2,1)S(1)} %shard_map.94.refs_7_), channel_id=1, source_target_pairs={{0,24},{1,25},{2,26},{3,27},{4,28},{5,29},{6,30},{7,31},{12,16},{1... | collective-permute-start | bytes 49160 | tf_op jit(solution)/shard_map/ppermute | solution.py:62
  26.0 1.7 %collective-permute-start.17 = (bf16[32,256]{1,0:T(8,128)(2,1)S(1)}, bf16[32,256]{1,0:T(8,128)(2,1)S(1)}, u32[]{:S(2)}, u32[]{:S(2)}) collective-permute-start(bf16[32,256]{1,0:T(8,128)(2,1)S(1)} %shard_map.94.refs_7_), channel_id=1, source_target_pairs={{0,24},{1,25},{2,26},{3,27},{4,28},{5,29},{6,30},{7,31},{10,16},{1... | collective-permute-start | bytes 49160 | tf_op jit(solution)/shard_map/ppermute | solution.py:62
  27.8 1.7 %collective-permute-start.19 = (bf16[32,256]{1,0:T(8,128)(2,1)S(1)}, bf16[32,256]{1,0:T(8,128)(2,1)S(1)}, u32[]{:S(2)}, u32[]{:S(2)}) collective-permute-start(bf16[32,256]{1,0:T(8,128)(2,1)S(1)} %shard_map.94.refs_7_), channel_id=1, source_target_pairs={{0,24},{1,25},{2,26},{3,27},{4,28},{5,29},{6,30},{7,31},{8,16},{9,... | collective-permute-start | bytes 49160 | tf_op jit(solution)/shard_map/ppermute | solution.py:62
  29.5 1.8 %collective-permute-done.18 = bf16[32,256]{1,0:T(8,128)(2,1)S(1)} collective-permute-done((bf16[32,256]{1,0:T(8,128)(2,1)S(1)}, bf16[32,256]{1,0:T(8,128)(2,1)S(1)}, u32[]{:S(2)}, u32[]{:S(2)}) %collective-permute-start.18) | collective-permute-done | bytes 16416 | tf_op jit(solution)/shard_map/ppermute | solution.py:62
  31.5 1.2 %collective-permute-start.20 = (bf16[32,256]{1,0:T(8,128)(2,1)S(1)}, bf16[32,256]{1,0:T(8,128)(2,1)S(1)}, u32[]{:S(2)}, u32[]{:S(2)}) collective-permute-start(bf16[32,256]{1,0:T(8,128)(2,1)S(1)} %shard_map.95.refs_7_), channel_id=1, source_target_pairs={{0,8},{1,9},{2,10},{3,11},{4,12},{5,13},{6,14},{7,15},{8,16},{9,17... | collective-permute-start | bytes 49160 | tf_op jit(solution)/shard_map/ppermute | solution.py:62
  32.8 1.2 %collective-permute-start.22 = (bf16[32,256]{1,0:T(8,128)(2,1)S(1)}, bf16[32,256]{1,0:T(8,128)(2,1)S(1)}, u32[]{:S(2)}, u32[]{:S(2)}) collective-permute-start(bf16[32,256]{1,0:T(8,128)(2,1)S(1)} %shard_map.95.refs_7_), channel_id=1, source_target_pairs={{0,8},{1,9},{2,10},{3,11},{4,12},{5,13},{6,14},{7,15},{8,0},{9,1},... | collective-permute-start | bytes 49160 | tf_op jit(solution)/shard_map/ppermute | solution.py:62
  34.0 1.1 %collective-permute-start.23 = (bf16[32,256]{1,0:T(8,128)(2,1)S(1)}, bf16[32,256]{1,0:T(8,128)(2,1)S(1)}, u32[]{:S(2)}, u32[]{:S(2)}) collective-permute-start(bf16[32,256]{1,0:T(8,128)(2,1)S(1)} %shard_map.95.refs_7_), channel_id=1, source_target_pairs={{0,8},{1,9},{2,10},{3,11},{4,12},{5,13},{6,14},{7,15},{8,0},{9,1},... | collective-permute-start | bytes 49160 | tf_op jit(solution)/shard_map/ppermute | solution.py:62
  35.2 1.5 %collective-permute-start.24 = (bf16[32,256]{1,0:T(8,128)(2,1)S(1)}, bf16[32,256]{1,0:T(8,128)(2,1)S(1)}, u32[]{:S(2)}, u32[]{:S(2)}) collective-permute-start(bf16[32,256]{1,0:T(8,128)(2,1)S(1)} %shard_map.95.refs_7_), channel_id=1, source_target_pairs={{0,8},{1,9},{2,10},{3,11},{4,12},{5,13},{6,14},{7,15},{8,0},{9,1},... | collective-permute-start | bytes 49160 | tf_op jit(solution)/shard_map/ppermute | solution.py:62
  36.6 1.1 %collective-permute-done.20 = bf16[32,256]{1,0:T(8,128)(2,1)S(1)} collective-permute-done((bf16[32,256]{1,0:T(8,128)(2,1)S(1)}, bf16[32,256]{1,0:T(8,128)(2,1)S(1)}, u32[]{:S(2)}, u32[]{:S(2)}) %collective-permute-start.20) | collective-permute-done | bytes 16416 | tf_op jit(solution)/shard_map/ppermute | solution.py:62
  37.8 0.7 %collective-permute-start.26 = (bf16[32,256]{1,0:T(8,128)(2,1)S(1)}, bf16[32,256]{1,0:T(8,128)(2,1)S(1)}, u32[]{:S(2)}, u32[]{:S(2)}) collective-permute-start(bf16[32,256]{1,0:T(8,128)(2,1)S(1)} %shard_map.95.refs_7_), channel_id=1, source_target_pairs={{0,8},{1,9},{2,10},{3,11},{4,12},{5,13},{6,14},{7,15},{8,0},{9,1},... | collective-permute-start | bytes 49160 | tf_op jit(solution)/shard_map/ppermute | solution.py:62
  39.2 1.7 %collective-permute-done.25 = bf16[32,256]{1,0:T(8,128)(2,1)S(1)} collective-permute-done((bf16[32,256]{1,0:T(8,128)(2,1)S(1)}, bf16[32,256]{1,0:T(8,128)(2,1)S(1)}, u32[]{:S(2)}, u32[]{:S(2)}) %collective-permute-start.25) | collective-permute-done | bytes 16416 | tf_op jit(solution)/shard_map/ppermute | solution.py:62
  41.0 1.7 %shard_map.96 = bf16[8,4,256]{2,1,0:T(4,128)(2,1)S(1)} custom-call(f32[1,2048]{1,0:T(1,128)S(1)} %get-tuple-element.13.refs_0_, f32[1,2048]{1,0:T(1,128)S(1)} %get-tuple-element.14.refs_1_, f32[1,2048]{1,0:T(1,128)S(1)} %get-tuple-element.15.refs_2_, bf16[2048,768]{1,0:T(8,128)(2,1)S(1)} %get-tuple-element.16.refs_3_, ...), custom_call_target="tpu_custom_call" | custom-call | tf_op jit(solution)/shard_map/pallas_call | solution.py:228
  42.8 8.2 %all_to_all.5 = bf16[8,4,256]{2,1,0:T(4,128)(2,1)S(1)} all-to-all(bf16[8,4,256]{2,1,0:T(4,128)(2,1)S(1)} %shard_map.96), channel_id=1, replica_groups=mesh['pipe'=4,'head'=8] {'head'}, dimensions={0} | all-to-all | bytes 32768 | tf_op jit(solution)/shard_map/all_to_all | solution.py:285
  51.0 0.6 %copy.39 = bf16[1,4,1,2048]{3,1,2,0:T(4,128)(2,1)} copy(bf16[1,4,1,2048]{3,1,2,0:T(4,128)(2,1)S(1)} %bitcast.14) | data formatting | bytes 32768
  (70 shorter events, 3.5 us)
Async XLA Ops:
  0.0 5.8 %collective-permute-start = (bf16[1,4,2048]{2,1,0:T(4,128)(2,1)}, bf16[1,4,2048]{2,1,0:T(4,128)(2,1)S(1)}, u32[]{:S(2)}, u32[]{:S(2)}) collective-permute-start(bf16[1,4,2048]{2,1,0:T(4,128)(2,1)} %bitcast.15), channel_id=1, source_target_pairs={{0,8},{1,9},{2,10},{3,11},{4,12},{5,13},{6,14},{7,15},{8,16},{9,17... | collective-permute-start | bytes 49160 | tf_op jit(solution)/shard_map/ppermute | solution.py:62
  3.8 2.0 %collective-permute-start.1 = (bf16[1,4,2048]{2,1,0:T(4,128)(2,1)}, bf16[1,4,2048]{2,1,0:T(4,128)(2,1)S(1)}, u32[]{:S(2)}, u32[]{:S(2)}) collective-permute-start(bf16[1,4,2048]{2,1,0:T(4,128)(2,1)} %bitcast.16), channel_id=1, source_target_pairs={{0,8},{1,9},{2,10},{3,11},{4,12},{5,13},{6,14},{7,15},{8,16},{9,17... | collective-permute-start | bytes 49160 | tf_op jit(solution)/shard_map/ppermute | solution.py:62
  3.8 3.5 %collective-permute-start.2 = (bf16[1,4,2048]{2,1,0:T(4,128)(2,1)}, bf16[1,4,2048]{2,1,0:T(4,128)(2,1)S(1)}, u32[]{:S(2)}, u32[]{:S(2)}) collective-permute-start(bf16[1,4,2048]{2,1,0:T(4,128)(2,1)} %bitcast.17), channel_id=1, source_target_pairs={{0,24},{1,25},{2,26},{3,27},{4,28},{5,29},{6,30},{7,31},{8,16},{9,... | collective-permute-start | bytes 49160 | tf_op jit(solution)/shard_map/ppermute | solution.py:62
  7.3 3.2 %collective-permute-start.3 = (bf16[4,4,2048]{2,1,0:T(4,128)(2,1)S(1)}, bf16[4,4,2048]{2,1,0:T(4,128)(2,1)S(1)}, u32[]{:S(2)}, u32[]{:S(2)}) collective-permute-start(bf16[4,4,2048]{2,1,0:T(4,128)(2,1)S(1)} %get-tuple-element.22.after_ref), channel_id=1, source_target_pairs={{1,0},{0,1},{3,2},{2,3},{5,4},{4,5},{7,6},{6,7},{9,8},{8,9},{11,10... | collective-permute-start | bytes 196616 | tf_op jit(solution)/shard_map/ppermute | solution.py:62
  10.6 4.5 %collective-permute-start.4 = (bf16[32,256]{1,0:T(8,128)(2,1)S(1)}, bf16[32,256]{1,0:T(8,128)(2,1)S(1)}, u32[]{:S(2)}, u32[]{:S(2)}) collective-permute-start(bf16[32,256]{1,0:T(8,128)(2,1)S(1)} %shard_map.93.refs_7_), channel_id=1, source_target_pairs={{7,8},{6,9},{5,10},{4,11},{3,12},{2,13},{1,14},{0,15},{8,16},{9,17... | collective-permute-start | bytes 49160 | tf_op jit(solution)/shard_map/ppermute | solution.py:62
  14.1 1.3 %collective-permute-start.5 = (bf16[32,256]{1,0:T(8,128)(2,1)S(1)}, bf16[32,256]{1,0:T(8,128)(2,1)S(1)}, u32[]{:S(2)}, u32[]{:S(2)}) collective-permute-start(bf16[32,256]{1,0:T(8,128)(2,1)S(1)} %shard_map.93.refs_7_), channel_id=1, source_target_pairs={{6,8},{7,9},{4,10},{5,11},{2,12},{3,13},{0,14},{1,15},{8,16},{9,17... | collective-permute-start | bytes 49160 | tf_op jit(solution)/shard_map/ppermute | solution.py:62
  14.1 1.5 %collective-permute-start.6 = (bf16[32,256]{1,0:T(8,128)(2,1)S(1)}, bf16[32,256]{1,0:T(8,128)(2,1)S(1)}, u32[]{:S(2)}, u32[]{:S(2)}) collective-permute-start(bf16[32,256]{1,0:T(8,128)(2,1)S(1)} %shard_map.93.refs_7_), channel_id=1, source_target_pairs={{5,8},{4,9},{7,10},{6,11},{1,12},{0,13},{3,14},{2,15},{8,0},{9,1},... | collective-permute-start | bytes 49160 | tf_op jit(solution)/shard_map/ppermute | solution.py:62
  14.6 1.3 %collective-permute-start.7 = (bf16[32,256]{1,0:T(8,128)(2,1)S(1)}, bf16[32,256]{1,0:T(8,128)(2,1)S(1)}, u32[]{:S(2)}, u32[]{:S(2)}) collective-permute-start(bf16[32,256]{1,0:T(8,128)(2,1)S(1)} %shard_map.93.refs_7_), channel_id=1, source_target_pairs={{4,8},{5,9},{6,10},{7,11},{0,12},{1,13},{2,14},{3,15},{8,0},{9,1},... | collective-permute-start | bytes 49160 | tf_op jit(solution)/shard_map/ppermute | solution.py:62
  16.8 9.2 %collective-permute-start.12 = (bf16[32,256]{1,0:T(8,128)(2,1)S(1)}, bf16[32,256]{1,0:T(8,128)(2,1)S(1)}, u32[]{:S(2)}, u32[]{:S(2)}) collective-permute-start(bf16[32,256]{1,0:T(8,128)(2,1)S(1)} %shard_map.94.refs_7_), channel_id=1, source_target_pairs={{0,8},{1,9},{2,10},{3,11},{4,12},{5,13},{6,14},{7,15},{15,16},{14,... | collective-permute-start | bytes 49160 | tf_op jit(solution)/shard_map/ppermute | solution.py:62
  21.6 6.2 %collective-permute-start.13 = (bf16[32,256]{1,0:T(8,128)(2,1)S(1)}, bf16[32,256]{1,0:T(8,128)(2,1)S(1)}, u32[]{:S(2)}, u32[]{:S(2)}) collective-permute-start(bf16[32,256]{1,0:T(8,128)(2,1)S(1)} %shard_map.94.refs_7_), channel_id=1, source_target_pairs={{0,8},{1,9},{2,10},{3,11},{4,12},{5,13},{6,14},{7,15},{14,16},{15,... | collective-permute-start | bytes 49160 | tf_op jit(solution)/shard_map/ppermute | solution.py:62
  24.2 3.6 %collective-permute-start.14 = (bf16[32,256]{1,0:T(8,128)(2,1)S(1)}, bf16[32,256]{1,0:T(8,128)(2,1)S(1)}, u32[]{:S(2)}, u32[]{:S(2)}) collective-permute-start(bf16[32,256]{1,0:T(8,128)(2,1)S(1)} %shard_map.94.refs_7_), channel_id=1, source_target_pairs={{0,24},{1,25},{2,26},{3,27},{4,28},{5,29},{6,30},{7,31},{13,16},{1... | collective-permute-start | bytes 49160 | tf_op jit(solution)/shard_map/ppermute | solution.py:62
  24.3 5.2 %collective-permute-start.15 = (bf16[32,256]{1,0:T(8,128)(2,1)S(1)}, bf16[32,256]{1,0:T(8,128)(2,1)S(1)}, u32[]{:S(2)}, u32[]{:S(2)}) collective-permute-start(bf16[32,256]{1,0:T(8,128)(2,1)S(1)} %shard_map.94.refs_7_), channel_id=1, source_target_pairs={{0,24},{1,25},{2,26},{3,27},{4,28},{5,29},{6,30},{7,31},{12,16},{1... | collective-permute-start | bytes 49160 | tf_op jit(solution)/shard_map/ppermute | solution.py:62
  26.0 3.5 %collective-permute-start.16 = (bf16[32,256]{1,0:T(8,128)(2,1)S(1)}, bf16[32,256]{1,0:T(8,128)(2,1)S(1)}, u32[]{:S(2)}, u32[]{:S(2)}) collective-permute-start(bf16[32,256]{1,0:T(8,128)(2,1)S(1)} %shard_map.94.refs_7_), channel_id=1, source_target_pairs={{0,24},{1,25},{2,26},{3,27},{4,28},{5,29},{6,30},{7,31},{11,16},{1... | collective-permute-start | bytes 49160 | tf_op jit(solution)/shard_map/ppermute | solution.py:62
  26.0 3.5 %collective-permute-start.17 = (bf16[32,256]{1,0:T(8,128)(2,1)S(1)}, bf16[32,256]{1,0:T(8,128)(2,1)S(1)}, u32[]{:S(2)}, u32[]{:S(2)}) collective-permute-start(bf16[32,256]{1,0:T(8,128)(2,1)S(1)} %shard_map.94.refs_7_), channel_id=1, source_target_pairs={{0,24},{1,25},{2,26},{3,27},{4,28},{5,29},{6,30},{7,31},{10,16},{1... | collective-permute-start | bytes 49160 | tf_op jit(solution)/shard_map/ppermute | solution.py:62
  27.7 3.6 %collective-permute-start.18 = (bf16[32,256]{1,0:T(8,128)(2,1)S(1)}, bf16[32,256]{1,0:T(8,128)(2,1)S(1)}, u32[]{:S(2)}, u32[]{:S(2)}) collective-permute-start(bf16[32,256]{1,0:T(8,128)(2,1)S(1)} %shard_map.94.refs_7_), channel_id=1, source_target_pairs={{0,24},{1,25},{2,26},{3,27},{4,28},{5,29},{6,30},{7,31},{9,16},{8,... | collective-permute-start | bytes 49160 | tf_op jit(solution)/shard_map/ppermute | solution.py:62
  27.8 3.7 %collective-permute-start.19 = (bf16[32,256]{1,0:T(8,128)(2,1)S(1)}, bf16[32,256]{1,0:T(8,128)(2,1)S(1)}, u32[]{:S(2)}, u32[]{:S(2)}) collective-permute-start(bf16[32,256]{1,0:T(8,128)(2,1)S(1)} %shard_map.94.refs_7_), channel_id=1, source_target_pairs={{0,24},{1,25},{2,26},{3,27},{4,28},{5,29},{6,30},{7,31},{8,16},{9,... | collective-permute-start | bytes 49160 | tf_op jit(solution)/shard_map/ppermute | solution.py:62
  31.5 6.3 %collective-permute-start.20 = (bf16[32,256]{1,0:T(8,128)(2,1)S(1)}, bf16[32,256]{1,0:T(8,128)(2,1)S(1)}, u32[]{:S(2)}, u32[]{:S(2)}) collective-permute-start(bf16[32,256]{1,0:T(8,128)(2,1)S(1)} %shard_map.95.refs_7_), channel_id=1, source_target_pairs={{0,8},{1,9},{2,10},{3,11},{4,12},{5,13},{6,14},{7,15},{8,16},{9,17... | collective-permute-start | bytes 49160 | tf_op jit(solution)/shard_map/ppermute | solution.py:62
  32.7 5.1 %collective-permute-start.21 = (bf16[32,256]{1,0:T(8,128)(2,1)S(1)}, bf16[32,256]{1,0:T(8,128)(2,1)S(1)}, u32[]{:S(2)}, u32[]{:S(2)}) collective-permute-start(bf16[32,256]{1,0:T(8,128)(2,1)S(1)} %shard_map.95.refs_7_), channel_id=1, source_target_pairs={{0,8},{1,9},{2,10},{3,11},{4,12},{5,13},{6,14},{7,15},{8,16},{9,17... | collective-permute-start | bytes 49160 | tf_op jit(solution)/shard_map/ppermute | solution.py:62
  32.8 5.8 %collective-permute-start.22 = (bf16[32,256]{1,0:T(8,128)(2,1)S(1)}, bf16[32,256]{1,0:T(8,128)(2,1)S(1)}, u32[]{:S(2)}, u32[]{:S(2)}) collective-permute-start(bf16[32,256]{1,0:T(8,128)(2,1)S(1)} %shard_map.95.refs_7_), channel_id=1, source_target_pairs={{0,8},{1,9},{2,10},{3,11},{4,12},{5,13},{6,14},{7,15},{8,0},{9,1},... | collective-permute-start | bytes 49160 | tf_op jit(solution)/shard_map/ppermute | solution.py:62
  34.0 4.9 %collective-permute-start.23 = (bf16[32,256]{1,0:T(8,128)(2,1)S(1)}, bf16[32,256]{1,0:T(8,128)(2,1)S(1)}, u32[]{:S(2)}, u32[]{:S(2)}) collective-permute-start(bf16[32,256]{1,0:T(8,128)(2,1)S(1)} %shard_map.95.refs_7_), channel_id=1, source_target_pairs={{0,8},{1,9},{2,10},{3,11},{4,12},{5,13},{6,14},{7,15},{8,0},{9,1},... | collective-permute-start | bytes 49160 | tf_op jit(solution)/shard_map/ppermute | solution.py:62
  35.2 4.1 %collective-permute-start.24 = (bf16[32,256]{1,0:T(8,128)(2,1)S(1)}, bf16[32,256]{1,0:T(8,128)(2,1)S(1)}, u32[]{:S(2)}, u32[]{:S(2)}) collective-permute-start(bf16[32,256]{1,0:T(8,128)(2,1)S(1)} %shard_map.95.refs_7_), channel_id=1, source_target_pairs={{0,8},{1,9},{2,10},{3,11},{4,12},{5,13},{6,14},{7,15},{8,0},{9,1},... | collective-permute-start | bytes 49160 | tf_op jit(solution)/shard_map/ppermute | solution.py:62
  37.8 3.2 %collective-permute-start.25 = (bf16[32,256]{1,0:T(8,128)(2,1)S(1)}, bf16[32,256]{1,0:T(8,128)(2,1)S(1)}, u32[]{:S(2)}, u32[]{:S(2)}) collective-permute-start(bf16[32,256]{1,0:T(8,128)(2,1)S(1)} %shard_map.95.refs_7_), channel_id=1, source_target_pairs={{0,8},{1,9},{2,10},{3,11},{4,12},{5,13},{6,14},{7,15},{8,0},{9,1},... | collective-permute-start | bytes 49160 | tf_op jit(solution)/shard_map/ppermute | solution.py:62
  37.8 3.2 %collective-permute-start.26 = (bf16[32,256]{1,0:T(8,128)(2,1)S(1)}, bf16[32,256]{1,0:T(8,128)(2,1)S(1)}, u32[]{:S(2)}, u32[]{:S(2)}) collective-permute-start(bf16[32,256]{1,0:T(8,128)(2,1)S(1)} %shard_map.95.refs_7_), channel_id=1, source_target_pairs={{0,8},{1,9},{2,10},{3,11},{4,12},{5,13},{6,14},{7,15},{8,0},{9,1},... | collective-permute-start | bytes 49160 | tf_op jit(solution)/shard_map/ppermute | solution.py:62
  38.5 2.5 %collective-permute-start.27 = (bf16[32,256]{1,0:T(8,128)(2,1)S(1)}, bf16[32,256]{1,0:T(8,128)(2,1)S(1)}, u32[]{:S(2)}, u32[]{:S(2)}) collective-permute-start(bf16[32,256]{1,0:T(8,128)(2,1)S(1)} %shard_map.95.refs_7_), channel_id=1, source_target_pairs={{0,8},{1,9},{2,10},{3,11},{4,12},{5,13},{6,14},{7,15},{8,0},{9,1},... | collective-permute-start | bytes 49160 | tf_op jit(solution)/shard_map/ppermute | solution.py:62
  (4 other events, 4.8 us)

commit v4 on v3

--- a/solution.py
+++ b/solution.py
@@ -169,20 +169,17 @@
                 at = pl.multiple_of(traced(maps, head, n_head) * width, width)
                 pieces.append((at, in_ref[slot * rows : (slot + 1) * rows, :]))
             residual = pieces[0][1]
-        square = None
-        for _, piece in pieces:
+        square, projected = None, None
+        for at, piece in pieces:
             value = piece.astype(jnp.float32)
             square = value * value if square is None else square + value * value
-        meansq = jnp.sum(square, axis=-1, keepdims=True) / feat
-        inverse = lax.rsqrt(meansq + 1e-06)
-        projected = None
-        for at, piece in pieces:
-            scale = 1.0 + scale_ref[:, pl.ds(at, width)]
-            shift = shift_ref[:, pl.ds(at, width)]
-            modded = (piece.astype(jnp.float32) * inverse * scale + shift).astype(jnp.bfloat16)
-            term = jnp.dot(modded, weight_ref[pl.ds(at, width), :], preferred_element_type=jnp.float32)
+            scaled = (value * (1.0 + scale_ref[:, pl.ds(at, width)])).astype(jnp.bfloat16)
+            shift = shift_ref[:, pl.ds(at, width)].astype(jnp.bfloat16)
+            both = jnp.concatenate([scaled, jnp.broadcast_to(shift, (16, width))], axis=0)
+            term = jnp.dot(both, weight_ref[pl.ds(at, width), :], preferred_element_type=jnp.float32)
             projected = term if projected is None else projected + term
-        projected = projected.astype(jnp.bfloat16)
+        inverse = lax.rsqrt(jnp.sum(square, axis=-1, keepdims=True) / feat + 1e-06)
+        projected = (projected[:rows] * inverse + projected[rows : rows + 1]).astype(jnp.bfloat16)
         query, fresh_keys, fresh_vals = (projected[:, part * width : (part + 1) * width] for part in range(3))
         lane_head = lax.broadcasted_iota(jnp.int32, (rows, width), 1) // head_dim
         queries = jnp.concatenate(
@@ -238,7 +235,7 @@
 def plans(n_head):
     keep = ("keep", 0)
     far = tuple(("swap", k) for k in range(n_head - 2, 0, -2))
-    entry = ((1, (keep,) + far), (0, (keep, ("swap", 1))))
+    entry = ((-1, (keep,) + far), (0, (keep, ("swap", 1))))
     return entry, ((1, tuple(("swap", k) for k in range(n_head - 1, -1, -1))),)
 
 
@@ -264,7 +261,7 @@
         4 + 3 * heads_dev,
         6 * feat * 3 * width,
     )
-    value, offsets = exchange(mine, entry_plan[:1], n_pipe - 1, own)
+    value, offsets = exchange(mine, entry_plan[:1], 1, own)
     caches = loaded(
         functools.partial(cache_kernel, micro, patch),
         (patch_start, stale_keys[0], stale_values[0]),

time: 51.8 us -> 50.7 us (0.979)
  starting transfers between devices: 29.3 us -> 28.1 us
    ppermute x28, starting transfers between devices: 29.3 us -> 28.1 us  [routed(): return lax.ppermute(value, ('pipe', 'head'), pairs)]
  transfers between devices with their start and end apart: 28 -> 28, of which waited for: 11 -> 13; matrix products, arithmetic and copies ran while one was open for 0% -> 0% of each run, Pallas kernels for 7% -> 7%
where the time goes in v4:
time: 50.7 us; the launch traced here: 50.5 us
  starting transfers between devices  28.1 us (55%)
  blocking collectives  8.3 us (16%)
  waiting for transfers between devices  8.04 us (16%)
  Pallas kernels  5.1 us (10%)
  local copies, waits for them, and re-layouts  0.78 us (2%)
    ppermute x28, starting transfers between devices, routed(): return lax.ppermute(value, ('pipe', 'head'), pairs)  28.1 us
    all_to_all x1, blocking collectives, whole_heads(): back = lax.all_to_all(held, 'head', split_axis=0, concat_axis=0, tiled=True)  8.3 us
    ppermute x28, waiting for transfers between devices, routed(): return lax.ppermute(value, ('pipe', 'head'), pairs)  8.04 us
    pallas_call x2, Pallas kernels, loaded(): pl.pallas_call(kernel, out_shape=[pltpu.VMEM(shape, dtype) for shape, dty...  3.5 us
    pallas_call x4, Pallas kernels, run_layer(): pl.pallas_call(functools.partial(layer_kernel, step, slots, micro, head_d...  1.6 us
  transfers between devices with their start and end apart: 28, of which 13 were waited for; matrix products, arithmetic and copies ran while one was open for 0% of the time, Pallas kernels for 7%

profile of v4, /device:TPU:5, one launch (start us, length us, event | category | flops | bytes accessed | tf_op | source)
XLA Modules:
  0.0 50.5 jit_solution(3852381646339628360)
XLA Ops:
  0.0 0.7 %collective-permute-start = (bf16[1,4,2048]{2,1,0:T(4,128)(2,1)}, bf16[1,4,2048]{2,1,0:T(4,128)(2,1)S(1)}, u32[]{:S(2)}, u32[]{:S(2)}) collective-permute-start(bf16[1,4,2048]{2,1,0:T(4,128)(2,1)} %bitcast.15), channel_id=1, source_target_pairs={{0,24},{1,25},{2,26},{3,27},{4,28},{5,29},{6,30},{7,31},{14,0},{15... | collective-permute-start | bytes 49160 | tf_op jit(solution)/shard_map/ppermute | solution.py:62
  0.7 3.8 %collective-permute-start.2 = (bf16[1,4,2048]{2,1,0:T(4,128)(2,1)}, bf16[1,4,2048]{2,1,0:T(4,128)(2,1)S(1)}, u32[]{:S(2)}, u32[]{:S(2)}) collective-permute-start(bf16[1,4,2048]{2,1,0:T(4,128)(2,1)} %bitcast.17), channel_id=1, source_target_pairs={{0,8},{1,9},{2,10},{3,11},{4,12},{5,13},{6,14},{7,15},{10,0},{11,1... | collective-permute-start | bytes 49160 | tf_op jit(solution)/shard_map/ppermute | solution.py:62
  4.5 1.9 %shard_map.91 = (f32[1,2048]{1,0:T(1,128)S(1)}, f32[1,2048]{1,0:T(1,128)S(1)}, f32[1,2048]{1,0:T(1,128)S(1)}, bf16[2048,768]{1,0:T(8,128)(2,1)S(1)}, bf16[1,4,2048]{2,1,0:T(4,128)(2,1)S(1)}) custom-call(f32[1,2048]{1,0:T(1,128)} %scale_in.1, f32[1,2048]{1,0:T(1,128)} %shift_in.1, f32[1,2048]{1,0:T(1,128)} %gate_in.1, bf16[2,2048,128]{2,1,0:T(8,128)(2,1)} %bitcast.11, ...), custom_call_target="tpu_custom_call" | custom-call | bytes 9437184 | tf_op jit(solution)/shard_map/pallas_call | solution.py:133
  6.6 1.3 %collective-permute-start.3 = (bf16[4,4,2048]{2,1,0:T(4,128)(2,1)S(1)}, bf16[4,4,2048]{2,1,0:T(4,128)(2,1)S(1)}, u32[]{:S(2)}, u32[]{:S(2)}) collective-permute-start(bf16[4,4,2048]{2,1,0:T(4,128)(2,1)S(1)} %get-tuple-element.22.after_ref), channel_id=1, source_target_pairs={{1,0},{0,1},{3,2},{2,3},{5,4},{4,5},{7,6},{6,7},{9,8},{8,9},{11,10... | collective-permute-start | bytes 196616 | tf_op jit(solution)/shard_map/ppermute | solution.py:62
  7.9 1.6 %shard_map.92 = (bf16[2048,256]{1,0:T(8,128)(2,1)S(1)}, bf16[2048,256]{1,0:T(8,128)(2,1)S(1)}, s32[8,2048]{1,0:T(8,128)S(1)}) custom-call(s32[4]{0:T(128)} %start_in.1, bf16[2,2048,128]{2,1,0:T(8,128)(2,1)} %bitcast.12, bf16[2,2048,128]{2,1,0:T(8,128)(2,1)} %bitcast.13, bf16[4,4,2048]{2,1,0:T(4,128)(2,1)S(1)} %get-tuple-element.22.after_ref), custom_call_target="tpu_custom_call" | custom-call | bytes 6291456 | tf_op jit(solution)/shard_map/pallas_call | solution.py:133
  9.4 0.9 %collective-permute-done.3 = bf16[4,4,2048]{2,1,0:T(4,128)(2,1)S(1)} collective-permute-done((bf16[4,4,2048]{2,1,0:T(4,128)(2,1)S(1)}, bf16[4,4,2048]{2,1,0:T(4,128)(2,1)S(1)}, u32[]{:S(2)}, u32[]{:S(2)}) %collective-permute-start.3) | collective-permute-done | bytes 65568 | tf_op jit(solution)/shard_map/ppermute | solution.py:62
  10.4 3.2 %collective-permute-start.4 = (bf16[32,256]{1,0:T(8,128)(2,1)S(1)}, bf16[32,256]{1,0:T(8,128)(2,1)S(1)}, u32[]{:S(2)}, u32[]{:S(2)}) collective-permute-start(bf16[32,256]{1,0:T(8,128)(2,1)S(1)} %shard_map.93.refs_7_), channel_id=1, source_target_pairs={{7,8},{6,9},{5,10},{4,11},{3,12},{2,13},{1,14},{0,15},{8,16},{9,17... | collective-permute-start | bytes 49160 | tf_op jit(solution)/shard_map/ppermute | solution.py:62
  14.3 0.4 collective-permute-start.8
  16.4 4.2 %collective-permute-start.12 = (bf16[32,256]{1,0:T(8,128)(2,1)S(1)}, bf16[32,256]{1,0:T(8,128)(2,1)S(1)}, u32[]{:S(2)}, u32[]{:S(2)}) collective-permute-start(bf16[32,256]{1,0:T(8,128)(2,1)S(1)} %shard_map.94.refs_7_), channel_id=1, source_target_pairs={{0,8},{1,9},{2,10},{3,11},{4,12},{5,13},{6,14},{7,15},{15,16},{14,... | collective-permute-start | bytes 49160 | tf_op jit(solution)/shard_map/ppermute | solution.py:62
  20.6 2.7 %collective-permute-start.13 = (bf16[32,256]{1,0:T(8,128)(2,1)S(1)}, bf16[32,256]{1,0:T(8,128)(2,1)S(1)}, u32[]{:S(2)}, u32[]{:S(2)}) collective-permute-start(bf16[32,256]{1,0:T(8,128)(2,1)S(1)} %shard_map.94.refs_7_), channel_id=1, source_target_pairs={{0,8},{1,9},{2,10},{3,11},{4,12},{5,13},{6,14},{7,15},{14,16},{15,... | collective-permute-start | bytes 49160 | tf_op jit(solution)/shard_map/ppermute | solution.py:62
  23.4 1.7 %collective-permute-start.15 = (bf16[32,256]{1,0:T(8,128)(2,1)S(1)}, bf16[32,256]{1,0:T(8,128)(2,1)S(1)}, u32[]{:S(2)}, u32[]{:S(2)}) collective-permute-start(bf16[32,256]{1,0:T(8,128)(2,1)S(1)} %shard_map.94.refs_7_), channel_id=1, source_target_pairs={{0,24},{1,25},{2,26},{3,27},{4,28},{5,29},{6,30},{7,31},{12,16},{1... | collective-permute-start | bytes 49160 | tf_op jit(solution)/shard_map/ppermute | solution.py:62
  25.1 1.7 %collective-permute-start.17 = (bf16[32,256]{1,0:T(8,128)(2,1)S(1)}, bf16[32,256]{1,0:T(8,128)(2,1)S(1)}, u32[]{:S(2)}, u32[]{:S(2)}) collective-permute-start(bf16[32,256]{1,0:T(8,128)(2,1)S(1)} %shard_map.94.refs_7_), channel_id=1, source_target_pairs={{0,24},{1,25},{2,26},{3,27},{4,28},{5,29},{6,30},{7,31},{10,16},{1... | collective-permute-start | bytes 49160 | tf_op jit(solution)/shard_map/ppermute | solution.py:62
  26.9 1.7 %collective-permute-start.19 = (bf16[32,256]{1,0:T(8,128)(2,1)S(1)}, bf16[32,256]{1,0:T(8,128)(2,1)S(1)}, u32[]{:S(2)}, u32[]{:S(2)}) collective-permute-start(bf16[32,256]{1,0:T(8,128)(2,1)S(1)} %shard_map.94.refs_7_), channel_id=1, source_target_pairs={{0,24},{1,25},{2,26},{3,27},{4,28},{5,29},{6,30},{7,31},{8,16},{9,... | collective-permute-start | bytes 49160 | tf_op jit(solution)/shard_map/ppermute | solution.py:62
  28.6 1.7 %collective-permute-done.18 = bf16[32,256]{1,0:T(8,128)(2,1)S(1)} collective-permute-done((bf16[32,256]{1,0:T(8,128)(2,1)S(1)}, bf16[32,256]{1,0:T(8,128)(2,1)S(1)}, u32[]{:S(2)}, u32[]{:S(2)}) %collective-permute-start.18) | collective-permute-done | bytes 16416 | tf_op jit(solution)/shard_map/ppermute | solution.py:62
  30.8 1.0 %collective-permute-start.20 = (bf16[32,256]{1,0:T(8,128)(2,1)S(1)}, bf16[32,256]{1,0:T(8,128)(2,1)S(1)}, u32[]{:S(2)}, u32[]{:S(2)}) collective-permute-start(bf16[32,256]{1,0:T(8,128)(2,1)S(1)} %shard_map.95.refs_7_), channel_id=1, source_target_pairs={{0,8},{1,9},{2,10},{3,11},{4,12},{5,13},{6,14},{7,15},{8,16},{9,17... | collective-permute-start | bytes 49160 | tf_op jit(solution)/shard_map/ppermute | solution.py:62
  31.9 1.5 %collective-permute-start.22 = (bf16[32,256]{1,0:T(8,128)(2,1)S(1)}, bf16[32,256]{1,0:T(8,128)(2,1)S(1)}, u32[]{:S(2)}, u32[]{:S(2)}) collective-permute-start(bf16[32,256]{1,0:T(8,128)(2,1)S(1)} %shard_map.95.refs_7_), channel_id=1, source_target_pairs={{0,8},{1,9},{2,10},{3,11},{4,12},{5,13},{6,14},{7,15},{8,0},{9,1},... | collective-permute-start | bytes 49160 | tf_op jit(solution)/shard_map/ppermute | solution.py:62
  33.4 0.9 %collective-permute-start.23 = (bf16[32,256]{1,0:T(8,128)(2,1)S(1)}, bf16[32,256]{1,0:T(8,128)(2,1)S(1)}, u32[]{:S(2)}, u32[]{:S(2)}) collective-permute-start(bf16[32,256]{1,0:T(8,128)(2,1)S(1)} %shard_map.95.refs_7_), channel_id=1, source_target_pairs={{0,8},{1,9},{2,10},{3,11},{4,12},{5,13},{6,14},{7,15},{8,0},{9,1},... | collective-permute-start | bytes 49160 | tf_op jit(solution)/shard_map/ppermute | solution.py:62
  34.3 0.9 %collective-permute-start.24 = (bf16[32,256]{1,0:T(8,128)(2,1)S(1)}, bf16[32,256]{1,0:T(8,128)(2,1)S(1)}, u32[]{:S(2)}, u32[]{:S(2)}) collective-permute-start(bf16[32,256]{1,0:T(8,128)(2,1)S(1)} %shard_map.95.refs_7_), channel_id=1, source_target_pairs={{0,8},{1,9},{2,10},{3,11},{4,12},{5,13},{6,14},{7,15},{8,0},{9,1},... | collective-permute-start | bytes 49160 | tf_op jit(solution)/shard_map/ppermute | solution.py:62
  35.2 1.5 %collective-permute-done.20 = bf16[32,256]{1,0:T(8,128)(2,1)S(1)} collective-permute-done((bf16[32,256]{1,0:T(8,128)(2,1)S(1)}, bf16[32,256]{1,0:T(8,128)(2,1)S(1)}, u32[]{:S(2)}, u32[]{:S(2)}) %collective-permute-start.20) | collective-permute-done | bytes 16416 | tf_op jit(solution)/shard_map/ppermute | solution.py:62
  37.8 0.5 %collective-permute-done.24 = bf16[32,256]{1,0:T(8,128)(2,1)S(1)} collective-permute-done((bf16[32,256]{1,0:T(8,128)(2,1)S(1)}, bf16[32,256]{1,0:T(8,128)(2,1)S(1)}, u32[]{:S(2)}, u32[]{:S(2)}) %collective-permute-start.24) | collective-permute-done | bytes 16416 | tf_op jit(solution)/shard_map/ppermute | solution.py:62
  38.4 1.5 %collective-permute-done.25 = bf16[32,256]{1,0:T(8,128)(2,1)S(1)} collective-permute-done((bf16[32,256]{1,0:T(8,128)(2,1)S(1)}, bf16[32,256]{1,0:T(8,128)(2,1)S(1)}, u32[]{:S(2)}, u32[]{:S(2)}) %collective-permute-start.25) | collective-permute-done | bytes 16416 | tf_op jit(solution)/shard_map/ppermute | solution.py:62
  40.0 1.6 %shard_map.96 = bf16[8,4,256]{2,1,0:T(4,128)(2,1)S(1)} custom-call(f32[1,2048]{1,0:T(1,128)S(1)} %get-tuple-element.13.refs_0_, f32[1,2048]{1,0:T(1,128)S(1)} %get-tuple-element.14.refs_1_, f32[1,2048]{1,0:T(1,128)S(1)} %get-tuple-element.15.refs_2_, bf16[2048,768]{1,0:T(8,128)(2,1)S(1)} %get-tuple-element.16.refs_3_, ...), custom_call_target="tpu_custom_call" | custom-call | tf_op jit(solution)/shard_map/pallas_call | solution.py:225
  41.6 8.3 %all_to_all.5 = bf16[8,4,256]{2,1,0:T(4,128)(2,1)S(1)} all-to-all(bf16[8,4,256]{2,1,0:T(4,128)(2,1)S(1)} %shard_map.96), channel_id=1, replica_groups=mesh['pipe'=4,'head'=8] {'head'}, dimensions={0} | all-to-all | bytes 32768 | tf_op jit(solution)/shard_map/all_to_all | solution.py:282
  49.9 0.6 %copy.39 = bf16[1,4,1,2048]{3,1,2,0:T(4,128)(2,1)} copy(bf16[1,4,1,2048]{3,1,2,0:T(4,128)(2,1)S(1)} %bitcast.14) | data formatting | bytes 32768
  (70 shorter events, 4.4 us)
Async XLA Ops:
  0.0 6.5 %collective-permute-start = (bf16[1,4,2048]{2,1,0:T(4,128)(2,1)}, bf16[1,4,2048]{2,1,0:T(4,128)(2,1)S(1)}, u32[]{:S(2)}, u32[]{:S(2)}) collective-permute-start(bf16[1,4,2048]{2,1,0:T(4,128)(2,1)} %bitcast.15), channel_id=1, source_target_pairs={{0,24},{1,25},{2,26},{3,27},{4,28},{5,29},{6,30},{7,31},{14,0},{15... | collective-permute-start | bytes 49160 | tf_op jit(solution)/shard_map/ppermute | solution.py:62
  0.7 5.8 %collective-permute-start.1 = (bf16[1,4,2048]{2,1,0:T(4,128)(2,1)}, bf16[1,4,2048]{2,1,0:T(4,128)(2,1)S(1)}, u32[]{:S(2)}, u32[]{:S(2)}) collective-permute-start(bf16[1,4,2048]{2,1,0:T(4,128)(2,1)} %bitcast.16), channel_id=1, source_target_pairs={{0,24},{1,25},{2,26},{3,27},{4,28},{5,29},{6,30},{7,31},{12,0},{13... | collective-permute-start | bytes 49160 | tf_op jit(solution)/shard_map/ppermute | solution.py:62
  0.7 5.9 %collective-permute-start.2 = (bf16[1,4,2048]{2,1,0:T(4,128)(2,1)}, bf16[1,4,2048]{2,1,0:T(4,128)(2,1)S(1)}, u32[]{:S(2)}, u32[]{:S(2)}) collective-permute-start(bf16[1,4,2048]{2,1,0:T(4,128)(2,1)} %bitcast.17), channel_id=1, source_target_pairs={{0,8},{1,9},{2,10},{3,11},{4,12},{5,13},{6,14},{7,15},{10,0},{11,1... | collective-permute-start | bytes 49160 | tf_op jit(solution)/shard_map/ppermute | solution.py:62
  6.6 3.8 %collective-permute-start.3 = (bf16[4,4,2048]{2,1,0:T(4,128)(2,1)S(1)}, bf16[4,4,2048]{2,1,0:T(4,128)(2,1)S(1)}, u32[]{:S(2)}, u32[]{:S(2)}) collective-permute-start(bf16[4,4,2048]{2,1,0:T(4,128)(2,1)S(1)} %get-tuple-element.22.after_ref), channel_id=1, source_target_pairs={{1,0},{0,1},{3,2},{2,3},{5,4},{4,5},{7,6},{6,7},{9,8},{8,9},{11,10... | collective-permute-start | bytes 196616 | tf_op jit(solution)/shard_map/ppermute | solution.py:62
  10.4 4.3 %collective-permute-start.4 = (bf16[32,256]{1,0:T(8,128)(2,1)S(1)}, bf16[32,256]{1,0:T(8,128)(2,1)S(1)}, u32[]{:S(2)}, u32[]{:S(2)}) collective-permute-start(bf16[32,256]{1,0:T(8,128)(2,1)S(1)} %shard_map.93.refs_7_), channel_id=1, source_target_pairs={{7,8},{6,9},{5,10},{4,11},{3,12},{2,13},{1,14},{0,15},{8,16},{9,17... | collective-permute-start | bytes 49160 | tf_op jit(solution)/shard_map/ppermute | solution.py:62
  13.8 1.5 %collective-permute-start.6 = (bf16[32,256]{1,0:T(8,128)(2,1)S(1)}, bf16[32,256]{1,0:T(8,128)(2,1)S(1)}, u32[]{:S(2)}, u32[]{:S(2)}) collective-permute-start(bf16[32,256]{1,0:T(8,128)(2,1)S(1)} %shard_map.93.refs_7_), channel_id=1, source_target_pairs={{5,8},{4,9},{7,10},{6,11},{1,12},{0,13},{3,14},{2,15},{8,0},{9,1},... | collective-permute-start | bytes 49160 | tf_op jit(solution)/shard_map/ppermute | solution.py:62
  14.3 1.3 %collective-permute-start.8 = (bf16[32,256]{1,0:T(8,128)(2,1)S(1)}, bf16[32,256]{1,0:T(8,128)(2,1)S(1)}, u32[]{:S(2)}, u32[]{:S(2)}) collective-permute-start(bf16[32,256]{1,0:T(8,128)(2,1)S(1)} %shard_map.93.refs_7_), channel_id=1, source_target_pairs={{3,8},{2,9},{1,10},{0,11},{7,12},{6,13},{5,14},{4,15},{8,0},{9,1},... | collective-permute-start | bytes 49160 | tf_op jit(solution)/shard_map/ppermute | solution.py:62
  14.9 1.2 %collective-permute-start.10 = (bf16[32,256]{1,0:T(8,128)(2,1)S(1)}, bf16[32,256]{1,0:T(8,128)(2,1)S(1)}, u32[]{:S(2)}, u32[]{:S(2)}) collective-permute-start(bf16[32,256]{1,0:T(8,128)(2,1)S(1)} %shard_map.93.refs_7_), channel_id=1, source_target_pairs={{1,8},{0,9},{3,10},{2,11},{5,12},{4,13},{7,14},{6,15},{8,0},{9,1},... | collective-permute-start | bytes 49160 | tf_op jit(solution)/shard_map/ppermute | solution.py:62
  16.4 8.7 %collective-permute-start.12 = (bf16[32,256]{1,0:T(8,128)(2,1)S(1)}, bf16[32,256]{1,0:T(8,128)(2,1)S(1)}, u32[]{:S(2)}, u32[]{:S(2)}) collective-permute-start(bf16[32,256]{1,0:T(8,128)(2,1)S(1)} %shard_map.94.refs_7_), channel_id=1, source_target_pairs={{0,8},{1,9},{2,10},{3,11},{4,12},{5,13},{6,14},{7,15},{15,16},{14,... | collective-permute-start | bytes 49160 | tf_op jit(solution)/shard_map/ppermute | solution.py:62
  20.6 6.2 %collective-permute-start.13 = (bf16[32,256]{1,0:T(8,128)(2,1)S(1)}, bf16[32,256]{1,0:T(8,128)(2,1)S(1)}, u32[]{:S(2)}, u32[]{:S(2)}) collective-permute-start(bf16[32,256]{1,0:T(8,128)(2,1)S(1)} %shard_map.94.refs_7_), channel_id=1, source_target_pairs={{0,8},{1,9},{2,10},{3,11},{4,12},{5,13},{6,14},{7,15},{14,16},{15,... | collective-permute-start | bytes 49160 | tf_op jit(solution)/shard_map/ppermute | solution.py:62
  23.3 3.6 %collective-permute-start.14 = (bf16[32,256]{1,0:T(8,128)(2,1)S(1)}, bf16[32,256]{1,0:T(8,128)(2,1)S(1)}, u32[]{:S(2)}, u32[]{:S(2)}) collective-permute-start(bf16[32,256]{1,0:T(8,128)(2,1)S(1)} %shard_map.94.refs_7_), channel_id=1, source_target_pairs={{0,24},{1,25},{2,26},{3,27},{4,28},{5,29},{6,30},{7,31},{13,16},{1... | collective-permute-start | bytes 49160 | tf_op jit(solution)/shard_map/ppermute | solution.py:62
  23.4 5.2 %collective-permute-start.15 = (bf16[32,256]{1,0:T(8,128)(2,1)S(1)}, bf16[32,256]{1,0:T(8,128)(2,1)S(1)}, u32[]{:S(2)}, u32[]{:S(2)}) collective-permute-start(bf16[32,256]{1,0:T(8,128)(2,1)S(1)} %shard_map.94.refs_7_), channel_id=1, source_target_pairs={{0,24},{1,25},{2,26},{3,27},{4,28},{5,29},{6,30},{7,31},{12,16},{1... | collective-permute-start | bytes 49160 | tf_op jit(solution)/shard_map/ppermute | solution.py:62
  25.1 3.5 %collective-permute-start.16 = (bf16[32,256]{1,0:T(8,128)(2,1)S(1)}, bf16[32,256]{1,0:T(8,128)(2,1)S(1)}, u32[]{:S(2)}, u32[]{:S(2)}) collective-permute-start(bf16[32,256]{1,0:T(8,128)(2,1)S(1)} %shard_map.94.refs_7_), channel_id=1, source_target_pairs={{0,24},{1,25},{2,26},{3,27},{4,28},{5,29},{6,30},{7,31},{11,16},{1... | collective-permute-start | bytes 49160 | tf_op jit(solution)/shard_map/ppermute | solution.py:62
  25.1 3.5 %collective-permute-start.17 = (bf16[32,256]{1,0:T(8,128)(2,1)S(1)}, bf16[32,256]{1,0:T(8,128)(2,1)S(1)}, u32[]{:S(2)}, u32[]{:S(2)}) collective-permute-start(bf16[32,256]{1,0:T(8,128)(2,1)S(1)} %shard_map.94.refs_7_), channel_id=1, source_target_pairs={{0,24},{1,25},{2,26},{3,27},{4,28},{5,29},{6,30},{7,31},{10,16},{1... | collective-permute-start | bytes 49160 | tf_op jit(solution)/shard_map/ppermute | solution.py:62
  26.8 3.5 %collective-permute-start.18 = (bf16[32,256]{1,0:T(8,128)(2,1)S(1)}, bf16[32,256]{1,0:T(8,128)(2,1)S(1)}, u32[]{:S(2)}, u32[]{:S(2)}) collective-permute-start(bf16[32,256]{1,0:T(8,128)(2,1)S(1)} %shard_map.94.refs_7_), channel_id=1, source_target_pairs={{0,24},{1,25},{2,26},{3,27},{4,28},{5,29},{6,30},{7,31},{9,16},{8,... | collective-permute-start | bytes 49160 | tf_op jit(solution)/shard_map/ppermute | solution.py:62
  26.9 3.9 %collective-permute-start.19 = (bf16[32,256]{1,0:T(8,128)(2,1)S(1)}, bf16[32,256]{1,0:T(8,128)(2,1)S(1)}, u32[]{:S(2)}, u32[]{:S(2)}) collective-permute-start(bf16[32,256]{1,0:T(8,128)(2,1)S(1)} %shard_map.94.refs_7_), channel_id=1, source_target_pairs={{0,24},{1,25},{2,26},{3,27},{4,28},{5,29},{6,30},{7,31},{8,16},{9,... | collective-permute-start | bytes 49160 | tf_op jit(solution)/shard_map/ppermute | solution.py:62
  30.8 6.0 %collective-permute-start.20 = (bf16[32,256]{1,0:T(8,128)(2,1)S(1)}, bf16[32,256]{1,0:T(8,128)(2,1)S(1)}, u32[]{:S(2)}, u32[]{:S(2)}) collective-permute-start(bf16[32,256]{1,0:T(8,128)(2,1)S(1)} %shard_map.95.refs_7_), channel_id=1, source_target_pairs={{0,8},{1,9},{2,10},{3,11},{4,12},{5,13},{6,14},{7,15},{8,16},{9,17... | collective-permute-start | bytes 49160 | tf_op jit(solution)/shard_map/ppermute | solution.py:62
  31.8 5.0 %collective-permute-start.21 = (bf16[32,256]{1,0:T(8,128)(2,1)S(1)}, bf16[32,256]{1,0:T(8,128)(2,1)S(1)}, u32[]{:S(2)}, u32[]{:S(2)}) collective-permute-start(bf16[32,256]{1,0:T(8,128)(2,1)S(1)} %shard_map.95.refs_7_), channel_id=1, source_target_pairs={{0,8},{1,9},{2,10},{3,11},{4,12},{5,13},{6,14},{7,15},{8,16},{9,17... | collective-permute-start | bytes 49160 | tf_op jit(solution)/shard_map/ppermute | solution.py:62
  31.9 5.5 %collective-permute-start.22 = (bf16[32,256]{1,0:T(8,128)(2,1)S(1)}, bf16[32,256]{1,0:T(8,128)(2,1)S(1)}, u32[]{:S(2)}, u32[]{:S(2)}) collective-permute-start(bf16[32,256]{1,0:T(8,128)(2,1)S(1)} %shard_map.95.refs_7_), channel_id=1, source_target_pairs={{0,8},{1,9},{2,10},{3,11},{4,12},{5,13},{6,14},{7,15},{8,0},{9,1},... | collective-permute-start | bytes 49160 | tf_op jit(solution)/shard_map/ppermute | solution.py:62
  33.4 4.4 %collective-permute-start.23 = (bf16[32,256]{1,0:T(8,128)(2,1)S(1)}, bf16[32,256]{1,0:T(8,128)(2,1)S(1)}, u32[]{:S(2)}, u32[]{:S(2)}) collective-permute-start(bf16[32,256]{1,0:T(8,128)(2,1)S(1)} %shard_map.95.refs_7_), channel_id=1, source_target_pairs={{0,8},{1,9},{2,10},{3,11},{4,12},{5,13},{6,14},{7,15},{8,0},{9,1},... | collective-permute-start | bytes 49160 | tf_op jit(solution)/shard_map/ppermute | solution.py:62
  34.3 4.1 %collective-permute-start.24 = (bf16[32,256]{1,0:T(8,128)(2,1)S(1)}, bf16[32,256]{1,0:T(8,128)(2,1)S(1)}, u32[]{:S(2)}, u32[]{:S(2)}) collective-permute-start(bf16[32,256]{1,0:T(8,128)(2,1)S(1)} %shard_map.95.refs_7_), channel_id=1, source_target_pairs={{0,8},{1,9},{2,10},{3,11},{4,12},{5,13},{6,14},{7,15},{8,0},{9,1},... | collective-permute-start | bytes 49160 | tf_op jit(solution)/shard_map/ppermute | solution.py:62
  36.7 3.2 %collective-permute-start.25 = (bf16[32,256]{1,0:T(8,128)(2,1)S(1)}, bf16[32,256]{1,0:T(8,128)(2,1)S(1)}, u32[]{:S(2)}, u32[]{:S(2)}) collective-permute-start(bf16[32,256]{1,0:T(8,128)(2,1)S(1)} %shard_map.95.refs_7_), channel_id=1, source_target_pairs={{0,8},{1,9},{2,10},{3,11},{4,12},{5,13},{6,14},{7,15},{8,0},{9,1},... | collective-permute-start | bytes 49160 | tf_op jit(solution)/shard_map/ppermute | solution.py:62
  36.7 3.2 %collective-permute-start.26 = (bf16[32,256]{1,0:T(8,128)(2,1)S(1)}, bf16[32,256]{1,0:T(8,128)(2,1)S(1)}, u32[]{:S(2)}, u32[]{:S(2)}) collective-permute-start(bf16[32,256]{1,0:T(8,128)(2,1)S(1)} %shard_map.95.refs_7_), channel_id=1, source_target_pairs={{0,8},{1,9},{2,10},{3,11},{4,12},{5,13},{6,14},{7,15},{8,0},{9,1},... | collective-permute-start | bytes 49160 | tf_op jit(solution)/shard_map/ppermute | solution.py:62
  37.4 2.6 %collective-permute-start.27 = (bf16[32,256]{1,0:T(8,128)(2,1)S(1)}, bf16[32,256]{1,0:T(8,128)(2,1)S(1)}, u32[]{:S(2)}, u32[]{:S(2)}) collective-permute-start(bf16[32,256]{1,0:T(8,128)(2,1)S(1)} %shard_map.95.refs_7_), channel_id=1, source_target_pairs={{0,8},{1,9},{2,10},{3,11},{4,12},{5,13},{6,14},{7,15},{8,0},{9,1},... | collective-permute-start | bytes 49160 | tf_op jit(solution)/shard_map/ppermute | solution.py:62
  (4 other events, 4.7 us)

commit v5 on v4

--- a/solution.py
+++ b/solution.py
@@ -65,7 +65,7 @@
 def exchange(value, plan, stage, own=None, offsets=((),)):
     own = value if own is None else own
     for shift, moves in plan:
-        parts, known, turn = [], [], 0
+        parts, known, turn = [], [], 2 if shift < 0 else 0
         for kind, amount in moves:
             if kind == "keep":
                 parts.append(own)
@@ -234,8 +234,9 @@
 
 def plans(n_head):
     keep = ("keep", 0)
-    far = tuple(("swap", k) for k in range(n_head - 2, 0, -2))
-    entry = ((-1, (keep,) + far), (0, (keep, ("swap", 1))))
+    far = sorted(range(2, n_head, 2), key=lambda k: (k != n_head // 2, -k))
+    far = tuple(("swap", k) for k in far)
+    entry = ((0, (keep, ("swap", 1))), (-1, (keep,) + far))
     return entry, ((1, tuple(("swap", k) for k in range(n_head - 1, -1, -1))),)
 
 
@@ -271,11 +272,11 @@
         6 * positions * 2 * width,
         (value,),
     )
-    value, offsets = exchange(value, entry_plan[1:], 0, offsets=offsets)
+    value, offsets = exchange(value, entry_plan[1:], 1, offsets=offsets)
     constants = (*params, *caches)
     held = jnp.zeros((rows, width), jnp.bfloat16)
     for step in range(n_pipe):
-        out_shape = held.shape if step + 1 < n_pipe else (n_head, rows // n_head, width)
+        out_shape = held.shape
         held = run_layer(step, distinct(offsets, n_head), micro, head_dim, constants, held, value, out_shape)
         if step + 1 < n_pipe:
             value, offsets = exchange(held, step_plan, step)

time: 50.7 us -> 50.1 us (0.988)
  waiting for transfers between devices: 8.04 us -> 7.29 us
    ppermute x28, waiting for transfers between devices: 8.04 us -> 7.29 us  [routed(): return lax.ppermute(value, ('pipe', 'head'), pairs)]
where the time goes in v5:
time: 50.1 us; the launch traced here: 49.8 us
  starting transfers between devices  28.2 us (56%)
  blocking collectives  8.18 us (16%)
  waiting for transfers between devices  7.29 us (15%)
  Pallas kernels  5.09 us (10%)
  local copies, waits for them, and re-layouts  0.78 us (2%)
    ppermute x28, starting transfers between devices, routed(): return lax.ppermute(value, ('pipe', 'head'), pairs)  28.2 us
    all_to_all x1, blocking collectives, whole_heads(): back = lax.all_to_all(held, 'head', split_axis=0, concat_axis=0, tiled=True)  8.18 us
    ppermute x28, waiting for transfers between devices, routed(): return lax.ppermute(value, ('pipe', 'head'), pairs)  7.29 us
    pallas_call x2, Pallas kernels, loaded(): pl.pallas_call(kernel, out_shape=[pltpu.VMEM(shape, dtype) for shape, dty...  3.5 us
    pallas_call x4, Pallas kernels, run_layer(): pl.pallas_call(functools.partial(layer_kernel, step, slots, micro, head_d...  1.6 us
  transfers between devices with their start and end apart: 28, of which 13 were waited for; matrix products, arithmetic and copies ran while one was open for 0% of the time, Pallas kernels for 7%

profile of v5, /device:TPU:5, one launch (start us, length us, event | category | flops | bytes accessed | tf_op | source)
XLA Modules:
  0.0 49.8 jit_solution(1209765955134490155)
XLA Ops:
  0.0 1.2 %collective-permute-start = (bf16[1,4,2048]{2,1,0:T(4,128)(2,1)}, bf16[1,4,2048]{2,1,0:T(4,128)(2,1)S(1)}, u32[]{:S(2)}, u32[]{:S(2)}) collective-permute-start(bf16[1,4,2048]{2,1,0:T(4,128)(2,1)} %bitcast.15), channel_id=1, source_target_pairs={{1,0},{0,1},{3,2},{2,3},{5,4},{4,5},{7,6},{6,7},{9,8},{8,9},{11,10... | collective-permute-start | bytes 49160 | tf_op jit(solution)/shard_map/ppermute | solution.py:62
  1.2 1.9 %shard_map.91 = (f32[1,2048]{1,0:T(1,128)S(1)}, f32[1,2048]{1,0:T(1,128)S(1)}, f32[1,2048]{1,0:T(1,128)S(1)}, bf16[2048,768]{1,0:T(8,128)(2,1)S(1)}, bf16[1,4,2048]{2,1,0:T(4,128)(2,1)S(1)}) custom-call(f32[1,2048]{1,0:T(1,128)} %scale_in.1, f32[1,2048]{1,0:T(1,128)} %shift_in.1, f32[1,2048]{1,0:T(1,128)} %gate_in.1, bf16[2,2048,128]{2,1,0:T(8,128)(2,1)} %bitcast.11, ...), custom_call_target="tpu_custom_call" | custom-call | bytes 9437184 | tf_op jit(solution)/shard_map/pallas_call | solution.py:133
  3.2 1.5 %collective-permute-start.1 = (bf16[2,4,2048]{2,1,0:T(4,128)(2,1)S(1)}, bf16[2,4,2048]{2,1,0:T(4,128)(2,1)S(1)}, u32[]{:S(2)}, u32[]{:S(2)}) collective-permute-start(bf16[2,4,2048]{2,1,0:T(4,128)(2,1)S(1)} %get-tuple-element.22.after_ref), channel_id=1, source_target_pairs={{0,8},{1,9},{2,10},{3,11},{4,12},{5,13},{6,14},{7,15},{12,0},{13,1... | collective-permute-start | bytes 98312 | tf_op jit(solution)/shard_map/ppermute | solution.py:62
  4.8 0.4 collective-permute-start.3
  5.2 1.6 %shard_map.92 = (bf16[2048,256]{1,0:T(8,128)(2,1)S(1)}, bf16[2048,256]{1,0:T(8,128)(2,1)S(1)}, s32[8,2048]{1,0:T(8,128)S(1)}) custom-call(s32[4]{0:T(128)} %start_in.1, bf16[2,2048,128]{2,1,0:T(8,128)(2,1)} %bitcast.12, bf16[2,2048,128]{2,1,0:T(8,128)(2,1)} %bitcast.13, bf16[2,4,2048]{2,1,0:T(4,128)(2,1)S(1)} %get-tuple-element.22.after_ref), custom_call_target="tpu_custom_call" | custom-call | bytes 6291456 | tf_op jit(solution)/shard_map/pallas_call | solution.py:133
  6.9 5.6 %collective-permute-start.4 = (bf16[32,256]{1,0:T(8,128)(2,1)S(1)}, bf16[32,256]{1,0:T(8,128)(2,1)S(1)}, u32[]{:S(2)}, u32[]{:S(2)}) collective-permute-start(bf16[32,256]{1,0:T(8,128)(2,1)S(1)} %shard_map.93.refs_7_), channel_id=1, source_target_pairs={{7,8},{6,9},{5,10},{4,11},{3,12},{2,13},{1,14},{0,15},{8,16},{9,17... | collective-permute-start | bytes 49160 | tf_op jit(solution)/shard_map/ppermute | solution.py:62
  12.6 0.4 collective-permute-start.6
  13.1 0.4 collective-permute-start.8
  15.3 4.4 %collective-permute-start.12 = (bf16[32,256]{1,0:T(8,128)(2,1)S(1)}, bf16[32,256]{1,0:T(8,128)(2,1)S(1)}, u32[]{:S(2)}, u32[]{:S(2)}) collective-permute-start(bf16[32,256]{1,0:T(8,128)(2,1)S(1)} %shard_map.94.refs_7_), channel_id=1, source_target_pairs={{0,8},{1,9},{2,10},{3,11},{4,12},{5,13},{6,14},{7,15},{15,16},{14,... | collective-permute-start | bytes 49160 | tf_op jit(solution)/shard_map/ppermute | solution.py:62
  19.7 3.0 %collective-permute-start.13 = (bf16[32,256]{1,0:T(8,128)(2,1)S(1)}, bf16[32,256]{1,0:T(8,128)(2,1)S(1)}, u32[]{:S(2)}, u32[]{:S(2)}) collective-permute-start(bf16[32,256]{1,0:T(8,128)(2,1)S(1)} %shard_map.94.refs_7_), channel_id=1, source_target_pairs={{0,8},{1,9},{2,10},{3,11},{4,12},{5,13},{6,14},{7,15},{14,16},{15,... | collective-permute-start | bytes 49160 | tf_op jit(solution)/shard_map/ppermute | solution.py:62
  22.7 1.7 %collective-permute-start.15 = (bf16[32,256]{1,0:T(8,128)(2,1)S(1)}, bf16[32,256]{1,0:T(8,128)(2,1)S(1)}, u32[]{:S(2)}, u32[]{:S(2)}) collective-permute-start(bf16[32,256]{1,0:T(8,128)(2,1)S(1)} %shard_map.94.refs_7_), channel_id=1, source_target_pairs={{0,24},{1,25},{2,26},{3,27},{4,28},{5,29},{6,30},{7,31},{12,16},{1... | collective-permute-start | bytes 49160 | tf_op jit(solution)/shard_map/ppermute | solution.py:62
  24.5 1.7 %collective-permute-start.17 = (bf16[32,256]{1,0:T(8,128)(2,1)S(1)}, bf16[32,256]{1,0:T(8,128)(2,1)S(1)}, u32[]{:S(2)}, u32[]{:S(2)}) collective-permute-start(bf16[32,256]{1,0:T(8,128)(2,1)S(1)} %shard_map.94.refs_7_), channel_id=1, source_target_pairs={{0,24},{1,25},{2,26},{3,27},{4,28},{5,29},{6,30},{7,31},{10,16},{1... | collective-permute-start | bytes 49160 | tf_op jit(solution)/shard_map/ppermute | solution.py:62
  26.2 1.7 %collective-permute-start.19 = (bf16[32,256]{1,0:T(8,128)(2,1)S(1)}, bf16[32,256]{1,0:T(8,128)(2,1)S(1)}, u32[]{:S(2)}, u32[]{:S(2)}) collective-permute-start(bf16[32,256]{1,0:T(8,128)(2,1)S(1)} %shard_map.94.refs_7_), channel_id=1, source_target_pairs={{0,24},{1,25},{2,26},{3,27},{4,28},{5,29},{6,30},{7,31},{8,16},{9,... | collective-permute-start | bytes 49160 | tf_op jit(solution)/shard_map/ppermute | solution.py:62
  28.0 2.0 %collective-permute-done.18 = bf16[32,256]{1,0:T(8,128)(2,1)S(1)} collective-permute-done((bf16[32,256]{1,0:T(8,128)(2,1)S(1)}, bf16[32,256]{1,0:T(8,128)(2,1)S(1)}, u32[]{:S(2)}, u32[]{:S(2)}) %collective-permute-start.18) | collective-permute-done | bytes 16416 | tf_op jit(solution)/shard_map/ppermute | solution.py:62
  30.0 1.2 %collective-permute-start.20 = (bf16[32,256]{1,0:T(8,128)(2,1)S(1)}, bf16[32,256]{1,0:T(8,128)(2,1)S(1)}, u32[]{:S(2)}, u32[]{:S(2)}) collective-permute-start(bf16[32,256]{1,0:T(8,128)(2,1)S(1)} %shard_map.95.refs_7_), channel_id=1, source_target_pairs={{0,8},{1,9},{2,10},{3,11},{4,12},{5,13},{6,14},{7,15},{8,16},{9,17... | collective-permute-start | bytes 49160 | tf_op jit(solution)/shard_map/ppermute | solution.py:62
  31.3 1.0 %collective-permute-start.22 = (bf16[32,256]{1,0:T(8,128)(2,1)S(1)}, bf16[32,256]{1,0:T(8,128)(2,1)S(1)}, u32[]{:S(2)}, u32[]{:S(2)}) collective-permute-start(bf16[32,256]{1,0:T(8,128)(2,1)S(1)} %shard_map.95.refs_7_), channel_id=1, source_target_pairs={{0,8},{1,9},{2,10},{3,11},{4,12},{5,13},{6,14},{7,15},{8,0},{9,1},... | collective-permute-start | bytes 49160 | tf_op jit(solution)/shard_map/ppermute | solution.py:62
  32.4 1.3 %collective-permute-start.23 = (bf16[32,256]{1,0:T(8,128)(2,1)S(1)}, bf16[32,256]{1,0:T(8,128)(2,1)S(1)}, u32[]{:S(2)}, u32[]{:S(2)}) collective-permute-start(bf16[32,256]{1,0:T(8,128)(2,1)S(1)} %shard_map.95.refs_7_), channel_id=1, source_target_pairs={{0,8},{1,9},{2,10},{3,11},{4,12},{5,13},{6,14},{7,15},{8,0},{9,1},... | collective-permute-start | bytes 49160 | tf_op jit(solution)/shard_map/ppermute | solution.py:62
  33.6 0.9 %collective-permute-start.24 = (bf16[32,256]{1,0:T(8,128)(2,1)S(1)}, bf16[32,256]{1,0:T(8,128)(2,1)S(1)}, u32[]{:S(2)}, u32[]{:S(2)}) collective-permute-start(bf16[32,256]{1,0:T(8,128)(2,1)S(1)} %shard_map.95.refs_7_), channel_id=1, source_target_pairs={{0,8},{1,9},{2,10},{3,11},{4,12},{5,13},{6,14},{7,15},{8,0},{9,1},... | collective-permute-start | bytes 49160 | tf_op jit(solution)/shard_map/ppermute | solution.py:62
  34.5 1.5 %collective-permute-done.20 = bf16[32,256]{1,0:T(8,128)(2,1)S(1)} collective-permute-done((bf16[32,256]{1,0:T(8,128)(2,1)S(1)}, bf16[32,256]{1,0:T(8,128)(2,1)S(1)}, u32[]{:S(2)}, u32[]{:S(2)}) %collective-permute-start.20) | collective-permute-done | bytes 16416 | tf_op jit(solution)/shard_map/ppermute | solution.py:62
  37.1 0.6 %collective-permute-done.24 = bf16[32,256]{1,0:T(8,128)(2,1)S(1)} collective-permute-done((bf16[32,256]{1,0:T(8,128)(2,1)S(1)}, bf16[32,256]{1,0:T(8,128)(2,1)S(1)}, u32[]{:S(2)}, u32[]{:S(2)}) %collective-permute-start.24) | collective-permute-done | bytes 16416 | tf_op jit(solution)/shard_map/ppermute | solution.py:62
  37.7 1.5 %collective-permute-done.25 = bf16[32,256]{1,0:T(8,128)(2,1)S(1)} collective-permute-done((bf16[32,256]{1,0:T(8,128)(2,1)S(1)}, bf16[32,256]{1,0:T(8,128)(2,1)S(1)}, u32[]{:S(2)}, u32[]{:S(2)}) %collective-permute-start.25) | collective-permute-done | bytes 16416 | tf_op jit(solution)/shard_map/ppermute | solution.py:62
  39.4 1.6 %shard_map.96 = bf16[32,256]{1,0:T(8,128)(2,1)S(1)} custom-call(f32[1,2048]{1,0:T(1,128)S(1)} %get-tuple-element.13.refs_0_, f32[1,2048]{1,0:T(1,128)S(1)} %get-tuple-element.14.refs_1_, f32[1,2048]{1,0:T(1,128)S(1)} %get-tuple-element.15.refs_2_, bf16[2048,768]{1,0:T(8,128)(2,1)S(1)} %get-tuple-element.16.refs_3_, ...), custom_call_target="tpu_custom_call" | custom-call | tf_op jit(solution)/shard_map/pallas_call | solution.py:225
  41.0 8.2 %all_to_all.9 = bf16[8,4,256]{2,1,0:T(4,128)(2,1)S(1)} all-to-all(bf16[8,4,256]{2,1,0:T(4,128)(2,1)S(1)} %all_to_all.6), channel_id=1, replica_groups=mesh['pipe'=4,'head'=8] {'head'}, dimensions={0} | all-to-all | bytes 32768 | tf_op jit(solution)/shard_map/all_to_all | solution.py:283
  49.2 0.6 %copy.38 = bf16[1,4,1,2048]{3,1,2,0:T(4,128)(2,1)} copy(bf16[1,4,1,2048]{3,1,2,0:T(4,128)(2,1)S(1)} %bitcast.14) | data formatting | bytes 32768
  (71 shorter events, 3.8 us)
Async XLA Ops:
  0.0 3.2 %collective-permute-start = (bf16[1,4,2048]{2,1,0:T(4,128)(2,1)}, bf16[1,4,2048]{2,1,0:T(4,128)(2,1)S(1)}, u32[]{:S(2)}, u32[]{:S(2)}) collective-permute-start(bf16[1,4,2048]{2,1,0:T(4,128)(2,1)} %bitcast.15), channel_id=1, source_target_pairs={{1,0},{0,1},{3,2},{2,3},{5,4},{4,5},{7,6},{6,7},{9,8},{8,9},{11,10... | collective-permute-start | bytes 49160 | tf_op jit(solution)/shard_map/ppermute | solution.py:62
  3.2 3.6 %collective-permute-start.1 = (bf16[2,4,2048]{2,1,0:T(4,128)(2,1)S(1)}, bf16[2,4,2048]{2,1,0:T(4,128)(2,1)S(1)}, u32[]{:S(2)}, u32[]{:S(2)}) collective-permute-start(bf16[2,4,2048]{2,1,0:T(4,128)(2,1)S(1)} %get-tuple-element.22.after_ref), channel_id=1, source_target_pairs={{0,8},{1,9},{2,10},{3,11},{4,12},{5,13},{6,14},{7,15},{12,0},{13,1... | collective-permute-start | bytes 98312 | tf_op jit(solution)/shard_map/ppermute | solution.py:62
  4.7 2.1 %collective-permute-start.2 = (bf16[2,4,2048]{2,1,0:T(4,128)(2,1)S(1)}, bf16[2,4,2048]{2,1,0:T(4,128)(2,1)S(1)}, u32[]{:S(2)}, u32[]{:S(2)}) collective-permute-start(bf16[2,4,2048]{2,1,0:T(4,128)(2,1)S(1)} %get-tuple-element.22.after_ref), channel_id=1, source_target_pairs={{0,8},{1,9},{2,10},{3,11},{4,12},{5,13},{6,14},{7,15},{14,0},{15,1... | collective-permute-start | bytes 98312 | tf_op jit(solution)/shard_map/ppermute | solution.py:62
  4.8 2.1 %collective-permute-start.3 = (bf16[2,4,2048]{2,1,0:T(4,128)(2,1)S(1)}, bf16[2,4,2048]{2,1,0:T(4,128)(2,1)S(1)}, u32[]{:S(2)}, u32[]{:S(2)}) collective-permute-start(bf16[2,4,2048]{2,1,0:T(4,128)(2,1)S(1)} %get-tuple-element.22.after_ref), channel_id=1, source_target_pairs={{0,8},{1,9},{2,10},{3,11},{4,12},{5,13},{6,14},{7,15},{10,0},{11,1... | collective-permute-start | bytes 98312 | tf_op jit(solution)/shard_map/ppermute | solution.py:62
  6.9 6.6 %collective-permute-start.4 = (bf16[32,256]{1,0:T(8,128)(2,1)S(1)}, bf16[32,256]{1,0:T(8,128)(2,1)S(1)}, u32[]{:S(2)}, u32[]{:S(2)}) collective-permute-start(bf16[32,256]{1,0:T(8,128)(2,1)S(1)} %shard_map.93.refs_7_), channel_id=1, source_target_pairs={{7,8},{6,9},{5,10},{4,11},{3,12},{2,13},{1,14},{0,15},{8,16},{9,17... | collective-permute-start | bytes 49160 | tf_op jit(solution)/shard_map/ppermute | solution.py:62
  12.6 1.5 %collective-permute-start.6 = (bf16[32,256]{1,0:T(8,128)(2,1)S(1)}, bf16[32,256]{1,0:T(8,128)(2,1)S(1)}, u32[]{:S(2)}, u32[]{:S(2)}) collective-permute-start(bf16[32,256]{1,0:T(8,128)(2,1)S(1)} %shard_map.93.refs_7_), channel_id=1, source_target_pairs={{5,8},{4,9},{7,10},{6,11},{1,12},{0,13},{3,14},{2,15},{8,0},{9,1},... | collective-permute-start | bytes 49160 | tf_op jit(solution)/shard_map/ppermute | solution.py:62
  13.1 1.3 %collective-permute-start.8 = (bf16[32,256]{1,0:T(8,128)(2,1)S(1)}, bf16[32,256]{1,0:T(8,128)(2,1)S(1)}, u32[]{:S(2)}, u32[]{:S(2)}) collective-permute-start(bf16[32,256]{1,0:T(8,128)(2,1)S(1)} %shard_map.93.refs_7_), channel_id=1, source_target_pairs={{3,8},{2,9},{1,10},{0,11},{7,12},{6,13},{5,14},{4,15},{8,0},{9,1},... | collective-permute-start | bytes 49160 | tf_op jit(solution)/shard_map/ppermute | solution.py:62
  13.7 1.2 %collective-permute-start.10 = (bf16[32,256]{1,0:T(8,128)(2,1)S(1)}, bf16[32,256]{1,0:T(8,128)(2,1)S(1)}, u32[]{:S(2)}, u32[]{:S(2)}) collective-permute-start(bf16[32,256]{1,0:T(8,128)(2,1)S(1)} %shard_map.93.refs_7_), channel_id=1, source_target_pairs={{1,8},{0,9},{3,10},{2,11},{5,12},{4,13},{7,14},{6,15},{8,0},{9,1},... | collective-permute-start | bytes 49160 | tf_op jit(solution)/shard_map/ppermute | solution.py:62
  15.3 9.2 %collective-permute-start.12 = (bf16[32,256]{1,0:T(8,128)(2,1)S(1)}, bf16[32,256]{1,0:T(8,128)(2,1)S(1)}, u32[]{:S(2)}, u32[]{:S(2)}) collective-permute-start(bf16[32,256]{1,0:T(8,128)(2,1)S(1)} %shard_map.94.refs_7_), channel_id=1, source_target_pairs={{0,8},{1,9},{2,10},{3,11},{4,12},{5,13},{6,14},{7,15},{15,16},{14,... | collective-permute-start | bytes 49160 | tf_op jit(solution)/shard_map/ppermute | solution.py:62
  19.7 6.5 %collective-permute-start.13 = (bf16[32,256]{1,0:T(8,128)(2,1)S(1)}, bf16[32,256]{1,0:T(8,128)(2,1)S(1)}, u32[]{:S(2)}, u32[]{:S(2)}) collective-permute-start(bf16[32,256]{1,0:T(8,128)(2,1)S(1)} %shard_map.94.refs_7_), channel_id=1, source_target_pairs={{0,8},{1,9},{2,10},{3,11},{4,12},{5,13},{6,14},{7,15},{14,16},{15,... | collective-permute-start | bytes 49160 | tf_op jit(solution)/shard_map/ppermute | solution.py:62
  22.7 3.6 %collective-permute-start.14 = (bf16[32,256]{1,0:T(8,128)(2,1)S(1)}, bf16[32,256]{1,0:T(8,128)(2,1)S(1)}, u32[]{:S(2)}, u32[]{:S(2)}) collective-permute-start(bf16[32,256]{1,0:T(8,128)(2,1)S(1)} %shard_map.94.refs_7_), channel_id=1, source_target_pairs={{0,24},{1,25},{2,26},{3,27},{4,28},{5,29},{6,30},{7,31},{13,16},{1... | collective-permute-start | bytes 49160 | tf_op jit(solution)/shard_map/ppermute | solution.py:62
  22.7 5.2 %collective-permute-start.15 = (bf16[32,256]{1,0:T(8,128)(2,1)S(1)}, bf16[32,256]{1,0:T(8,128)(2,1)S(1)}, u32[]{:S(2)}, u32[]{:S(2)}) collective-permute-start(bf16[32,256]{1,0:T(8,128)(2,1)S(1)} %shard_map.94.refs_7_), channel_id=1, source_target_pairs={{0,24},{1,25},{2,26},{3,27},{4,28},{5,29},{6,30},{7,31},{12,16},{1... | collective-permute-start | bytes 49160 | tf_op jit(solution)/shard_map/ppermute | solution.py:62
  24.4 3.5 %collective-permute-start.16 = (bf16[32,256]{1,0:T(8,128)(2,1)S(1)}, bf16[32,256]{1,0:T(8,128)(2,1)S(1)}, u32[]{:S(2)}, u32[]{:S(2)}) collective-permute-start(bf16[32,256]{1,0:T(8,128)(2,1)S(1)} %shard_map.94.refs_7_), channel_id=1, source_target_pairs={{0,24},{1,25},{2,26},{3,27},{4,28},{5,29},{6,30},{7,31},{11,16},{1... | collective-permute-start | bytes 49160 | tf_op jit(solution)/shard_map/ppermute | solution.py:62
  24.5 3.5 %collective-permute-start.17 = (bf16[32,256]{1,0:T(8,128)(2,1)S(1)}, bf16[32,256]{1,0:T(8,128)(2,1)S(1)}, u32[]{:S(2)}, u32[]{:S(2)}) collective-permute-start(bf16[32,256]{1,0:T(8,128)(2,1)S(1)} %shard_map.94.refs_7_), channel_id=1, source_target_pairs={{0,24},{1,25},{2,26},{3,27},{4,28},{5,29},{6,30},{7,31},{10,16},{1... | collective-permute-start | bytes 49160 | tf_op jit(solution)/shard_map/ppermute | solution.py:62
  26.2 3.8 %collective-permute-start.18 = (bf16[32,256]{1,0:T(8,128)(2,1)S(1)}, bf16[32,256]{1,0:T(8,128)(2,1)S(1)}, u32[]{:S(2)}, u32[]{:S(2)}) collective-permute-start(bf16[32,256]{1,0:T(8,128)(2,1)S(1)} %shard_map.94.refs_7_), channel_id=1, source_target_pairs={{0,24},{1,25},{2,26},{3,27},{4,28},{5,29},{6,30},{7,31},{9,16},{8,... | collective-permute-start | bytes 49160 | tf_op jit(solution)/shard_map/ppermute | solution.py:62
  26.2 3.8 %collective-permute-start.19 = (bf16[32,256]{1,0:T(8,128)(2,1)S(1)}, bf16[32,256]{1,0:T(8,128)(2,1)S(1)}, u32[]{:S(2)}, u32[]{:S(2)}) collective-permute-start(bf16[32,256]{1,0:T(8,128)(2,1)S(1)} %shard_map.94.refs_7_), channel_id=1, source_target_pairs={{0,24},{1,25},{2,26},{3,27},{4,28},{5,29},{6,30},{7,31},{8,16},{9,... | collective-permute-start | bytes 49160 | tf_op jit(solution)/shard_map/ppermute | solution.py:62
  30.0 6.0 %collective-permute-start.20 = (bf16[32,256]{1,0:T(8,128)(2,1)S(1)}, bf16[32,256]{1,0:T(8,128)(2,1)S(1)}, u32[]{:S(2)}, u32[]{:S(2)}) collective-permute-start(bf16[32,256]{1,0:T(8,128)(2,1)S(1)} %shard_map.95.refs_7_), channel_id=1, source_target_pairs={{0,8},{1,9},{2,10},{3,11},{4,12},{5,13},{6,14},{7,15},{8,16},{9,17... | collective-permute-start | bytes 49160 | tf_op jit(solution)/shard_map/ppermute | solution.py:62
  31.2 5.0 %collective-permute-start.21 = (bf16[32,256]{1,0:T(8,128)(2,1)S(1)}, bf16[32,256]{1,0:T(8,128)(2,1)S(1)}, u32[]{:S(2)}, u32[]{:S(2)}) collective-permute-start(bf16[32,256]{1,0:T(8,128)(2,1)S(1)} %shard_map.95.refs_7_), channel_id=1, source_target_pairs={{0,8},{1,9},{2,10},{3,11},{4,12},{5,13},{6,14},{7,15},{8,16},{9,17... | collective-permute-start | bytes 49160 | tf_op jit(solution)/shard_map/ppermute | solution.py:62
  31.3 5.4 %collective-permute-start.22 = (bf16[32,256]{1,0:T(8,128)(2,1)S(1)}, bf16[32,256]{1,0:T(8,128)(2,1)S(1)}, u32[]{:S(2)}, u32[]{:S(2)}) collective-permute-start(bf16[32,256]{1,0:T(8,128)(2,1)S(1)} %shard_map.95.refs_7_), channel_id=1, source_target_pairs={{0,8},{1,9},{2,10},{3,11},{4,12},{5,13},{6,14},{7,15},{8,0},{9,1},... | collective-permute-start | bytes 49160 | tf_op jit(solution)/shard_map/ppermute | solution.py:62
  32.4 4.8 %collective-permute-start.23 = (bf16[32,256]{1,0:T(8,128)(2,1)S(1)}, bf16[32,256]{1,0:T(8,128)(2,1)S(1)}, u32[]{:S(2)}, u32[]{:S(2)}) collective-permute-start(bf16[32,256]{1,0:T(8,128)(2,1)S(1)} %shard_map.95.refs_7_), channel_id=1, source_target_pairs={{0,8},{1,9},{2,10},{3,11},{4,12},{5,13},{6,14},{7,15},{8,0},{9,1},... | collective-permute-start | bytes 49160 | tf_op jit(solution)/shard_map/ppermute | solution.py:62
  33.6 4.1 %collective-permute-start.24 = (bf16[32,256]{1,0:T(8,128)(2,1)S(1)}, bf16[32,256]{1,0:T(8,128)(2,1)S(1)}, u32[]{:S(2)}, u32[]{:S(2)}) collective-permute-start(bf16[32,256]{1,0:T(8,128)(2,1)S(1)} %shard_map.95.refs_7_), channel_id=1, source_target_pairs={{0,8},{1,9},{2,10},{3,11},{4,12},{5,13},{6,14},{7,15},{8,0},{9,1},... | collective-permute-start | bytes 49160 | tf_op jit(solution)/shard_map/ppermute | solution.py:62
  36.0 3.2 %collective-permute-start.25 = (bf16[32,256]{1,0:T(8,128)(2,1)S(1)}, bf16[32,256]{1,0:T(8,128)(2,1)S(1)}, u32[]{:S(2)}, u32[]{:S(2)}) collective-permute-start(bf16[32,256]{1,0:T(8,128)(2,1)S(1)} %shard_map.95.refs_7_), channel_id=1, source_target_pairs={{0,8},{1,9},{2,10},{3,11},{4,12},{5,13},{6,14},{7,15},{8,0},{9,1},... | collective-permute-start | bytes 49160 | tf_op jit(solution)/shard_map/ppermute | solution.py:62
  36.2 3.2 %collective-permute-start.26 = (bf16[32,256]{1,0:T(8,128)(2,1)S(1)}, bf16[32,256]{1,0:T(8,128)(2,1)S(1)}, u32[]{:S(2)}, u32[]{:S(2)}) collective-permute-start(bf16[32,256]{1,0:T(8,128)(2,1)S(1)} %shard_map.95.refs_7_), channel_id=1, source_target_pairs={{0,8},{1,9},{2,10},{3,11},{4,12},{5,13},{6,14},{7,15},{8,0},{9,1},... | collective-permute-start | bytes 49160 | tf_op jit(solution)/shard_map/ppermute | solution.py:62
  36.7 2.7 %collective-permute-start.27 = (bf16[32,256]{1,0:T(8,128)(2,1)S(1)}, bf16[32,256]{1,0:T(8,128)(2,1)S(1)}, u32[]{:S(2)}, u32[]{:S(2)}) collective-permute-start(bf16[32,256]{1,0:T(8,128)(2,1)S(1)} %shard_map.95.refs_7_), channel_id=1, source_target_pairs={{0,8},{1,9},{2,10},{3,11},{4,12},{5,13},{6,14},{7,15},{8,0},{9,1},... | collective-permute-start | bytes 49160 | tf_op jit(solution)/shard_map/ppermute | solution.py:62
  (4 other events, 4.8 us)

commit v6 on v5

--- a/solution.py
+++ b/solution.py
@@ -46,7 +46,7 @@
     n_pipe, n_head = lax.axis_size("pipe"), lax.axis_size("head")
     target = (stage + shift) % n_pipe
     onto = {p: (p + shift) % n_pipe for p in range(n_pipe)}
-    if shift and turn > 1 and n_pipe % 2 == 0:
+    if shift and turn > (2 if stage == 1 and shift == 1 else 1) and n_pipe % 2 == 0:
         rest = [p for p in range(n_pipe) if p not in (stage, target)]
         onto = {stage: target, target: stage}
         for first, second in zip(rest[::2], rest[1::2]):
@@ -150,6 +150,7 @@
     rows, width = held_ref.shape
     heads_dev = width // head_dim
     by_token = len(in_ref.shape) == 3
+    scaled_ref, order_ref = refs[10:]
     own = pl.multiple_of(head * width, width)
 
     @pl.when(stage != step)
@@ -169,15 +170,14 @@
                 at = pl.multiple_of(traced(maps, head, n_head) * width, width)
                 pieces.append((at, in_ref[slot * rows : (slot + 1) * rows, :]))
             residual = pieces[0][1]
-        square, projected = None, None
+        square = None
         for at, piece in pieces:
             value = piece.astype(jnp.float32)
             square = value * value if square is None else square + value * value
-            scaled = (value * (1.0 + scale_ref[:, pl.ds(at, width)])).astype(jnp.bfloat16)
-            shift = shift_ref[:, pl.ds(at, width)].astype(jnp.bfloat16)
-            both = jnp.concatenate([scaled, jnp.broadcast_to(shift, (16, width))], axis=0)
-            term = jnp.dot(both, weight_ref[pl.ds(at, width), :], preferred_element_type=jnp.float32)
-            projected = term if projected is None else projected + term
+            scaled = value * (1.0 + scale_ref[:, pl.ds(at, width)])
+            scaled_ref[:rows, pl.ds(at, width)] = scaled.astype(jnp.bfloat16)
+        scaled_ref[rows:, :] = jnp.broadcast_to(shift_ref[...].astype(jnp.bfloat16), (16, feat))
+        projected = jnp.dot(scaled_ref[...], weight_ref[...], preferred_element_type=jnp.float32)
         inverse = lax.rsqrt(jnp.sum(square, axis=-1, keepdims=True) / feat + 1e-06)
         projected = (projected[:rows] * inverse + projected[rows : rows + 1]).astype(jnp.bfloat16)
         query, fresh_keys, fresh_vals = (projected[:, part * width : (part + 1) * width] for part in range(3))
@@ -211,7 +211,6 @@
         gate = gate_ref[:, pl.ds(own, width)]
         result = residual.astype(jnp.float32) + gate * jnp.concatenate(attended, axis=1)
         if by_token:
-            order_ref = refs[10]
             part = rows // n_head
             for slot, maps in slots:
                 order_ref[traced(maps, head, n_head)] = result[slot * part : (slot + 1) * part, :]
@@ -227,7 +226,10 @@
         out_shape=jax.ShapeDtypeStruct(out_shape, held.dtype),
         in_specs=[VMEM] * (len(constants) + 2),
         out_specs=VMEM,
-        scratch_shapes=[pltpu.VMEM((n_head, rows // n_head, width), jnp.float32)],
+        scratch_shapes=[
+            pltpu.VMEM((rows + 16, n_head * width), jnp.bfloat16),
+            pltpu.VMEM((n_head, rows // n_head, width), jnp.float32),
+        ],
         compiler_params=pltpu.CompilerParams(vmem_limit_bytes=LIMIT),
     )(*(pltpu.with_memory_space_constraint(array, pltpu.VMEM) for array in constants), held, blocks)
 

time: 50.1 us -> 49.9 us (level)
  starting transfers between devices: 28.2 us -> 27.6 us
    ppermute x28, starting transfers between devices: 28.2 us -> 27.6 us  [routed(): return lax.ppermute(value, ('pipe', 'head'), pairs)]
  transfers between devices with their start and end apart: 28 -> 28, of which waited for: 13 -> 12; matrix products, arithmetic and copies ran while one was open for 0% -> 0% of each run, Pallas kernels for 7% -> 7%
where the time goes in v6:
time: 49.9 us; the launch traced here: 49.6 us
  starting transfers between devices  27.6 us (55%)
  blocking collectives  8.2 us (16%)
  waiting for transfers between devices  7.75 us (16%)
  Pallas kernels  5.09 us (10%)
  local copies, waits for them, and re-layouts  0.78 us (2%)
    ppermute x28, starting transfers between devices, routed(): return lax.ppermute(value, ('pipe', 'head'), pairs)  27.6 us
    all_to_all x1, blocking collectives, whole_heads(): back = lax.all_to_all(held, 'head', split_axis=0, concat_axis=0, tiled=True)  8.2 us
    ppermute x28, waiting for transfers between devices, routed(): return lax.ppermute(value, ('pipe', 'head'), pairs)  7.75 us
    pallas_call x2, Pallas kernels, loaded(): pl.pallas_call(kernel, out_shape=[pltpu.VMEM(shape, dtype) for shape, dty...  3.5 us
    pallas_call x4, Pallas kernels, run_layer(): pl.pallas_call(functools.partial(layer_kernel, step, slots, micro, head_d...  1.6 us
  transfers between devices with their start and end apart: 28, of which 12 were waited for; matrix products, arithmetic and copies ran while one was open for 0% of the time, Pallas kernels for 7%

profile of v6, /device:TPU:5, one launch (start us, length us, event | category | flops | bytes accessed | tf_op | source)
XLA Modules:
  0.0 49.6 jit_solution(14099284728133224593)
XLA Ops:
  0.0 1.2 %collective-permute-start = (bf16[1,4,2048]{2,1,0:T(4,128)(2,1)}, bf16[1,4,2048]{2,1,0:T(4,128)(2,1)S(1)}, u32[]{:S(2)}, u32[]{:S(2)}) collective-permute-start(bf16[1,4,2048]{2,1,0:T(4,128)(2,1)} %bitcast.15), channel_id=1, source_target_pairs={{1,0},{0,1},{3,2},{2,3},{5,4},{4,5},{7,6},{6,7},{9,8},{8,9},{11,10... | collective-permute-start | bytes 49160 | tf_op jit(solution)/shard_map/ppermute | solution.py:62
  1.2 1.9 %shard_map.91 = (f32[1,2048]{1,0:T(1,128)S(1)}, f32[1,2048]{1,0:T(1,128)S(1)}, f32[1,2048]{1,0:T(1,128)S(1)}, bf16[2048,768]{1,0:T(8,128)(2,1)S(1)}, bf16[1,4,2048]{2,1,0:T(4,128)(2,1)S(1)}) custom-call(f32[1,2048]{1,0:T(1,128)} %scale_in.1, f32[1,2048]{1,0:T(1,128)} %shift_in.1, f32[1,2048]{1,0:T(1,128)} %gate_in.1, bf16[2,2048,128]{2,1,0:T(8,128)(2,1)} %bitcast.11, ...), custom_call_target="tpu_custom_call" | custom-call | bytes 9437184 | tf_op jit(solution)/shard_map/pallas_call | solution.py:133
  3.2 1.5 %collective-permute-start.1 = (bf16[2,4,2048]{2,1,0:T(4,128)(2,1)S(1)}, bf16[2,4,2048]{2,1,0:T(4,128)(2,1)S(1)}, u32[]{:S(2)}, u32[]{:S(2)}) collective-permute-start(bf16[2,4,2048]{2,1,0:T(4,128)(2,1)S(1)} %get-tuple-element.22.after_ref), channel_id=1, source_target_pairs={{0,8},{1,9},{2,10},{3,11},{4,12},{5,13},{6,14},{7,15},{12,0},{13,1... | collective-permute-start | bytes 98312 | tf_op jit(solution)/shard_map/ppermute | solution.py:62
  4.8 0.4 collective-permute-start.3
  5.2 1.6 %shard_map.92 = (bf16[2048,256]{1,0:T(8,128)(2,1)S(1)}, bf16[2048,256]{1,0:T(8,128)(2,1)S(1)}, s32[8,2048]{1,0:T(8,128)S(1)}) custom-call(s32[4]{0:T(128)} %start_in.1, bf16[2,2048,128]{2,1,0:T(8,128)(2,1)} %bitcast.12, bf16[2,2048,128]{2,1,0:T(8,128)(2,1)} %bitcast.13, bf16[2,4,2048]{2,1,0:T(4,128)(2,1)S(1)} %get-tuple-element.22.after_ref), custom_call_target="tpu_custom_call" | custom-call | bytes 6291456 | tf_op jit(solution)/shard_map/pallas_call | solution.py:133
  6.9 5.6 %collective-permute-start.4 = (bf16[32,256]{1,0:T(8,128)(2,1)S(1)}, bf16[32,256]{1,0:T(8,128)(2,1)S(1)}, u32[]{:S(2)}, u32[]{:S(2)}) collective-permute-start(bf16[32,256]{1,0:T(8,128)(2,1)S(1)} %shard_map.93.refs_7_), channel_id=1, source_target_pairs={{7,8},{6,9},{5,10},{4,11},{3,12},{2,13},{1,14},{0,15},{8,16},{9,17... | collective-permute-start | bytes 49160 | tf_op jit(solution)/shard_map/ppermute | solution.py:62
  12.6 0.4 collective-permute-start.6
  15.2 4.4 %collective-permute-start.12 = (bf16[32,256]{1,0:T(8,128)(2,1)S(1)}, bf16[32,256]{1,0:T(8,128)(2,1)S(1)}, u32[]{:S(2)}, u32[]{:S(2)}) collective-permute-start(bf16[32,256]{1,0:T(8,128)(2,1)S(1)} %shard_map.94.refs_7_), channel_id=1, source_target_pairs={{0,8},{1,9},{2,10},{3,11},{4,12},{5,13},{6,14},{7,15},{15,16},{14,... | collective-permute-start | bytes 49160 | tf_op jit(solution)/shard_map/ppermute | solution.py:62
  19.6 3.0 %collective-permute-start.13 = (bf16[32,256]{1,0:T(8,128)(2,1)S(1)}, bf16[32,256]{1,0:T(8,128)(2,1)S(1)}, u32[]{:S(2)}, u32[]{:S(2)}) collective-permute-start(bf16[32,256]{1,0:T(8,128)(2,1)S(1)} %shard_map.94.refs_7_), channel_id=1, source_target_pairs={{0,8},{1,9},{2,10},{3,11},{4,12},{5,13},{6,14},{7,15},{14,16},{15,... | collective-permute-start | bytes 49160 | tf_op jit(solution)/shard_map/ppermute | solution.py:62
  22.8 1.7 %collective-permute-start.16 = (bf16[32,256]{1,0:T(8,128)(2,1)S(1)}, bf16[32,256]{1,0:T(8,128)(2,1)S(1)}, u32[]{:S(2)}, u32[]{:S(2)}) collective-permute-start(bf16[32,256]{1,0:T(8,128)(2,1)S(1)} %shard_map.94.refs_7_), channel_id=1, source_target_pairs={{0,24},{1,25},{2,26},{3,27},{4,28},{5,29},{6,30},{7,31},{11,16},{1... | collective-permute-start | bytes 49160 | tf_op jit(solution)/shard_map/ppermute | solution.py:62
  24.5 1.7 %collective-permute-start.18 = (bf16[32,256]{1,0:T(8,128)(2,1)S(1)}, bf16[32,256]{1,0:T(8,128)(2,1)S(1)}, u32[]{:S(2)}, u32[]{:S(2)}) collective-permute-start(bf16[32,256]{1,0:T(8,128)(2,1)S(1)} %shard_map.94.refs_7_), channel_id=1, source_target_pairs={{0,24},{1,25},{2,26},{3,27},{4,28},{5,29},{6,30},{7,31},{9,16},{8,... | collective-permute-start | bytes 49160 | tf_op jit(solution)/shard_map/ppermute | solution.py:62
  26.3 1.5 %collective-permute-done.17 = bf16[32,256]{1,0:T(8,128)(2,1)S(1)} collective-permute-done((bf16[32,256]{1,0:T(8,128)(2,1)S(1)}, bf16[32,256]{1,0:T(8,128)(2,1)S(1)}, u32[]{:S(2)}, u32[]{:S(2)}) %collective-permute-start.17) | collective-permute-done | bytes 16416 | tf_op jit(solution)/shard_map/ppermute | solution.py:62
  28.0 1.7 %collective-permute-done.19 = bf16[32,256]{1,0:T(8,128)(2,1)S(1)} collective-permute-done((bf16[32,256]{1,0:T(8,128)(2,1)S(1)}, bf16[32,256]{1,0:T(8,128)(2,1)S(1)}, u32[]{:S(2)}, u32[]{:S(2)}) %collective-permute-start.19) | collective-permute-done | bytes 16416 | tf_op jit(solution)/shard_map/ppermute | solution.py:62
  29.7 1.2 %collective-permute-start.21 = (bf16[32,256]{1,0:T(8,128)(2,1)S(1)}, bf16[32,256]{1,0:T(8,128)(2,1)S(1)}, u32[]{:S(2)}, u32[]{:S(2)}) collective-permute-start(bf16[32,256]{1,0:T(8,128)(2,1)S(1)} %shard_map.95.refs_7_), channel_id=1, source_target_pairs={{0,8},{1,9},{2,10},{3,11},{4,12},{5,13},{6,14},{7,15},{8,16},{9,17... | collective-permute-start | bytes 49160 | tf_op jit(solution)/shard_map/ppermute | solution.py:62
  30.9 1.3 %collective-permute-start.22 = (bf16[32,256]{1,0:T(8,128)(2,1)S(1)}, bf16[32,256]{1,0:T(8,128)(2,1)S(1)}, u32[]{:S(2)}, u32[]{:S(2)}) collective-permute-start(bf16[32,256]{1,0:T(8,128)(2,1)S(1)} %shard_map.95.refs_7_), channel_id=1, source_target_pairs={{0,8},{1,9},{2,10},{3,11},{4,12},{5,13},{6,14},{7,15},{8,0},{9,1},... | collective-permute-start | bytes 49160 | tf_op jit(solution)/shard_map/ppermute | solution.py:62
  32.2 1.4 %collective-permute-start.23 = (bf16[32,256]{1,0:T(8,128)(2,1)S(1)}, bf16[32,256]{1,0:T(8,128)(2,1)S(1)}, u32[]{:S(2)}, u32[]{:S(2)}) collective-permute-start(bf16[32,256]{1,0:T(8,128)(2,1)S(1)} %shard_map.95.refs_7_), channel_id=1, source_target_pairs={{0,8},{1,9},{2,10},{3,11},{4,12},{5,13},{6,14},{7,15},{8,0},{9,1},... | collective-permute-start | bytes 49160 | tf_op jit(solution)/shard_map/ppermute | solution.py:62
  33.6 0.8 %collective-permute-start.24 = (bf16[32,256]{1,0:T(8,128)(2,1)S(1)}, bf16[32,256]{1,0:T(8,128)(2,1)S(1)}, u32[]{:S(2)}, u32[]{:S(2)}) collective-permute-start(bf16[32,256]{1,0:T(8,128)(2,1)S(1)} %shard_map.95.refs_7_), channel_id=1, source_target_pairs={{0,8},{1,9},{2,10},{3,11},{4,12},{5,13},{6,14},{7,15},{8,0},{9,1},... | collective-permute-start | bytes 49160 | tf_op jit(solution)/shard_map/ppermute | solution.py:62
  34.4 1.5 %collective-permute-done.20 = bf16[32,256]{1,0:T(8,128)(2,1)S(1)} collective-permute-done((bf16[32,256]{1,0:T(8,128)(2,1)S(1)}, bf16[32,256]{1,0:T(8,128)(2,1)S(1)}, u32[]{:S(2)}, u32[]{:S(2)}) %collective-permute-start.20) | collective-permute-done | bytes 16416 | tf_op jit(solution)/shard_map/ppermute | solution.py:62
  36.0 0.9 %collective-permute-start.26 = (bf16[32,256]{1,0:T(8,128)(2,1)S(1)}, bf16[32,256]{1,0:T(8,128)(2,1)S(1)}, u32[]{:S(2)}, u32[]{:S(2)}) collective-permute-start(bf16[32,256]{1,0:T(8,128)(2,1)S(1)} %shard_map.95.refs_7_), channel_id=1, source_target_pairs={{0,8},{1,9},{2,10},{3,11},{4,12},{5,13},{6,14},{7,15},{8,0},{9,1},... | collective-permute-start | bytes 49160 | tf_op jit(solution)/shard_map/ppermute | solution.py:62
  36.8 0.5 %collective-permute-start.27 = (bf16[32,256]{1,0:T(8,128)(2,1)S(1)}, bf16[32,256]{1,0:T(8,128)(2,1)S(1)}, u32[]{:S(2)}, u32[]{:S(2)}) collective-permute-start(bf16[32,256]{1,0:T(8,128)(2,1)S(1)} %shard_map.95.refs_7_), channel_id=1, source_target_pairs={{0,8},{1,9},{2,10},{3,11},{4,12},{5,13},{6,14},{7,15},{8,0},{9,1},... | collective-permute-start | bytes 49160 | tf_op jit(solution)/shard_map/ppermute | solution.py:62
  37.7 1.5 %collective-permute-done.25 = bf16[32,256]{1,0:T(8,128)(2,1)S(1)} collective-permute-done((bf16[32,256]{1,0:T(8,128)(2,1)S(1)}, bf16[32,256]{1,0:T(8,128)(2,1)S(1)}, u32[]{:S(2)}, u32[]{:S(2)}) %collective-permute-start.25) | collective-permute-done | bytes 16416 | tf_op jit(solution)/shard_map/ppermute | solution.py:62
  39.2 1.6 %shard_map.96 = bf16[32,256]{1,0:T(8,128)(2,1)S(1)} custom-call(f32[1,2048]{1,0:T(1,128)S(1)} %get-tuple-element.13.refs_0_, f32[1,2048]{1,0:T(1,128)S(1)} %get-tuple-element.14.refs_1_, f32[1,2048]{1,0:T(1,128)S(1)} %get-tuple-element.15.refs_2_, bf16[2048,768]{1,0:T(8,128)(2,1)S(1)} %get-tuple-element.16.refs_3_, ...), custom_call_target="tpu_custom_call" | custom-call | tf_op jit(solution)/shard_map/pallas_call | solution.py:224
  40.8 8.2 %all_to_all.9 = bf16[8,4,256]{2,1,0:T(4,128)(2,1)S(1)} all-to-all(bf16[8,4,256]{2,1,0:T(4,128)(2,1)S(1)} %all_to_all.6), channel_id=1, replica_groups=mesh['pipe'=4,'head'=8] {'head'}, dimensions={0} | all-to-all | bytes 32768 | tf_op jit(solution)/shard_map/all_to_all | solution.py:285
  49.0 0.6 %copy.38 = bf16[1,4,1,2048]{3,1,2,0:T(4,128)(2,1)} copy(bf16[1,4,1,2048]{3,1,2,0:T(4,128)(2,1)S(1)} %bitcast.14) | data formatting | bytes 32768
  (71 shorter events, 3.3 us)
Async XLA Ops:
  0.0 3.2 %collective-permute-start = (bf16[1,4,2048]{2,1,0:T(4,128)(2,1)}, bf16[1,4,2048]{2,1,0:T(4,128)(2,1)S(1)}, u32[]{:S(2)}, u32[]{:S(2)}) collective-permute-start(bf16[1,4,2048]{2,1,0:T(4,128)(2,1)} %bitcast.15), channel_id=1, source_target_pairs={{1,0},{0,1},{3,2},{2,3},{5,4},{4,5},{7,6},{6,7},{9,8},{8,9},{11,10... | collective-permute-start | bytes 49160 | tf_op jit(solution)/shard_map/ppermute | solution.py:62
  3.2 3.6 %collective-permute-start.1 = (bf16[2,4,2048]{2,1,0:T(4,128)(2,1)S(1)}, bf16[2,4,2048]{2,1,0:T(4,128)(2,1)S(1)}, u32[]{:S(2)}, u32[]{:S(2)}) collective-permute-start(bf16[2,4,2048]{2,1,0:T(4,128)(2,1)S(1)} %get-tuple-element.22.after_ref), channel_id=1, source_target_pairs={{0,8},{1,9},{2,10},{3,11},{4,12},{5,13},{6,14},{7,15},{12,0},{13,1... | collective-permute-start | bytes 98312 | tf_op jit(solution)/shard_map/ppermute | solution.py:62
  4.7 2.1 %collective-permute-start.2 = (bf16[2,4,2048]{2,1,0:T(4,128)(2,1)S(1)}, bf16[2,4,2048]{2,1,0:T(4,128)(2,1)S(1)}, u32[]{:S(2)}, u32[]{:S(2)}) collective-permute-start(bf16[2,4,2048]{2,1,0:T(4,128)(2,1)S(1)} %get-tuple-element.22.after_ref), channel_id=1, source_target_pairs={{0,8},{1,9},{2,10},{3,11},{4,12},{5,13},{6,14},{7,15},{14,0},{15,1... | collective-permute-start | bytes 98312 | tf_op jit(solution)/shard_map/ppermute | solution.py:62
  4.8 2.1 %collective-permute-start.3 = (bf16[2,4,2048]{2,1,0:T(4,128)(2,1)S(1)}, bf16[2,4,2048]{2,1,0:T(4,128)(2,1)S(1)}, u32[]{:S(2)}, u32[]{:S(2)}) collective-permute-start(bf16[2,4,2048]{2,1,0:T(4,128)(2,1)S(1)} %get-tuple-element.22.after_ref), channel_id=1, source_target_pairs={{0,8},{1,9},{2,10},{3,11},{4,12},{5,13},{6,14},{7,15},{10,0},{11,1... | collective-permute-start | bytes 98312 | tf_op jit(solution)/shard_map/ppermute | solution.py:62
  6.9 6.6 %collective-permute-start.4 = (bf16[32,256]{1,0:T(8,128)(2,1)S(1)}, bf16[32,256]{1,0:T(8,128)(2,1)S(1)}, u32[]{:S(2)}, u32[]{:S(2)}) collective-permute-start(bf16[32,256]{1,0:T(8,128)(2,1)S(1)} %shard_map.93.refs_7_), channel_id=1, source_target_pairs={{7,8},{6,9},{5,10},{4,11},{3,12},{2,13},{1,14},{0,15},{8,16},{9,17... | collective-permute-start | bytes 49160 | tf_op jit(solution)/shard_map/ppermute | solution.py:62
  12.6 1.5 %collective-permute-start.6 = (bf16[32,256]{1,0:T(8,128)(2,1)S(1)}, bf16[32,256]{1,0:T(8,128)(2,1)S(1)}, u32[]{:S(2)}, u32[]{:S(2)}) collective-permute-start(bf16[32,256]{1,0:T(8,128)(2,1)S(1)} %shard_map.93.refs_7_), channel_id=1, source_target_pairs={{5,8},{4,9},{7,10},{6,11},{1,12},{0,13},{3,14},{2,15},{8,0},{9,1},... | collective-permute-start | bytes 49160 | tf_op jit(solution)/shard_map/ppermute | solution.py:62
  13.1 1.3 %collective-permute-start.8 = (bf16[32,256]{1,0:T(8,128)(2,1)S(1)}, bf16[32,256]{1,0:T(8,128)(2,1)S(1)}, u32[]{:S(2)}, u32[]{:S(2)}) collective-permute-start(bf16[32,256]{1,0:T(8,128)(2,1)S(1)} %shard_map.93.refs_7_), channel_id=1, source_target_pairs={{3,8},{2,9},{1,10},{0,11},{7,12},{6,13},{5,14},{4,15},{8,0},{9,1},... | collective-permute-start | bytes 49160 | tf_op jit(solution)/shard_map/ppermute | solution.py:62
  13.7 1.2 %collective-permute-start.10 = (bf16[32,256]{1,0:T(8,128)(2,1)S(1)}, bf16[32,256]{1,0:T(8,128)(2,1)S(1)}, u32[]{:S(2)}, u32[]{:S(2)}) collective-permute-start(bf16[32,256]{1,0:T(8,128)(2,1)S(1)} %shard_map.93.refs_7_), channel_id=1, source_target_pairs={{1,8},{0,9},{3,10},{2,11},{5,12},{4,13},{7,14},{6,15},{8,0},{9,1},... | collective-permute-start | bytes 49160 | tf_op jit(solution)/shard_map/ppermute | solution.py:62
  15.2 9.2 %collective-permute-start.12 = (bf16[32,256]{1,0:T(8,128)(2,1)S(1)}, bf16[32,256]{1,0:T(8,128)(2,1)S(1)}, u32[]{:S(2)}, u32[]{:S(2)}) collective-permute-start(bf16[32,256]{1,0:T(8,128)(2,1)S(1)} %shard_map.94.refs_7_), channel_id=1, source_target_pairs={{0,8},{1,9},{2,10},{3,11},{4,12},{5,13},{6,14},{7,15},{15,16},{14,... | collective-permute-start | bytes 49160 | tf_op jit(solution)/shard_map/ppermute | solution.py:62
  19.6 4.9 %collective-permute-start.13 = (bf16[32,256]{1,0:T(8,128)(2,1)S(1)}, bf16[32,256]{1,0:T(8,128)(2,1)S(1)}, u32[]{:S(2)}, u32[]{:S(2)}) collective-permute-start(bf16[32,256]{1,0:T(8,128)(2,1)S(1)} %shard_map.94.refs_7_), channel_id=1, source_target_pairs={{0,8},{1,9},{2,10},{3,11},{4,12},{5,13},{6,14},{7,15},{14,16},{15,... | collective-permute-start | bytes 49160 | tf_op jit(solution)/shard_map/ppermute | solution.py:62
  22.6 3.6 %collective-permute-start.14 = (bf16[32,256]{1,0:T(8,128)(2,1)S(1)}, bf16[32,256]{1,0:T(8,128)(2,1)S(1)}, u32[]{:S(2)}, u32[]{:S(2)}) collective-permute-start(bf16[32,256]{1,0:T(8,128)(2,1)S(1)} %shard_map.94.refs_7_), channel_id=1, source_target_pairs={{0,8},{1,9},{2,10},{3,11},{4,12},{5,13},{6,14},{7,15},{13,16},{12,... | collective-permute-start | bytes 49160 | tf_op jit(solution)/shard_map/ppermute | solution.py:62
  22.7 3.6 %collective-permute-start.15 = (bf16[32,256]{1,0:T(8,128)(2,1)S(1)}, bf16[32,256]{1,0:T(8,128)(2,1)S(1)}, u32[]{:S(2)}, u32[]{:S(2)}) collective-permute-start(bf16[32,256]{1,0:T(8,128)(2,1)S(1)} %shard_map.94.refs_7_), channel_id=1, source_target_pairs={{0,24},{1,25},{2,26},{3,27},{4,28},{5,29},{6,30},{7,31},{12,16},{1... | collective-permute-start | bytes 49160 | tf_op jit(solution)/shard_map/ppermute | solution.py:62
  22.8 3.5 %collective-permute-start.16 = (bf16[32,256]{1,0:T(8,128)(2,1)S(1)}, bf16[32,256]{1,0:T(8,128)(2,1)S(1)}, u32[]{:S(2)}, u32[]{:S(2)}) collective-permute-start(bf16[32,256]{1,0:T(8,128)(2,1)S(1)} %shard_map.94.refs_7_), channel_id=1, source_target_pairs={{0,24},{1,25},{2,26},{3,27},{4,28},{5,29},{6,30},{7,31},{11,16},{1... | collective-permute-start | bytes 49160 | tf_op jit(solution)/shard_map/ppermute | solution.py:62
  24.5 3.4 %collective-permute-start.17 = (bf16[32,256]{1,0:T(8,128)(2,1)S(1)}, bf16[32,256]{1,0:T(8,128)(2,1)S(1)}, u32[]{:S(2)}, u32[]{:S(2)}) collective-permute-start(bf16[32,256]{1,0:T(8,128)(2,1)S(1)} %shard_map.94.refs_7_), channel_id=1, source_target_pairs={{0,24},{1,25},{2,26},{3,27},{4,28},{5,29},{6,30},{7,31},{10,16},{1... | collective-permute-start | bytes 49160 | tf_op jit(solution)/shard_map/ppermute | solution.py:62
  24.5 3.4 %collective-permute-start.18 = (bf16[32,256]{1,0:T(8,128)(2,1)S(1)}, bf16[32,256]{1,0:T(8,128)(2,1)S(1)}, u32[]{:S(2)}, u32[]{:S(2)}) collective-permute-start(bf16[32,256]{1,0:T(8,128)(2,1)S(1)} %shard_map.94.refs_7_), channel_id=1, source_target_pairs={{0,24},{1,25},{2,26},{3,27},{4,28},{5,29},{6,30},{7,31},{9,16},{8,... | collective-permute-start | bytes 49160 | tf_op jit(solution)/shard_map/ppermute | solution.py:62
  26.2 3.4 %collective-permute-start.19 = (bf16[32,256]{1,0:T(8,128)(2,1)S(1)}, bf16[32,256]{1,0:T(8,128)(2,1)S(1)}, u32[]{:S(2)}, u32[]{:S(2)}) collective-permute-start(bf16[32,256]{1,0:T(8,128)(2,1)S(1)} %shard_map.94.refs_7_), channel_id=1, source_target_pairs={{0,24},{1,25},{2,26},{3,27},{4,28},{5,29},{6,30},{7,31},{8,16},{9,... | collective-permute-start | bytes 49160 | tf_op jit(solution)/shard_map/ppermute | solution.py:62
  29.6 6.3 %collective-permute-start.20 = (bf16[32,256]{1,0:T(8,128)(2,1)S(1)}, bf16[32,256]{1,0:T(8,128)(2,1)S(1)}, u32[]{:S(2)}, u32[]{:S(2)}) collective-permute-start(bf16[32,256]{1,0:T(8,128)(2,1)S(1)} %shard_map.95.refs_7_), channel_id=1, source_target_pairs={{0,8},{1,9},{2,10},{3,11},{4,12},{5,13},{6,14},{7,15},{8,16},{9,17... | collective-permute-start | bytes 49160 | tf_op jit(solution)/shard_map/ppermute | solution.py:62
  29.7 6.3 %collective-permute-start.21 = (bf16[32,256]{1,0:T(8,128)(2,1)S(1)}, bf16[32,256]{1,0:T(8,128)(2,1)S(1)}, u32[]{:S(2)}, u32[]{:S(2)}) collective-permute-start(bf16[32,256]{1,0:T(8,128)(2,1)S(1)} %shard_map.95.refs_7_), channel_id=1, source_target_pairs={{0,8},{1,9},{2,10},{3,11},{4,12},{5,13},{6,14},{7,15},{8,16},{9,17... | collective-permute-start | bytes 49160 | tf_op jit(solution)/shard_map/ppermute | solution.py:62
  30.9 6.0 %collective-permute-start.22 = (bf16[32,256]{1,0:T(8,128)(2,1)S(1)}, bf16[32,256]{1,0:T(8,128)(2,1)S(1)}, u32[]{:S(2)}, u32[]{:S(2)}) collective-permute-start(bf16[32,256]{1,0:T(8,128)(2,1)S(1)} %shard_map.95.refs_7_), channel_id=1, source_target_pairs={{0,8},{1,9},{2,10},{3,11},{4,12},{5,13},{6,14},{7,15},{8,0},{9,1},... | collective-permute-start | bytes 49160 | tf_op jit(solution)/shard_map/ppermute | solution.py:62
  32.2 5.2 %collective-permute-start.23 = (bf16[32,256]{1,0:T(8,128)(2,1)S(1)}, bf16[32,256]{1,0:T(8,128)(2,1)S(1)}, u32[]{:S(2)}, u32[]{:S(2)}) collective-permute-start(bf16[32,256]{1,0:T(8,128)(2,1)S(1)} %shard_map.95.refs_7_), channel_id=1, source_target_pairs={{0,8},{1,9},{2,10},{3,11},{4,12},{5,13},{6,14},{7,15},{8,0},{9,1},... | collective-permute-start | bytes 49160 | tf_op jit(solution)/shard_map/ppermute | solution.py:62
  33.6 4.1 %collective-permute-start.24 = (bf16[32,256]{1,0:T(8,128)(2,1)S(1)}, bf16[32,256]{1,0:T(8,128)(2,1)S(1)}, u32[]{:S(2)}, u32[]{:S(2)}) collective-permute-start(bf16[32,256]{1,0:T(8,128)(2,1)S(1)} %shard_map.95.refs_7_), channel_id=1, source_target_pairs={{0,8},{1,9},{2,10},{3,11},{4,12},{5,13},{6,14},{7,15},{8,0},{9,1},... | collective-permute-start | bytes 49160 | tf_op jit(solution)/shard_map/ppermute | solution.py:62
  36.0 3.2 %collective-permute-start.25 = (bf16[32,256]{1,0:T(8,128)(2,1)S(1)}, bf16[32,256]{1,0:T(8,128)(2,1)S(1)}, u32[]{:S(2)}, u32[]{:S(2)}) collective-permute-start(bf16[32,256]{1,0:T(8,128)(2,1)S(1)} %shard_map.95.refs_7_), channel_id=1, source_target_pairs={{0,8},{1,9},{2,10},{3,11},{4,12},{5,13},{6,14},{7,15},{8,0},{9,1},... | collective-permute-start | bytes 49160 | tf_op jit(solution)/shard_map/ppermute | solution.py:62
  36.0 3.2 %collective-permute-start.26 = (bf16[32,256]{1,0:T(8,128)(2,1)S(1)}, bf16[32,256]{1,0:T(8,128)(2,1)S(1)}, u32[]{:S(2)}, u32[]{:S(2)}) collective-permute-start(bf16[32,256]{1,0:T(8,128)(2,1)S(1)} %shard_map.95.refs_7_), channel_id=1, source_target_pairs={{0,8},{1,9},{2,10},{3,11},{4,12},{5,13},{6,14},{7,15},{8,0},{9,1},... | collective-permute-start | bytes 49160 | tf_op jit(solution)/shard_map/ppermute | solution.py:62
  36.8 2.4 %collective-permute-start.27 = (bf16[32,256]{1,0:T(8,128)(2,1)S(1)}, bf16[32,256]{1,0:T(8,128)(2,1)S(1)}, u32[]{:S(2)}, u32[]{:S(2)}) collective-permute-start(bf16[32,256]{1,0:T(8,128)(2,1)S(1)} %shard_map.95.refs_7_), channel_id=1, source_target_pairs={{0,8},{1,9},{2,10},{3,11},{4,12},{5,13},{6,14},{7,15},{8,0},{9,1},... | collective-permute-start | bytes 49160 | tf_op jit(solution)/shard_map/ppermute | solution.py:62
  (4 other events, 4.8 us)
